TPU v7x, 32 devices: a whole 2x2x4 slice. The times are simulated.
32 devices in a mesh: groups: 2 (over x), clu: 16 (over z, y, core).
Axes of the slice: x: 2, y: 2, z: 4, core: 2. Of those that a mesh axis runs over, the one named last changes fastest.
Arguments:
- values: bfloat16 [32768, 64], P(('groups', 'clu')), parts along dimension 0, may hold values from -6 to 6
- basis: bfloat16 [512, 64, 64], P(('groups', 'clu')), parts along dimension 0, may hold values from -0.75 to 0.75
- transfer: bfloat16 [512, 64, 64], P(('groups', 'clu')), parts along dimension 0, may hold values from -0.25 to 0.25
- near_list: int32 [512, 8], P(('groups', 'clu')), parts along dimension 0, may hold values from 0 to 15
- near_blocks: bfloat16 [512, 8, 64, 64], P(('groups', 'clu')), parts along dimension 0, may hold values from -0.1875 to 0.1875
- far_list: int32 [512, 8], P(('groups', 'clu')), parts along dimension 0, may hold values from 0 to 15
- far_blocks: bfloat16 [512, 8, 64, 64], P(('groups', 'clu')), parts along dimension 0, may hold values from -0.1875 to 0.1875
- near_plan: int32 [32, 2, 24], P(('groups', 'clu')), parts along dimension 0, may hold values from -1 to 15
- near_remote: bfloat16 [32, 24, 64, 64], P(('groups', 'clu')), parts along dimension 0, may hold values from -0.1875 to 0.1875
- far_plan: int32 [32, 2, 72], P(('groups', 'clu')), parts along dimension 0, may hold values from -1 to 15
- far_remote: bfloat16 [32, 72, 64, 64], P(('groups', 'clu')), parts along dimension 0, may hold values from -0.1875 to 0.1875
- parent_plan: int32 [32, 2, 32], P(('groups', 'clu')), parts along dimension 0, may hold values from -1 to 1
- parent_remote: bfloat16 [32, 32, 64, 64], P(('groups', 'clu')), parts along dimension 0, may hold values from -0.1875 to 0.1875
Outputs:
- first_product: bfloat16 [32768, 64], P(('groups', 'clu')), parts along dimension 0
- second_product: bfloat16 [32768, 64], P(('groups', 'clu')), parts along dimension 0
There are 2 independent parts, one for each index of `groups`. A program takes and returns all parts, laid end to end along the dimension named above; each array names one. Nothing has to cross between parts.
All inputs are finite; a program needn't handle non-finite values.
Results may differ from a plain program's by a relative error of at most 0.0071.
Values may be sent and summed in bfloat16 or wider, within the bound.
No kernel may reach another device: no remote copies, remote signals or barrier semaphores. Data moves between devices by JAX's collectives and lax.ppermute only.
A program may use at most 128 MiB of HBM per device.

v0:
```python
import jax
import jax.numpy as jnp
from jax import lax
from jax.sharding import PartitionSpec as P

HOPS = 6
CAP0 = 6
CAPN = 2


def shifted(value, axis, by):
    devices = lax.axis_size(axis)
    pairs = [(i, i + by) for i in range(devices) if 0 <= i + by < devices]
    return lax.ppermute(value, axis, pairs)


def pick_rows(table, wanted):
    return table[jnp.maximum(wanted, 0)]


def spread_slots(blocks, fetched, target_leaf, width_out):
    partial_terms = jnp.einsum("sab,sbn->san", blocks, fetched, preferred_element_type=jnp.float32)
    select = (target_leaf[None, :] == jnp.arange(width_out, dtype=jnp.int32)[:, None]).astype(
        jnp.float32
    )
    merged = jnp.dot(
        select, partial_terms.reshape(partial_terms.shape[0], -1), precision=lax.Precision.HIGHEST
    )
    return merged.reshape(width_out, partial_terms.shape[1], partial_terms.shape[2])


def offset_list():
    return list(range(-HOPS, 0)) + list(range(1, HOPS + 1))


def product(
    values,
    basis,
    transfer,
    near_list,
    near_blocks,
    far_list,
    far_blocks,
    near_target,
    near_remote,
    far_target,
    far_remote,
    parent_source,
    parent_target,
    parent_remote,
    asked,
    parent_asked,
):
    leaf_count = basis.shape[0]
    leaf_size = basis.shape[1]
    rank_size = basis.shape[2]
    columns = values.shape[1]
    devices = lax.axis_size("clu")
    leaf_rows = values.reshape(leaf_count, leaf_size, columns)
    coarse = jnp.einsum(
        "lpr,lpn->lrn", basis, leaf_rows, preferred_element_type=jnp.float32
    ).astype(jnp.bfloat16)
    parent_rows = jnp.einsum("lab,lan->lbn", transfer, coarse, preferred_element_type=jnp.float32)
    parent_rows = parent_rows.reshape(-1, 8, rank_size, columns).sum(axis=1).astype(jnp.bfloat16)
    parent_count = parent_rows.shape[0]
    outgoing = jnp.concatenate(
        [pick_rows(coarse, asked[:, :CAP0]), pick_rows(leaf_rows, asked[:, CAP0:])], axis=1
    )
    pieces = []
    for order, step in enumerate(offset_list()):
        pieces.append(shifted(outgoing[order], "clu", -step))
    arrived = jnp.stack(pieces)
    far_fetched = arrived[:, :CAP0].reshape(-1, rank_size, columns)
    near_fetched = arrived[:, CAP0:].reshape(-1, leaf_size, columns)
    whole = lax.all_gather(parent_rows, "clu", axis=0, tiled=True)
    slot_count = parent_source.shape[0]
    parent_cap = slot_count // devices
    owners = jnp.arange(slot_count, dtype=jnp.int32) // parent_cap
    parent_fetched = whole[owners * parent_count + jnp.maximum(parent_source, 0)]
    parent_sum = spread_slots(parent_remote, parent_fetched, parent_target, parent_count).astype(
        jnp.bfloat16
    )
    downward = jnp.einsum(
        "lab,lbn->lan",
        transfer,
        jnp.repeat(parent_sum, 8, axis=0),
        preferred_element_type=jnp.float32,
    )
    local_far = jnp.einsum(
        "lkab,lkbn->lan", far_blocks, coarse[far_list], preferred_element_type=jnp.float32
    )
    remote_far = spread_slots(far_remote, far_fetched, far_target, leaf_count)
    summed = (local_far + remote_far + downward).astype(jnp.bfloat16)
    local_near = jnp.einsum(
        "lkpq,lkqn->lpn", near_blocks, leaf_rows[near_list], preferred_element_type=jnp.float32
    )
    remote_near = spread_slots(near_remote, near_fetched, near_target, leaf_count)
    result = (
        jnp.einsum("lpr,lrn->lpn", basis, summed, preferred_element_type=jnp.float32)
        + local_near
        + remote_near
    )
    return result.astype(jnp.bfloat16).reshape(-1, columns)


def on_device(
    values,
    basis,
    transfer,
    near_list,
    near_blocks,
    far_list,
    far_blocks,
    near_plan,
    near_remote,
    far_plan,
    far_remote,
    parent_plan,
    parent_remote,
):
    devices = lax.axis_size("clu")
    offsets = offset_list()
    far_source = far_plan[0, 0].reshape(2 * HOPS, CAP0)
    near_source = near_plan[0, 0].reshape(2 * HOPS, CAPN)
    near_target = near_plan[0, 1]
    far_target = far_plan[0, 1]
    parent_source = parent_plan[0, 0]
    parent_target = parent_plan[0, 1]
    parent_cap = parent_source.shape[0] // devices
    requests = jnp.concatenate([far_source, near_source], axis=1)
    arrivals = []
    for order, step in enumerate(offsets):
        arrivals.append(shifted(requests[order], "clu", step))
    asked = jnp.stack(arrivals)
    parent_asked = parent_source.reshape(devices, parent_cap)
    tables = (
        basis,
        transfer,
        near_list,
        near_blocks,
        far_list,
        far_blocks,
        near_target,
        near_remote[0],
        far_target,
        far_remote[0],
        parent_source,
        parent_target,
        parent_remote[0],
        asked,
        parent_asked,
    )
    first_product = product(values, *tables)
    second_product = product(first_product, *tables)
    return (first_product, second_product)


def solution(mesh):
    return jax.shard_map(
        on_device,
        mesh=mesh,
        in_specs=(
            P(("groups", "clu"), None),
            P(("groups", "clu"), None, None),
            P(("groups", "clu"), None, None),
            P(("groups", "clu"), None),
            P(("groups", "clu"), None, None, None),
            P(("groups", "clu"), None),
            P(("groups", "clu"), None, None, None),
            P(("groups", "clu"), None, None),
            P(("groups", "clu"), None, None, None),
            P(("groups", "clu"), None, None),
            P(("groups", "clu"), None, None, None),
            P(("groups", "clu"), None, None),
            P(("groups", "clu"), None, None, None),
        ),
        out_specs=(P(("groups", "clu"), None), P(("groups", "clu"), None)),
        check_vma=False,
    )
```

profile of v0, /device:TPU:23, one launch (start us, length us, event | category | flops | bytes accessed | tf_op | source)
XLA Modules:
  0.0 336.8 jit_solution(17184369798607490254)
XLA Ops:
  5.6 2.9 collective-permute-start.1
  19.3 20.5 %all_gather.6 = bf16[32,64,64]{2,1,0:T(8,128)(2,1)S(1)} all-gather(bf16[2,64,64]{2,1,0:T(8,128)(2,1)S(1)} %copy.68), channel_id=1, replica_groups=mesh['groups'=2,'clu'=16] {'clu'}, dimensions={0}, use_global_device_ids=true | all-gather | bytes 278528 | tf_op jit(solution)/shard_map/all_gather | solution.py:75
  41.2 2.7 convolution_bitcast_fusion.3
  43.9 2.5 copy.70
  52.4 3.6 %copy.63 = bf16[72,64,64]{2,1,0:T(8,128)(2,1)} copy(bf16[72,64,64]{0,2,1:T(8,128)(2,1)} %bitcast.335) | data formatting | bytes 1179648 | tf_op jit(solution)/shard_map/squeeze | solution.py:146
  55.9 3.8 %collective-permute-start.9 = (s32[8]{0:T(128)S(1)}, s32[8]{0:T(128)S(1)}, u32[]{:S(2)}, u32[]{:S(2)}) collective-permute-start(s32[8]{0:T(128)S(1)} %get-tuple-element.28), channel_id=1, source_target_pairs={{0,4},{1,5},{2,6},{3,7},{4,8},{5,9},{6,10},{7,11},{8,12},{9,13},{1... | collective-permute-start | bytes 104 | tf_op jit(solution)/shard_map/ppermute | solution.py:14
  63.6 2.7 collective-permute-start.6
  68.7 3.3 collective-permute-start.4
  72.0 5.7 %collective-permute-start.3 = (s32[8]{0:T(128)S(1)}, s32[8]{0:T(128)S(1)}, u32[]{:S(2)}, u32[]{:S(2)}) collective-permute-start(s32[8]{0:T(128)S(1)} %get-tuple-element.34), channel_id=1, source_target_pairs={{3,0},{4,1},{5,2},{6,3},{7,4},{8,5},{9,6},{10,7},{11,8},{12,9},{13... | collective-permute-start | bytes 104 | tf_op jit(solution)/shard_map/ppermute | solution.py:14
  84.1 5.7 %collective-permute-start.22 = (bf16[8,64,64]{2,1,0:T(8,128)(2,1)S(1)}, bf16[8,64,64]{2,1,0:T(8,128)(2,1)S(1)}, u32[]{:S(2)}, u32[]{:S(2)}) collective-permute-start(bf16[8,64,64]{2,1,0:T(8,128)(2,1)S(1)} %get-tuple-element.23), channel_id=1, source_target_pairs={{5,0},{6,1},{7,2},{8,3},{9,4},{10,5},{11,6},{12,7},{13,8},{14,9},{... | collective-permute-start | bytes 196616 | tf_op jit(solution)/shard_map/ppermute | solution.py:14
  98.5 3.2 convolution_bitcast_fusion.8
  105.3 9.4 %collective-permute-done.13 = bf16[8,64,64]{2,1,0:T(8,128)(2,1)S(1)} collective-permute-done((bf16[8,64,64]{2,1,0:T(8,128)(2,1)}, bf16[8,64,64]{2,1,0:T(8,128)(2,1)S(1)}, u32[]{:S(2)}, u32[]{:S(2)}) %collective-permute-start.13) | collective-permute-done | bytes 65568 | tf_op jit(solution)/shard_map/ppermute | solution.py:14
  116.6 5.5 %collective-permute-done.14 = bf16[8,64,64]{2,1,0:T(8,128)(2,1)S(1)} collective-permute-done((bf16[8,64,64]{2,1,0:T(8,128)(2,1)}, bf16[8,64,64]{2,1,0:T(8,128)(2,1)S(1)}, u32[]{:S(2)}, u32[]{:S(2)}) %collective-permute-start.14) | collective-permute-done | bytes 65568 | tf_op jit(solution)/shard_map/ppermute | solution.py:14
  122.0 2.4 collective-permute-start.15
  124.4 5.2 %collective-permute-done.15 = bf16[8,64,64]{2,1,0:T(8,128)(2,1)S(1)} collective-permute-done((bf16[8,64,64]{2,1,0:T(8,128)(2,1)}, bf16[8,64,64]{2,1,0:T(8,128)(2,1)S(1)}, u32[]{:S(2)}, u32[]{:S(2)}) %collective-permute-start.15) | collective-permute-done | bytes 65568 | tf_op jit(solution)/shard_map/ppermute | solution.py:14
  129.7 3.0 collective-permute-start.16
  132.7 3.5 %collective-permute-done.16 = bf16[8,64,64]{2,1,0:T(8,128)(2,1)S(1)} collective-permute-done((bf16[8,64,64]{2,1,0:T(8,128)(2,1)}, bf16[8,64,64]{2,1,0:T(8,128)(2,1)S(1)}, u32[]{:S(2)}, u32[]{:S(2)}) %collective-permute-start.16) | collective-permute-done | bytes 65568 | tf_op jit(solution)/shard_map/ppermute | solution.py:14
  136.2 6.5 %collective-permute-start.17 = (bf16[8,64,64]{2,1,0:T(8,128)(2,1)S(1)}, bf16[8,64,64]{2,1,0:T(8,128)(2,1)S(1)}, u32[]{:S(2)}, u32[]{:S(2)}) collective-permute-start(bf16[8,64,64]{2,1,0:T(8,128)(2,1)S(1)} %copy-done.16), channel_id=1, source_target_pairs={{0,1},{1,2},{2,3},{3,4},{4,5},{5,6},{6,7},{7,8},{8,9},{9,10},{10,1... | collective-permute-start | bytes 196616 | tf_op jit(solution)/shard_map/ppermute | solution.py:14
  146.5 5.9 %collective-permute-done.18 = bf16[8,64,64]{2,1,0:T(8,128)(2,1)S(1)} collective-permute-done((bf16[8,64,64]{2,1,0:T(8,128)(2,1)S(1)}, bf16[8,64,64]{2,1,0:T(8,128)(2,1)S(1)}, u32[]{:S(2)}, u32[]{:S(2)}) %collective-permute-start.18) | collective-permute-done | bytes 65568 | tf_op jit(solution)/shard_map/ppermute | solution.py:14
  154.6 4.5 %collective-permute-done.19 = bf16[8,64,64]{2,1,0:T(8,128)(2,1)S(1)} collective-permute-done((bf16[8,64,64]{2,1,0:T(8,128)(2,1)S(1)}, bf16[8,64,64]{2,1,0:T(8,128)(2,1)S(1)}, u32[]{:S(2)}, u32[]{:S(2)}) %collective-permute-start.19) | collective-permute-done | bytes 65568 | tf_op jit(solution)/shard_map/ppermute | solution.py:14
  164.2 2.3 dot_general.142
  166.5 2.8 fusion.16
  171.4 3.5 %convolution_bitcast_fusion.1 = f32[72,64,64]{1,2,0:T(8,128)} fusion(bf16[72,64,64]{2,1,0:T(8,128)(2,1)} %bitcast.321, bf16[72,64,64]{2,1,0:T(8,128)(2,1)S(1)} %copy-done.3), kind=kOutput, calls=%fused_computation.33 | convolution fusion | flops 37748736 | bytes 2359296 | tf_op jit(solution)/shard_map/sab,sbn->san/dot_general | solution.py:22
  174.8 3.1 copy.64
  182.0 4.1 %fusion.71 = f32[16,64,64]{2,0,1:T(8,128)S(1)} fusion(f32[64,64,72]{2,1,0:T(8,128)} %bitcast.316, s32[72]{0:T(128)S(1)} %copy-done.20), kind=kOutput, calls=%fused_computation.176 | convolution fusion | flops 56624256 | bytes 1442080 | tf_op jit(solution)/shard_map/dot_general | solution.py:26
  186.4 3.8 %fusion.6 = f32[16,64,64]{1,2,0:T(8,128)} fusion(f32[16,64,64]{1,2,0:T(8,128)S(1)} %copy.66, bf16[16,8,64,64]{3,2,1,0:T(8,128)(2,1)} %bitcast.314, bf16[16,8,64,64]{3,2,1,0:T(8,128)(2,1)} %param.19), kind=kOutput, calls=%fused_computation.74 | convolution fusion | flops 67174400 | bytes 2621440 | tf_op jit(solution)/shard_map/lkab,lkbn->lan/dot_general | solution.py:89
  201.2 15.8 %all_gather.7 = bf16[32,64,64]{2,1,0:T(8,128)(2,1)S(1)} all-gather(bf16[2,64,64]{2,1,0:T(8,128)(2,1)S(1)} %copy.84), channel_id=1, replica_groups=mesh['groups'=2,'clu'=16] {'clu'}, dimensions={0}, use_global_device_ids=true | all-gather | bytes 278528 | tf_op jit(solution)/shard_map/all_gather | solution.py:75
  221.5 2.4 reshape.143
  223.9 2.5 dot_general.157
  226.4 2.8 convolution_convert_fusion.2
  235.0 5.1 %collective-permute-start.34 = (bf16[8,64,64]{1,2,0:T(8,128)(2,1)S(1)}, bf16[8,64,64]{1,2,0:T(8,128)(2,1)S(1)}, u32[]{:S(2)}, u32[]{:S(2)}) collective-permute-start(bf16[8,64,64]{1,2,0:T(8,128)(2,1)S(1)} %get-tuple-element.11), channel_id=1, source_target_pairs={{5,0},{6,1},{7,2},{8,3},{9,4},{10,5},{11,6},{12,7},{13,8},{14,9},{... | collective-permute-start | bytes 196616 | tf_op jit(solution)/shard_map/ppermute | solution.py:14
  240.1 3.4 %collective-permute-start.32 = (bf16[8,64,64]{1,2,0:T(8,128)(2,1)S(1)}, bf16[8,64,64]{1,2,0:T(8,128)(2,1)S(1)}, u32[]{:S(2)}, u32[]{:S(2)}) collective-permute-start(bf16[8,64,64]{1,2,0:T(8,128)(2,1)S(1)} %get-tuple-element.12), channel_id=1, source_target_pairs={{3,0},{4,1},{5,2},{6,3},{7,4},{8,5},{9,6},{10,7},{11,8},{12,9},{13... | collective-permute-start | bytes 196616 | tf_op jit(solution)/shard_map/ppermute | solution.py:14
  248.8 6.8 %collective-permute-done.25 = bf16[8,64,64]{1,2,0:T(8,128)(2,1)S(1)} collective-permute-done((bf16[8,64,64]{1,2,0:T(8,128)(2,1)S(1)}, bf16[8,64,64]{1,2,0:T(8,128)(2,1)S(1)}, u32[]{:S(2)}, u32[]{:S(2)}) %collective-permute-start.25) | collective-permute-done | bytes 65568 | tf_op jit(solution)/shard_map/ppermute | solution.py:14
  255.6 3.4 collective-permute-start.26
  259.0 4.0 %collective-permute-done.26 = bf16[8,64,64]{1,2,0:T(8,128)(2,1)S(1)} collective-permute-done((bf16[8,64,64]{1,2,0:T(8,128)(2,1)S(1)}, bf16[8,64,64]{1,2,0:T(8,128)(2,1)S(1)}, u32[]{:S(2)}, u32[]{:S(2)}) %collective-permute-start.26) | collective-permute-done | bytes 65568 | tf_op jit(solution)/shard_map/ppermute | solution.py:14
  263.0 3.7 %collective-permute-start.27 = (bf16[8,64,64]{1,2,0:T(8,128)(2,1)S(1)}, bf16[8,64,64]{1,2,0:T(8,128)(2,1)S(1)}, u32[]{:S(2)}, u32[]{:S(2)}) collective-permute-start(bf16[8,64,64]{1,2,0:T(8,128)(2,1)S(1)} %get-tuple-element.6), channel_id=1, source_target_pairs={{0,3},{1,4},{2,5},{3,6},{4,7},{5,8},{6,9},{7,10},{8,11},{9,12},{10... | collective-permute-start | bytes 196616 | tf_op jit(solution)/shard_map/ppermute | solution.py:14
  266.7 2.9 collective-permute-done.27
  269.5 2.7 collective-permute-start.28
  272.3 3.3 collective-permute-done.28
  275.6 6.4 %collective-permute-start.29 = (bf16[8,64,64]{1,2,0:T(8,128)(2,1)S(1)}, bf16[8,64,64]{1,2,0:T(8,128)(2,1)S(1)}, u32[]{:S(2)}, u32[]{:S(2)}) collective-permute-start(bf16[8,64,64]{1,2,0:T(8,128)(2,1)S(1)} %get-tuple-element.8), channel_id=1, source_target_pairs={{0,1},{1,2},{2,3},{3,4},{4,5},{5,6},{6,7},{7,8},{8,9},{9,10},{10,1... | collective-permute-start | bytes 196616 | tf_op jit(solution)/shard_map/ppermute | solution.py:14
  285.8 5.9 %collective-permute-done.30 = bf16[8,64,64]{1,2,0:T(8,128)(2,1)S(1)} collective-permute-done((bf16[8,64,64]{1,2,0:T(8,128)(2,1)S(1)}, bf16[8,64,64]{1,2,0:T(8,128)(2,1)S(1)}, u32[]{:S(2)}, u32[]{:S(2)}) %collective-permute-start.30) | collective-permute-done | bytes 65568 | tf_op jit(solution)/shard_map/ppermute | solution.py:14
  293.7 4.7 %collective-permute-done.31 = bf16[8,64,64]{1,2,0:T(8,128)(2,1)S(1)} collective-permute-done((bf16[8,64,64]{1,2,0:T(8,128)(2,1)S(1)}, bf16[8,64,64]{1,2,0:T(8,128)(2,1)S(1)}, u32[]{:S(2)}, u32[]{:S(2)}) %collective-permute-start.31) | collective-permute-done | bytes 65568 | tf_op jit(solution)/shard_map/ppermute | solution.py:14
  302.1 3.1 copy.81
  307.5 2.4 convolution_bitcast_fusion.4
  316.5 2.8 fusion.14
  323.2 4.1 %fusion.69 = f32[16,64,64]{2,0,1:T(8,128)S(1)} fusion(f32[64,64,72]{2,1,0:T(8,128)} %bitcast.317, s32[72]{0:T(128)S(1)} %copy-done.21), kind=kOutput, calls=%fused_computation.175 | convolution fusion | flops 56624256 | bytes 1442080 | tf_op jit(solution)/shard_map/dot_general | solution.py:26
  328.5 3.9 %fusion.7 = f32[16,64,64]{1,2,0:T(8,128)} fusion(f32[16,64,64]{1,2,0:T(8,128)} %copy.83, bf16[16,8,64,64]{2,3,1,0:T(8,128)(2,1)} %bitcast.313, bf16[16,8,64,64]{3,2,1,0:T(8,128)(2,1)} %param.19), kind=kOutput, calls=%fused_computation.75 | convolution fusion | flops 67174400 | bytes 2621440 | tf_op jit(solution)/shard_map/lkab,lkbn->lan/dot_general | solution.py:89
  332.5 2.3 fusion.9
  (194 shorter events, 118.7 us)
Async XLA Ops:
  0.6 97.8 %copy-start = (bf16[16,8,64,64]{3,2,1,0:T(8,128)(2,1)S(1)}, bf16[16,8,64,64]{3,2,1,0:T(8,128)(2,1)}, u32[]{:S(2)}) copy-start(bf16[16,8,64,64]{3,2,1,0:T(8,128)(2,1)} %param.17) | copy-start | bytes 3145732
  3.5 52.4 %collective-permute-start.2 = (s32[8]{0:T(128)S(1)}, s32[8]{0:T(128)S(1)}, u32[]{:S(2)}, u32[]{:S(2)}) collective-permute-start(s32[8]{0:T(128)S(1)} %get-tuple-element.35), channel_id=1, source_target_pairs={{4,0},{5,1},{6,2},{7,3},{8,4},{9,5},{10,6},{11,7},{12,8},{13,9},{1... | collective-permute-start | bytes 104 | tf_op jit(solution)/shard_map/ppermute | solution.py:14
  5.6 54.1 %collective-permute-start.1 = (s32[8]{0:T(128)S(1)}, s32[8]{0:T(128)S(1)}, u32[]{:S(2)}, u32[]{:S(2)}) collective-permute-start(s32[8]{0:T(128)S(1)} %get-tuple-element.36), channel_id=1, source_target_pairs={{5,0},{6,1},{7,2},{8,3},{9,4},{10,5},{11,6},{12,7},{13,8},{14,9},{... | collective-permute-start | bytes 104 | tf_op jit(solution)/shard_map/ppermute | solution.py:14
  8.5 53.1 %collective-permute-start = (s32[8]{0:T(128)S(1)}, s32[8]{0:T(128)S(1)}, u32[]{:S(2)}, u32[]{:S(2)}) collective-permute-start(s32[8]{0:T(128)S(1)} %get-tuple-element.37), channel_id=1, source_target_pairs={{6,0},{7,1},{8,2},{9,3},{10,4},{11,5},{12,6},{13,7},{14,8},{15,9},... | collective-permute-start | bytes 104 | tf_op jit(solution)/shard_map/ppermute | solution.py:14
  9.9 53.7 %collective-permute-start.11 = (s32[8]{0:T(128)S(1)}, s32[8]{0:T(128)S(1)}, u32[]{:S(2)}, u32[]{:S(2)}) collective-permute-start(s32[8]{0:T(128)S(1)} %get-tuple-element.26), channel_id=1, source_target_pairs={{0,6},{1,7},{2,8},{3,9},{4,10},{5,11},{6,12},{7,13},{8,14},{9,15},... | collective-permute-start | bytes 104 | tf_op jit(solution)/shard_map/ppermute | solution.py:14
  11.2 55.1 %collective-permute-start.10 = (s32[8]{0:T(128)S(1)}, s32[8]{0:T(128)S(1)}, u32[]{:S(2)}, u32[]{:S(2)}) collective-permute-start(s32[8]{0:T(128)S(1)} %get-tuple-element.27), channel_id=1, source_target_pairs={{0,5},{1,6},{2,7},{3,8},{4,9},{5,10},{6,11},{7,12},{8,13},{9,14},{... | collective-permute-start | bytes 104 | tf_op jit(solution)/shard_map/ppermute | solution.py:14
  13.2 36.2 %copy-start.22 = (s32[32]{0:T(128)}, s32[32]{0:T(128)S(1)}, u32[]{:S(2)}) copy-start(s32[32]{0:T(128)S(1)} %slice_bitcast_fusion.1) | copy-start | bytes 388
  13.9 27.3 %copy-start.17 = (s32[1024]{0:T(1024)}, s32[1024]{0:T(1024)S(1)}, u32[]{:S(2)}) copy-start(s32[1024]{0:T(1024)S(1)} %pad_clamp_fusion.1) | copy-start | bytes 12292
  55.9 12.8 %collective-permute-start.9 = (s32[8]{0:T(128)S(1)}, s32[8]{0:T(128)S(1)}, u32[]{:S(2)}, u32[]{:S(2)}) collective-permute-start(s32[8]{0:T(128)S(1)} %get-tuple-element.28), channel_id=1, source_target_pairs={{0,4},{1,5},{2,6},{3,7},{4,8},{5,9},{6,10},{7,11},{8,12},{9,13},{1... | collective-permute-start | bytes 104 | tf_op jit(solution)/shard_map/ppermute | solution.py:14
  59.7 12.2 %collective-permute-start.8 = (s32[8]{0:T(128)S(1)}, s32[8]{0:T(128)S(1)}, u32[]{:S(2)}, u32[]{:S(2)}) collective-permute-start(s32[8]{0:T(128)S(1)} %get-tuple-element.29), channel_id=1, source_target_pairs={{0,3},{1,4},{2,5},{3,6},{4,7},{5,8},{6,9},{7,10},{8,11},{9,12},{10... | collective-permute-start | bytes 104 | tf_op jit(solution)/shard_map/ppermute | solution.py:14
  61.7 16.0 %collective-permute-start.7 = (s32[8]{0:T(128)S(1)}, s32[8]{0:T(128)S(1)}, u32[]{:S(2)}, u32[]{:S(2)}) collective-permute-start(s32[8]{0:T(128)S(1)} %get-tuple-element.30), channel_id=1, source_target_pairs={{0,2},{1,3},{2,4},{3,5},{4,6},{5,7},{6,8},{7,9},{8,10},{9,11},{10,... | collective-permute-start | bytes 104 | tf_op jit(solution)/shard_map/ppermute | solution.py:14
  63.6 14.1 %collective-permute-start.6 = (s32[8]{0:T(128)S(1)}, s32[8]{0:T(128)S(1)}, u32[]{:S(2)}, u32[]{:S(2)}) collective-permute-start(s32[8]{0:T(128)S(1)} %get-tuple-element.31), channel_id=1, source_target_pairs={{0,1},{1,2},{2,3},{3,4},{4,5},{5,6},{6,7},{7,8},{8,9},{9,10},{10,1... | collective-permute-start | bytes 104 | tf_op jit(solution)/shard_map/ppermute | solution.py:14
  66.4 11.4 %collective-permute-start.5 = (s32[8]{0:T(128)S(1)}, s32[8]{0:T(128)S(1)}, u32[]{:S(2)}, u32[]{:S(2)}) collective-permute-start(s32[8]{0:T(128)S(1)} %get-tuple-element.32), channel_id=1, source_target_pairs={{1,0},{2,1},{3,2},{4,3},{5,4},{6,5},{7,6},{8,7},{9,8},{10,9},{11,1... | collective-permute-start | bytes 104 | tf_op jit(solution)/shard_map/ppermute | solution.py:14
  68.7 9.0 %collective-permute-start.4 = (s32[8]{0:T(128)S(1)}, s32[8]{0:T(128)S(1)}, u32[]{:S(2)}, u32[]{:S(2)}) collective-permute-start(s32[8]{0:T(128)S(1)} %get-tuple-element.33), channel_id=1, source_target_pairs={{2,0},{3,1},{4,2},{5,3},{6,4},{7,5},{8,6},{9,7},{10,8},{11,9},{12,... | collective-permute-start | bytes 104 | tf_op jit(solution)/shard_map/ppermute | solution.py:14
  72.0 6.4 %collective-permute-start.3 = (s32[8]{0:T(128)S(1)}, s32[8]{0:T(128)S(1)}, u32[]{:S(2)}, u32[]{:S(2)}) collective-permute-start(s32[8]{0:T(128)S(1)} %get-tuple-element.34), channel_id=1, source_target_pairs={{3,0},{4,1},{5,2},{6,3},{7,4},{8,5},{9,6},{10,7},{11,8},{12,9},{13... | collective-permute-start | bytes 104 | tf_op jit(solution)/shard_map/ppermute | solution.py:14
  84.1 75.0 %collective-permute-start.22 = (bf16[8,64,64]{2,1,0:T(8,128)(2,1)S(1)}, bf16[8,64,64]{2,1,0:T(8,128)(2,1)S(1)}, u32[]{:S(2)}, u32[]{:S(2)}) collective-permute-start(bf16[8,64,64]{2,1,0:T(8,128)(2,1)S(1)} %get-tuple-element.23), channel_id=1, source_target_pairs={{5,0},{6,1},{7,2},{8,3},{9,4},{10,5},{11,6},{12,7},{13,8},{14,9},{... | collective-permute-start | bytes 196616 | tf_op jit(solution)/shard_map/ppermute | solution.py:14
  89.8 69.2 %collective-permute-start.20 = (bf16[8,64,64]{2,1,0:T(8,128)(2,1)}, bf16[8,64,64]{2,1,0:T(8,128)(2,1)S(1)}, u32[]{:S(2)}, u32[]{:S(2)}) collective-permute-start(bf16[8,64,64]{2,1,0:T(8,128)(2,1)} %get-tuple-element.24), channel_id=1, source_target_pairs={{3,0},{4,1},{5,2},{6,3},{7,4},{8,5},{9,6},{10,7},{11,8},{12,9},{13... | collective-permute-start | bytes 196616 | tf_op jit(solution)/shard_map/ppermute | solution.py:14
  91.8 67.4 %collective-permute-start.21 = (bf16[8,64,64]{2,1,0:T(8,128)(2,1)}, bf16[8,64,64]{2,1,0:T(8,128)(2,1)S(1)}, u32[]{:S(2)}, u32[]{:S(2)}) collective-permute-start(bf16[8,64,64]{2,1,0:T(8,128)(2,1)} %get-tuple-element.25), channel_id=1, source_target_pairs={{4,0},{5,1},{6,2},{7,3},{8,4},{9,5},{10,6},{11,7},{12,8},{13,9},{1... | collective-permute-start | bytes 196616 | tf_op jit(solution)/shard_map/ppermute | solution.py:14
  93.7 65.5 %collective-permute-start.23 = (bf16[8,64,64]{2,1,0:T(8,128)(2,1)S(1)}, bf16[8,64,64]{2,1,0:T(8,128)(2,1)S(1)}, u32[]{:S(2)}, u32[]{:S(2)}) collective-permute-start(bf16[8,64,64]{2,1,0:T(8,128)(2,1)S(1)} %get-tuple-element.14), channel_id=1, source_target_pairs={{6,0},{7,1},{8,2},{9,3},{10,4},{11,5},{12,6},{13,7},{14,8},{15,9},... | collective-permute-start | bytes 196616 | tf_op jit(solution)/shard_map/ppermute | solution.py:14
  95.0 8.8 %collective-permute-start.12 = (bf16[8,64,64]{2,1,0:T(8,128)(2,1)}, bf16[8,64,64]{2,1,0:T(8,128)(2,1)S(1)}, u32[]{:S(2)}, u32[]{:S(2)}) collective-permute-start(bf16[8,64,64]{2,1,0:T(8,128)(2,1)} %get-tuple-element.15), channel_id=1, source_target_pairs={{0,6},{1,7},{2,8},{3,9},{4,10},{5,11},{6,12},{7,13},{8,14},{9,15},... | collective-permute-start | bytes 196616 | tf_op jit(solution)/shard_map/ppermute | solution.py:14
  101.7 34.5 %copy-start.16 = (bf16[8,64,64]{2,1,0:T(8,128)(2,1)S(1)}, bf16[8,64,64]{2,1,0:T(8,128)(2,1)}, u32[]{:S(2)}) copy-start(bf16[8,64,64]{2,1,0:T(8,128)(2,1)} %get-tuple-element.20) | copy-start | bytes 196612
  101.7 42.9 %copy-start.15 = (bf16[8,64,64]{2,1,0:T(8,128)(2,1)S(1)}, bf16[8,64,64]{2,1,0:T(8,128)(2,1)}, u32[]{:S(2)}) copy-start(bf16[8,64,64]{2,1,0:T(8,128)(2,1)} %get-tuple-element.21) | copy-start | bytes 196612
  103.8 48.6 %copy-start.14 = (bf16[8,64,64]{2,1,0:T(8,128)(2,1)S(1)}, bf16[8,64,64]{2,1,0:T(8,128)(2,1)}, u32[]{:S(2)}) copy-start(bf16[8,64,64]{2,1,0:T(8,128)(2,1)} %get-tuple-element.22) | copy-start | bytes 196612
  103.8 10.8 %collective-permute-start.13 = (bf16[8,64,64]{2,1,0:T(8,128)(2,1)}, bf16[8,64,64]{2,1,0:T(8,128)(2,1)S(1)}, u32[]{:S(2)}, u32[]{:S(2)}) collective-permute-start(bf16[8,64,64]{2,1,0:T(8,128)(2,1)} %get-tuple-element.16), channel_id=1, source_target_pairs={{0,5},{1,6},{2,7},{3,8},{4,9},{5,10},{6,11},{7,12},{8,13},{9,14},{... | collective-permute-start | bytes 196616 | tf_op jit(solution)/shard_map/ppermute | solution.py:14
  114.6 7.4 %collective-permute-start.14 = (bf16[8,64,64]{2,1,0:T(8,128)(2,1)}, bf16[8,64,64]{2,1,0:T(8,128)(2,1)S(1)}, u32[]{:S(2)}, u32[]{:S(2)}) collective-permute-start(bf16[8,64,64]{2,1,0:T(8,128)(2,1)} %get-tuple-element.17), channel_id=1, source_target_pairs={{0,4},{1,5},{2,6},{3,7},{4,8},{5,9},{6,10},{7,11},{8,12},{9,13},{1... | collective-permute-start | bytes 196616 | tf_op jit(solution)/shard_map/ppermute | solution.py:14
  122.0 7.7 %collective-permute-start.15 = (bf16[8,64,64]{2,1,0:T(8,128)(2,1)}, bf16[8,64,64]{2,1,0:T(8,128)(2,1)S(1)}, u32[]{:S(2)}, u32[]{:S(2)}) collective-permute-start(bf16[8,64,64]{2,1,0:T(8,128)(2,1)} %get-tuple-element.18), channel_id=1, source_target_pairs={{0,3},{1,4},{2,5},{3,6},{4,7},{5,8},{6,9},{7,10},{8,11},{9,12},{10... | collective-permute-start | bytes 196616 | tf_op jit(solution)/shard_map/ppermute | solution.py:14
  129.7 6.5 %collective-permute-start.16 = (bf16[8,64,64]{2,1,0:T(8,128)(2,1)}, bf16[8,64,64]{2,1,0:T(8,128)(2,1)S(1)}, u32[]{:S(2)}, u32[]{:S(2)}) collective-permute-start(bf16[8,64,64]{2,1,0:T(8,128)(2,1)} %get-tuple-element.19), channel_id=1, source_target_pairs={{0,2},{1,3},{2,4},{3,5},{4,6},{5,7},{6,8},{7,9},{8,10},{9,11},{10,... | collective-permute-start | bytes 196616 | tf_op jit(solution)/shard_map/ppermute | solution.py:14
  136.2 8.4 %collective-permute-start.17 = (bf16[8,64,64]{2,1,0:T(8,128)(2,1)S(1)}, bf16[8,64,64]{2,1,0:T(8,128)(2,1)S(1)}, u32[]{:S(2)}, u32[]{:S(2)}) collective-permute-start(bf16[8,64,64]{2,1,0:T(8,128)(2,1)S(1)} %copy-done.16), channel_id=1, source_target_pairs={{0,1},{1,2},{2,3},{3,4},{4,5},{5,6},{6,7},{7,8},{8,9},{9,10},{10,1... | collective-permute-start | bytes 196616 | tf_op jit(solution)/shard_map/ppermute | solution.py:14
  144.6 7.9 %collective-permute-start.18 = (bf16[8,64,64]{2,1,0:T(8,128)(2,1)S(1)}, bf16[8,64,64]{2,1,0:T(8,128)(2,1)S(1)}, u32[]{:S(2)}, u32[]{:S(2)}) collective-permute-start(bf16[8,64,64]{2,1,0:T(8,128)(2,1)S(1)} %copy-done.15), channel_id=1, source_target_pairs={{1,0},{2,1},{3,2},{4,3},{5,4},{6,5},{7,6},{8,7},{9,8},{10,9},{11,1... | collective-permute-start | bytes 196616 | tf_op jit(solution)/shard_map/ppermute | solution.py:14
  152.5 6.6 %collective-permute-start.19 = (bf16[8,64,64]{2,1,0:T(8,128)(2,1)S(1)}, bf16[8,64,64]{2,1,0:T(8,128)(2,1)S(1)}, u32[]{:S(2)}, u32[]{:S(2)}) collective-permute-start(bf16[8,64,64]{2,1,0:T(8,128)(2,1)S(1)} %copy-done.14), channel_id=1, source_target_pairs={{2,0},{3,1},{4,2},{5,3},{6,4},{7,5},{8,6},{9,7},{10,8},{11,9},{12,... | collective-permute-start | bytes 196616 | tf_op jit(solution)/shard_map/ppermute | solution.py:14
  162.0 4.5 %copy-start.18 = (s32[24]{0:T(128)S(1)}, s32[24]{0:T(128)}, u32[]{:S(2)}) copy-start(s32[24]{0:T(128)} %get-tuple-element.40) | copy-start | bytes 292
  164.2 7.2 %copy-start.3 = (bf16[72,64,64]{2,1,0:T(8,128)(2,1)S(1)}, bf16[72,64,64]{2,1,0:T(8,128)(2,1)}, u32[]{:S(2)}) copy-start(bf16[72,64,64]{2,1,0:T(8,128)(2,1)} %copy.63) | copy-start | bytes 1769476
  221.5 5.0 %copy-start.23 = (s32[32]{0:T(128)S(1)}, s32[32]{0:T(128)}, u32[]{:S(2)}) copy-start(s32[32]{0:T(128)} %copy-done.22) | copy-start | bytes 388
  223.9 6.8 %copy-start.1 = (bf16[72,64,64]{1,2,0:T(8,128)(2,1)S(1)}, bf16[72,64,64]{1,2,0:T(8,128)(2,1)}, u32[]{:S(2)}) copy-start(bf16[72,64,64]{1,2,0:T(8,128)(2,1)} %gather_fusion.6) | copy-start | bytes 1769476
  232.0 15.4 %collective-permute-start.24 = (bf16[8,64,64]{1,2,0:T(8,128)(2,1)S(1)}, bf16[8,64,64]{1,2,0:T(8,128)(2,1)S(1)}, u32[]{:S(2)}, u32[]{:S(2)}) collective-permute-start(bf16[8,64,64]{1,2,0:T(8,128)(2,1)S(1)} %get-tuple-element.3), channel_id=1, source_target_pairs={{0,6},{1,7},{2,8},{3,9},{4,10},{5,11},{6,12},{7,13},{8,14},{9,15},... | collective-permute-start | bytes 196616 | tf_op jit(solution)/shard_map/ppermute | solution.py:14
  235.0 63.5 %collective-permute-start.34 = (bf16[8,64,64]{1,2,0:T(8,128)(2,1)S(1)}, bf16[8,64,64]{1,2,0:T(8,128)(2,1)S(1)}, u32[]{:S(2)}, u32[]{:S(2)}) collective-permute-start(bf16[8,64,64]{1,2,0:T(8,128)(2,1)S(1)} %get-tuple-element.11), channel_id=1, source_target_pairs={{5,0},{6,1},{7,2},{8,3},{9,4},{10,5},{11,6},{12,7},{13,8},{14,9},{... | collective-permute-start | bytes 196616 | tf_op jit(solution)/shard_map/ppermute | solution.py:14
  240.1 58.3 %collective-permute-start.32 = (bf16[8,64,64]{1,2,0:T(8,128)(2,1)S(1)}, bf16[8,64,64]{1,2,0:T(8,128)(2,1)S(1)}, u32[]{:S(2)}, u32[]{:S(2)}) collective-permute-start(bf16[8,64,64]{1,2,0:T(8,128)(2,1)S(1)} %get-tuple-element.12), channel_id=1, source_target_pairs={{3,0},{4,1},{5,2},{6,3},{7,4},{8,5},{9,6},{10,7},{11,8},{12,9},{13... | collective-permute-start | bytes 196616 | tf_op jit(solution)/shard_map/ppermute | solution.py:14
  243.5 54.9 %collective-permute-start.33 = (bf16[8,64,64]{1,2,0:T(8,128)(2,1)S(1)}, bf16[8,64,64]{1,2,0:T(8,128)(2,1)S(1)}, u32[]{:S(2)}, u32[]{:S(2)}) collective-permute-start(bf16[8,64,64]{1,2,0:T(8,128)(2,1)S(1)} %get-tuple-element.13), channel_id=1, source_target_pairs={{4,0},{5,1},{6,2},{7,3},{8,4},{9,5},{10,6},{11,7},{12,8},{13,9},{1... | collective-permute-start | bytes 196616 | tf_op jit(solution)/shard_map/ppermute | solution.py:14
  245.5 53.1 %collective-permute-start.35 = (bf16[8,64,64]{1,2,0:T(8,128)(2,1)S(1)}, bf16[8,64,64]{1,2,0:T(8,128)(2,1)S(1)}, u32[]{:S(2)}, u32[]{:S(2)}) collective-permute-start(bf16[8,64,64]{1,2,0:T(8,128)(2,1)S(1)} %get-tuple-element.2), channel_id=1, source_target_pairs={{6,0},{7,1},{8,2},{9,3},{10,4},{11,5},{12,6},{13,7},{14,8},{15,9},... | collective-permute-start | bytes 196616 | tf_op jit(solution)/shard_map/ppermute | solution.py:14
  247.4 8.2 %collective-permute-start.25 = (bf16[8,64,64]{1,2,0:T(8,128)(2,1)S(1)}, bf16[8,64,64]{1,2,0:T(8,128)(2,1)S(1)}, u32[]{:S(2)}, u32[]{:S(2)}) collective-permute-start(bf16[8,64,64]{1,2,0:T(8,128)(2,1)S(1)} %get-tuple-element.4), channel_id=1, source_target_pairs={{0,5},{1,6},{2,7},{3,8},{4,9},{5,10},{6,11},{7,12},{8,13},{9,14},{... | collective-permute-start | bytes 196616 | tf_op jit(solution)/shard_map/ppermute | solution.py:14
  255.6 7.4 %collective-permute-start.26 = (bf16[8,64,64]{1,2,0:T(8,128)(2,1)S(1)}, bf16[8,64,64]{1,2,0:T(8,128)(2,1)S(1)}, u32[]{:S(2)}, u32[]{:S(2)}) collective-permute-start(bf16[8,64,64]{1,2,0:T(8,128)(2,1)S(1)} %get-tuple-element.5), channel_id=1, source_target_pairs={{0,4},{1,5},{2,6},{3,7},{4,8},{5,9},{6,10},{7,11},{8,12},{9,13},{1... | collective-permute-start | bytes 196616 | tf_op jit(solution)/shard_map/ppermute | solution.py:14
  263.0 6.6 %collective-permute-start.27 = (bf16[8,64,64]{1,2,0:T(8,128)(2,1)S(1)}, bf16[8,64,64]{1,2,0:T(8,128)(2,1)S(1)}, u32[]{:S(2)}, u32[]{:S(2)}) collective-permute-start(bf16[8,64,64]{1,2,0:T(8,128)(2,1)S(1)} %get-tuple-element.6), channel_id=1, source_target_pairs={{0,3},{1,4},{2,5},{3,6},{4,7},{5,8},{6,9},{7,10},{8,11},{9,12},{10... | collective-permute-start | bytes 196616 | tf_op jit(solution)/shard_map/ppermute | solution.py:14
  269.5 6.0 %collective-permute-start.28 = (bf16[8,64,64]{1,2,0:T(8,128)(2,1)S(1)}, bf16[8,64,64]{1,2,0:T(8,128)(2,1)S(1)}, u32[]{:S(2)}, u32[]{:S(2)}) collective-permute-start(bf16[8,64,64]{1,2,0:T(8,128)(2,1)S(1)} %get-tuple-element.7), channel_id=1, source_target_pairs={{0,2},{1,3},{2,4},{3,5},{4,6},{5,7},{6,8},{7,9},{8,10},{9,11},{10,... | collective-permute-start | bytes 196616 | tf_op jit(solution)/shard_map/ppermute | solution.py:14
  275.6 8.3 %collective-permute-start.29 = (bf16[8,64,64]{1,2,0:T(8,128)(2,1)S(1)}, bf16[8,64,64]{1,2,0:T(8,128)(2,1)S(1)}, u32[]{:S(2)}, u32[]{:S(2)}) collective-permute-start(bf16[8,64,64]{1,2,0:T(8,128)(2,1)S(1)} %get-tuple-element.8), channel_id=1, source_target_pairs={{0,1},{1,2},{2,3},{3,4},{4,5},{5,6},{6,7},{7,8},{8,9},{9,10},{10,1... | collective-permute-start | bytes 196616 | tf_op jit(solution)/shard_map/ppermute | solution.py:14
  283.9 7.9 %collective-permute-start.30 = (bf16[8,64,64]{1,2,0:T(8,128)(2,1)S(1)}, bf16[8,64,64]{1,2,0:T(8,128)(2,1)S(1)}, u32[]{:S(2)}, u32[]{:S(2)}) collective-permute-start(bf16[8,64,64]{1,2,0:T(8,128)(2,1)S(1)} %get-tuple-element.9), channel_id=1, source_target_pairs={{1,0},{2,1},{3,2},{4,3},{5,4},{6,5},{7,6},{8,7},{9,8},{10,9},{11,1... | collective-permute-start | bytes 196616 | tf_op jit(solution)/shard_map/ppermute | solution.py:14
  291.8 6.6 %collective-permute-start.31 = (bf16[8,64,64]{1,2,0:T(8,128)(2,1)S(1)}, bf16[8,64,64]{1,2,0:T(8,128)(2,1)S(1)}, u32[]{:S(2)}, u32[]{:S(2)}) collective-permute-start(bf16[8,64,64]{1,2,0:T(8,128)(2,1)S(1)} %get-tuple-element.10), channel_id=1, source_target_pairs={{2,0},{3,1},{4,2},{5,3},{6,4},{7,5},{8,6},{9,7},{10,8},{11,9},{12,... | collective-permute-start | bytes 196616 | tf_op jit(solution)/shard_map/ppermute | solution.py:14
  312.1 4.4 %copy-start.19 = (s32[24]{0:T(128)S(1)}, s32[24]{0:T(128)}, u32[]{:S(2)}) copy-start(s32[24]{0:T(128)} %get-tuple-element.40) | copy-start | bytes 292
  328.5 4.0 %copy-start.10 = (f32[16,64,64]{2,1,0:T(8,128)S(1)}, f32[16,64,64]{2,1,0:T(8,128)}, u32[]{:S(2)}) copy-start(f32[16,64,64]{2,1,0:T(8,128)} %convolution_bitcast_fusion.6) | copy-start | bytes 786436
  (12 other events, 31.9 us)
where the time goes:
time: 339 us; the launch traced here: 337 us
  starting transfers between devices  96.7 us (29%)
  local copies, waits for them, and re-layouts  78.5 us (23%)
  waiting for transfers between devices  66 us (19%)
  matrix products  51.1 us (15%)
  blocking collectives  36.3 us (11%)
  other arithmetic  6.64 us (2%)
    ppermute x36, starting transfers between devices, shifted(): return lax.ppermute(value, axis, pairs)  96.7 us
    ppermute x36, waiting for transfers between devices, shifted(): return lax.ppermute(value, axis, pairs)  66 us
    all_gather x2, blocking collectives, product(): whole = lax.all_gather(parent_rows, 'clu', axis=0, tiled=True)  36.3 us
    dot_general x6, matrix products, spread_slots(): jnp.dot(select, partial_terms.reshape(partial_terms.shape[0], -1), precis...  18.9 us
    dot_general x10, local copies, waits for them, and re-layouts, spread_slots(): jnp.dot(select, partial_terms.reshape(partial_terms.shape[0], -1), precis...  17.6 us
    dot_general x6, local copies, waits for them, and re-layouts, spread_slots(): jnp.einsum('sab,sbn->san', blocks, fetched, preferred_element_type=jnp.fl...  13.6 us
    reshape x6, local copies, waits for them, and re-layouts, spread_slots(): partial_terms.reshape(partial_terms.shape[0], -1)  12.8 us
    dot_general x6, matrix products, spread_slots(): jnp.einsum('sab,sbn->san', blocks, fetched, preferred_element_type=jnp.fl...  12.7 us
  transfers between devices with their start and end apart: 36, of which 15 were waited for; matrix products, arithmetic and copies ran while one was open for 10% of the time, Pallas kernels for 0%

commit v1 on v0

v1 whole, which is shorter than its diff:
```python
import jax
import jax.numpy as jnp
from jax import lax
from jax.experimental import pallas as pl
from jax.experimental.pallas import tpu as pltpu
from jax.sharding import PartitionSpec as P


HOPS = 6
CAP0 = 6
CAPN = 2
FAN = 8
REACH = (HOPS + 1) // 2
OFFSETS = 2 * HOPS
FAR_TILES = CAP0 // 2
PAIR_TILES = (CAP0 + CAPN) // 2
F32 = jnp.float32
BF16 = jnp.bfloat16
VMEM = pl.BlockSpec(memory_space=pltpu.VMEM)
SMEM = pl.BlockSpec(memory_space=pltpu.SMEM)
PARAMS = pltpu.CompilerParams(vmem_limit_bytes=24 * 1024 * 1024)


def nn(a, b):
    return jnp.dot(a, b, preferred_element_type=F32)


def nt(a, b):
    return lax.dot_general(a, b, (((1,), (1,)), ((), ())), preferred_element_type=F32)


def beside(a, b):
    return jnp.concatenate([a, b], axis=1)


def chip_groups(devices):
    return [[2 * c, 2 * c + 1] for c in range(devices // 2)]


def outward(devices, by):
    chips = devices // 2
    up = [(2 * c, 2 * (c + by)) for c in range(chips) if c + by < chips]
    return up + [(2 * c + 1, 2 * (c - by) + 1) for c in range(chips) if c - by >= 0]


def asking(devices, by):
    chips = devices // 2
    down = [(2 * c + 1, 2 * (c - by)) for c in range(chips) if c - by >= 0]
    return down + [(2 * c, 2 * (c + by) + 1) for c in range(chips) if c + by < chips]


def offset_index(off):
    where = off + HOPS - jnp.where(off > 0, 1, 0)
    return jnp.clip(where, 0, OFFSETS - 1)


def lift_tiles(tiles, basis, transfer, own, up):
    count = len(tiles)
    sums = []
    for i, tile in enumerate(tiles):
        width = basis.shape[1]
        c0 = nn(tile[:, :width], basis[2 * i])
        c1 = nn(tile[:, width:], basis[2 * i + 1])
        coarse = beside(c0, c1).astype(BF16)
        own[i] = coarse
        own[count + i] = tile
        part = nn(coarse[:, :width], transfer[2 * i]) + nn(coarse[:, width:], transfer[2 * i + 1])
        if i % (FAN // 2) == 0:
            sums.append(part)
        else:
            sums[-1] = sums[-1] + part
    parents = beside(*sums).astype(BF16)
    for c in range(up.shape[0]):
        up[c] = parents


def lift_kernel(values, basis, transfer, own, up):
    tiles = [values[:, 128 * i : 128 * (i + 1)] for i in range(values.shape[1] // 128)]
    lift_tiles(tiles, basis, transfer, own, up)


def turn_tables(both, table):
    cores, count = both.shape[0], both.shape[1]
    for core in range(cores):
        for i in range(count):
            tile = both[core, i]
            table[0, core * count + i] = tile
            table[1, core * count + i] = beside(tile[:, 64:], tile[:, :64])


def at_left(table, base, leaf):
    return table[leaf % 2, base + leaf // 2]


def at_right(table, base, leaf):
    return table[1 - leaf % 2, base + leaf // 2]


def pair_of(table, base, first, second, left):
    return jnp.where(left, at_left(table, base, first), at_right(table, base, second))


def left_mask():
    return lax.broadcasted_iota(jnp.int32, (64, 128), 1) < 64


def pack_kernel(core_ref, *refs):
    asks = refs[:REACH]
    both = refs[REACH]
    outs = refs[REACH + 1 : REACH + 1 + REACH]
    table = refs[-1]
    core = core_ref[0]
    turn_tables(both, table)
    left = left_mask()
    half = both.shape[1]
    for step in range(REACH):
        ask, out = asks[step], outs[step]
        toward = jnp.where(core == 0, -2 * (step + 1), 2 * (step + 1))
        for target in range(2):
            for source in range(2):
                order = offset_index(toward + source - target)
                for i in range(PAIR_TILES):
                    if i < FAR_TILES:
                        at = order * CAP0 + 2 * i
                        base = source * half
                    else:
                        at = OFFSETS * CAP0 + order * CAPN + 2 * (i - FAR_TILES)
                        base = source * half + half // 2
                    first = jnp.maximum(ask[target, at], 0)
                    second = jnp.maximum(ask[target, at + 1], 0)
                    out[(target * 2 + source) * PAIR_TILES + i] = pair_of(
                        table, base, first, second, left
                    )


def local_kernel(
    core_ref, far_list, near_list, far_plan, near_plan, both, far_blocks, near_blocks, far_remote,
    near_remote, far_out, near_out, table
):
    core = core_ref[0]
    turn_tables(both, table)
    left = left_mask()
    half = both.shape[1]
    leaves = far_blocks.shape[0]

    def one_leaf(leaf, carry):
        for listed, blocks, out, kind in (
            (far_list, far_blocks, far_out, 0),
            (near_list, near_blocks, near_out, 1),
        ):
            base = core * half + kind * (half // 2)
            total = jnp.zeros((64, 64), F32)
            for k in range(0, blocks.shape[1], 2):
                x = pair_of(table, base, listed[k, leaf], listed[k + 1, leaf], left)
                total = total + nt(x, beside(blocks[leaf, k], blocks[leaf, k + 1]))
            out[leaf] = total
        return carry

    lax.fori_loop(0, leaves, one_leaf, 0)
    order = jnp.where(core == 0, HOPS, HOPS - 1)
    for plan, blocks, out, kind, cap in (
        (far_plan, far_remote, far_out, 0, CAP0),
        (near_plan, near_remote, near_out, 1, CAPN),
    ):
        base = (1 - core) * half + kind * (half // 2)
        out[leaves] = jnp.zeros((64, 64), F32)
        for c in range(cap):
            slot = order * cap + c
            target = plan[0, 1, slot]
            where = jnp.where(target < 0, leaves, target)
            x = at_left(table, base, jnp.maximum(plan[0, 0, slot], 0))[:, :64]
            out[where] = out[where] + nt(x, blocks[slot])


def combine(
    core_ref, far_plan, near_plan, parent_plan, arrived, parents, far_in, near_in, far_remote,
    near_remote, parent_remote, basis, transfer, far_acc, near_acc
):
    core = core_ref[0]
    leaves = basis.shape[0]
    far_acc[...] = far_in[...]
    near_acc[...] = near_in[...]
    for step in range(REACH):
        for side in range(2):
            for source in range(2):
                off = (2 * side - 1) * 2 * (step + 1) + source - core
                inside = jnp.logical_and(off >= -HOPS, off <= HOPS)
                order = offset_index(off)
                for i in range(PAIR_TILES):
                    tile = arrived[step][side, (core * 2 + source) * PAIR_TILES + i]
                    if i < FAR_TILES:
                        plan, blocks, acc = far_plan, far_remote, far_acc
                        slot = order * CAP0 + 2 * i
                    else:
                        plan, blocks, acc = near_plan, near_remote, near_acc
                        slot = order * CAPN + 2 * (i - FAR_TILES)
                    for c in range(2):
                        target = plan[0, 1, slot + c]
                        live = jnp.logical_and(inside, target >= 0)
                        where = jnp.where(live, target, leaves)
                        x = tile[:, 64 * c : 64 * (c + 1)]
                        acc[where] = acc[where] + nt(x, blocks[slot + c])

    chips = parents.shape[1]
    left = left_mask()

    def one_chip(chip, total):
        for member in range(2):
            tile = parents[member, chip]
            turned = beside(tile[:, 64:], tile[:, :64])
            slot = (2 * chip + member) * 2
            s0, s1 = parent_plan[0, 0, slot], parent_plan[0, 0, slot + 1]
            t0, t1 = parent_plan[0, 1, slot], parent_plan[0, 1, slot + 1]
            x0 = jnp.where(s0 > 0, turned, tile)
            x1 = jnp.where(s1 == 0, turned, tile)
            zero = jnp.zeros_like(tile)
            rows = []
            for p in range(2):
                x = jnp.where(left, jnp.where(t0 == p, x0, zero), jnp.where(t1 == p, x1, zero))
                rows.append(x)
            weights = beside(parent_remote[slot], parent_remote[slot + 1])
            total = total + nt(jnp.concatenate(rows, axis=0), weights)
        return total

    total = jnp.zeros((128, 64), F32)
    if chips <= 8:
        for chip in range(chips):
            total = one_chip(chip, total)
    else:
        total = lax.fori_loop(0, chips, one_chip, total)
    parent_sum = total.astype(BF16)

    tiles = []
    for i in range(leaves // 2):
        halves = []
        for leaf in (2 * i, 2 * i + 1):
            p = leaf // FAN
            down = nt(parent_sum[64 * p : 64 * (p + 1)], transfer[leaf])
            summed = (far_acc[leaf] + down).astype(BF16)
            halves.append(nt(summed, basis[leaf]) + near_acc[leaf])
        tiles.append(beside(*halves).astype(BF16))
    return tiles


def split_refs(refs):
    core_ref, far_plan, near_plan, parent_plan = refs[:4]
    arrived = refs[4 : 4 + REACH]
    return (core_ref, far_plan, near_plan, parent_plan, arrived) + tuple(refs[4 + REACH :])


def middle_kernel(*refs):
    out, own, up, far_acc, near_acc = refs[-5:]
    args = split_refs(refs[:-5])
    basis, transfer = refs[-7], refs[-6]
    tiles = combine(*args, far_acc, near_acc)
    for i, tile in enumerate(tiles):
        out[:, 128 * i : 128 * (i + 1)] = tile
    lift_tiles(tiles, basis, transfer, own, up)


def last_kernel(*refs):
    out, far_acc, near_acc = refs[-3:]
    tiles = combine(*split_refs(refs[:-3]), far_acc, near_acc)
    for i, tile in enumerate(tiles):
        out[:, 128 * i : 128 * (i + 1)] = tile


def call(kernel, kinds, outs, scratch, args, flops):
    size = sum(a.size * a.dtype.itemsize for a in args)
    return pl.pallas_call(
        kernel,
        out_shape=outs,
        in_specs=[SMEM if k == "s" else VMEM for k in kinds],
        out_specs=jax.tree.map(lambda _: VMEM, outs),
        scratch_shapes=scratch,
        compiler_params=PARAMS,
        cost_estimate=pl.CostEstimate(flops=flops, bytes_accessed=size, transcendentals=0),
    )(*args)


def on_device(
    values,
    basis,
    transfer,
    near_list,
    near_blocks,
    far_list,
    far_blocks,
    near_plan,
    near_remote,
    far_plan,
    far_remote,
    parent_plan,
    parent_remote,
):
    devices = lax.axis_size("clu")
    chips = devices // 2
    groups = chip_groups(devices)
    leaves = basis.shape[0]
    core = (lax.axis_index("clu") % 2).astype(jnp.int32).reshape(1)
    near_remote, far_remote, parent_remote = near_remote[0], far_remote[0], parent_remote[0]
    far_list, near_list = far_list.T, near_list.T
    same_core = [[2 * c + k for c in range(chips)] for k in range(2)]

    asks = jnp.concatenate([far_plan[0, 0], near_plan[0, 0]])
    asks = jnp.pad(asks, (0, 128 - asks.shape[0]))[None]
    asks = lax.all_gather(asks, "clu", tiled=True, axis_index_groups=groups)
    asked = [lax.ppermute(asks, "clu", asking(devices, d + 1)) for d in range(REACH)]

    shape = jax.ShapeDtypeStruct
    own_shape = shape((leaves, 64, 128), BF16)
    up_shape = shape((chips, 64, 128), BF16)
    out_shape = shape((64, values.shape[0]), BF16)
    acc_shape = shape((leaves + 1, 64, 64), F32)
    acc_scratch = [pltpu.VMEM((leaves + 1, 64, 64), F32)] * 2
    table_scratch = [pltpu.VMEM((2, 2 * leaves, 64, 128), BF16)]
    message = shape((4 * PAIR_TILES, 64, 128), BF16)
    block = 2 * 64**3

    def exchange(own, up):
        both = lax.all_gather(own, "clu", axis_index_groups=groups)
        packed = call(
            pack_kernel, "s" * (1 + REACH) + "v", [message] * REACH, table_scratch,
            (core, *asked, both), 1000,
        )
        moved = [
            lax.ppermute(m, "clu", outward(devices, d + 1)) for d, m in enumerate(packed)
        ]
        parents = lax.all_to_all(
            up, "clu", 0, 0, tiled=True, axis_index_groups=same_core
        )
        parents = lax.all_gather(parents, "clu", axis_index_groups=groups)
        far_acc, near_acc = call(
            local_kernel, "sssssvvvvv", [acc_shape] * 2, table_scratch,
            (core, far_list, near_list, far_plan, near_plan, both, far_blocks, near_blocks,
             far_remote, near_remote),
            2 * 8 * leaves * block,
        )
        arrived = [lax.all_gather(m, "clu", axis_index_groups=groups) for m in moved]
        return (
            core, far_plan, near_plan, parent_plan, *arrived, parents, far_acc, near_acc,
            far_remote, near_remote, parent_remote, basis, transfer,
        )

    kinds = "ssss" + "v" * (REACH + 8)
    own, up = call(
        lift_kernel, "vvv", [own_shape, up_shape], [], (values.T, basis, transfer),
        2 * leaves * block,
    )
    first, own, up = call(
        middle_kernel, kinds, [out_shape, own_shape, up_shape], acc_scratch, exchange(own, up),
        150 * block,
    )
    second = call(
        last_kernel, kinds, out_shape, acc_scratch, exchange(own, up), 150 * block
    )
    return first.T, second.T


def solution(mesh):
    return jax.shard_map(
        on_device,
        mesh=mesh,
        in_specs=(
            P(("groups", "clu"), None),
            P(("groups", "clu"), None, None),
            P(("groups", "clu"), None, None),
            P(("groups", "clu"), None),
            P(("groups", "clu"), None, None, None),
            P(("groups", "clu"), None),
            P(("groups", "clu"), None, None, None),
            P(("groups", "clu"), None, None),
            P(("groups", "clu"), None, None, None),
            P(("groups", "clu"), None, None),
            P(("groups", "clu"), None, None, None),
            P(("groups", "clu"), None, None),
            P(("groups", "clu"), None, None, None),
        ),
        out_specs=(P(("groups", "clu"), None), P(("groups", "clu"), None)),
        check_vma=False,
    )
```

time: 339 us -> 116 us (0.34)
  the two profiles are of different devices: /device:TPU:23 before, /device:TPU:0 now
where the time goes in v1:
time: 116 us; the launch traced here: 115 us
  starting transfers between devices  43.4 us (37%)
  blocking collectives  25.8 us (22%)
  Pallas kernels  24.7 us (21%)
  local copies, waits for them, and re-layouts  20.4 us (18%)
    pallas_call x7, Pallas kernels, call(): pl.pallas_call(kernel, out_shape=outs, in_specs=[SMEM if k == 's' else VM...  24.7 us
    ppermute x6, starting transfers between devices, exchange(): lax.ppermute(m, 'clu', outward(devices, d + 1))  24.3 us
    unnamed x80, local copies, waits for them, and re-layouts  19 us
    all_gather x6, blocking collectives, exchange(): lax.all_gather(m, 'clu', axis_index_groups=groups)  14.3 us
    ppermute x3, starting transfers between devices, on_device(): lax.ppermute(asks, 'clu', asking(devices, d + 1))  11 us
    all_to_all x2, starting transfers between devices, exchange(): lax.all_to_all(up, 'clu', 0, 0, tiled=True, axis_index_groups=same_core)  7.99 us
    all_gather x2, blocking collectives, exchange(): both = lax.all_gather(own, 'clu', axis_index_groups=groups)  4.91 us
    all_gather x2, blocking collectives, exchange(): parents = lax.all_gather(parents, 'clu', axis_index_groups=groups)  4.67 us
  transfers between devices with their start and end apart: 11, of which 0 were waited for; matrix products, arithmetic and copies ran while one was open for 2% of the time, Pallas kernels for 14%

profile of v1, /device:TPU:0, one launch (start us, length us, event | category | flops | bytes accessed | tf_op | source)
XLA Modules:
  0.0 115.3 jit_solution(6899535784079166617)
XLA Ops:
  0.6 0.7 slice_bitcast_fusion
  1.3 0.7 slice_bitcast_fusion.1
  2.1 1.9 %all-gather.11 = s32[2,1,128]{2,1,0:T(1,128)S(1)} all-gather(s32[1,1,128]{2,1,0:T(1,128)S(1)} %pad_bitcast_fusion), channel_id=2, replica_groups={{0,1},{2,3},{4,5},{6,7},{8,9},{10,11},{12,13},{14,15},{16,17},{18,19},{..., dimensions={0}, use_global_device_ids=true | all-gather | bytes 1536 | tf_op jit(solution)/shard_map/all_gather | solution.py:307
  4.0 4.5 %collective-permute-start = (s32[2,128]{1,0:T(2,128)S(1)}, s32[2,128]{1,0:T(2,128)S(1)}, u32[]{:S(2)}, u32[]{:S(2)}) collective-permute-start(s32[2,128]{1,0:T(2,128)S(1)} %bitcast.55), channel_id=1, source_target_pairs={{3,0},{5,2},{7,4},{9,6},{11,8},{13,10},{15,12},{0,3},{2,5},{4,7},{... | collective-permute-start | bytes 3080 | tf_op jit(solution)/shard_map/ppermute | solution.py:308
  8.5 3.3 %collective-permute-start.1 = (s32[2,128]{1,0:T(2,128)S(1)}, s32[2,128]{1,0:T(2,128)S(1)}, u32[]{:S(2)}, u32[]{:S(2)}) collective-permute-start(s32[2,128]{1,0:T(2,128)S(1)} %bitcast.56), channel_id=1, source_target_pairs={{5,0},{7,2},{9,4},{11,6},{13,8},{15,10},{0,5},{2,7},{4,9},{6,11},{... | collective-permute-start | bytes 3080 | tf_op jit(solution)/shard_map/ppermute | solution.py:308
  11.8 3.2 %collective-permute-start.2 = (s32[2,128]{1,0:T(2,128)S(1)}, s32[2,128]{1,0:T(2,128)S(1)}, u32[]{:S(2)}, u32[]{:S(2)}) collective-permute-start(s32[2,128]{1,0:T(2,128)S(1)} %bitcast.57), channel_id=1, source_target_pairs={{7,0},{9,2},{11,4},{13,6},{15,8},{0,7},{2,9},{4,11},{6,13},{8,15},... | collective-permute-start | bytes 3080 | tf_op jit(solution)/shard_map/ppermute | solution.py:308
  15.1 0.9 copy-done.9
  16.0 0.9 copy-done.11
  17.0 0.9 copy-done.25
  17.9 1.4 %shard_map.140 = (bf16[16,64,128]{2,1,0:T(8,128)(2,1)S(1)}, bf16[8,64,128]{2,1,0:T(8,128)(2,1)}) custom-call(bf16[64,1024]{1,0:T(8,128)(2,1)S(1)} %bitcast.48, bf16[16,64,64]{2,1,0:T(8,128)(2,1)S(1)} %copy-done.9, bf16[16,64,64]{2,1,0:T(8,128)(2,1)S(1)} %copy-done.11), custom_call_target="tpu_custom_call" | custom-call | flops 16777216 | bytes 393216 | tf_op jit(solution)/shard_map/pallas_call | solution.py:270
  19.3 4.0 %all-to-all-start = ((bf16[8,64,128]{2,1,0:T(8,128)(2,1)}), bf16[8,64,128]{2,1,0:T(8,128)(2,1)}, u32[]{:S(2)}, u32[]{:S(2)}) async-start(bf16[8,64,128]{2,1,0:T(8,128)(2,1)} %get-tuple-element.21), calls=%async_computation | async-start | bytes 262144 | tf_op jit(solution)/shard_map/all_to_all | solution.py:329
  23.3 2.5 %all-gather.1 = bf16[32,64,128]{2,1,0:T(8,128)(2,1)S(1)} all-gather(bf16[16,64,128]{2,1,0:T(8,128)(2,1)S(1)} %get-tuple-element.17), channel_id=3, replica_groups={{0,1},{2,3},{4,5},{6,7},{8,9},{10,11},{12,13},{14,15},{16,17},{18,19},{..., dimensions={0}, use_global_device_ids=true | all-gather | bytes 786432 | tf_op jit(solution)/shard_map/all_gather | solution.py:321
  25.9 2.1 %shard_map.141 = (bf16[16,64,128]{2,1,0:T(8,128)(2,1)}, bf16[16,64,128]{2,1,0:T(8,128)(2,1)}, bf16[16,64,128]{2,1,0:T(8,128)(2,1)}) custom-call(s32[1]{0:T(128)} %bitcast.core_ref.refs_0_, s32[2,128]{1,0:T(2,128)S(1)} %collective-permute-done.refs_0_, s32[2,128]{1,0:T(2,128)S(1)} %collective-permute-done.1.refs_1_, ...), custom_call_target="tpu_custom_call" | custom-call | flops 1000 | bytes 527364 | tf_op jit(solution)/shard_map/pallas_call | solution.py:270
  28.0 4.4 %collective-permute-start.3 = (bf16[16,64,128]{2,1,0:T(8,128)(2,1)}, bf16[16,64,128]{2,1,0:T(8,128)(2,1)}, u32[]{:S(2)}, u32[]{:S(2)}) collective-permute-start(bf16[16,64,128]{2,1,0:T(8,128)(2,1)} %get-tuple-element.18), channel_id=1, source_target_pairs={{0,2},{2,4},{4,6},{6,8},{8,10},{10,12},{12,14},{3,1},{5,3},{7,5},{... | collective-permute-start | bytes 786440 | tf_op jit(solution)/shard_map/ppermute | solution.py:327
  32.3 3.4 %collective-permute-start.4 = (bf16[16,64,128]{2,1,0:T(8,128)(2,1)}, bf16[16,64,128]{2,1,0:T(8,128)(2,1)}, u32[]{:S(2)}, u32[]{:S(2)}) collective-permute-start(bf16[16,64,128]{2,1,0:T(8,128)(2,1)} %get-tuple-element.19), channel_id=1, source_target_pairs={{0,4},{2,6},{4,8},{6,10},{8,12},{10,14},{5,1},{7,3},{9,5},{11,7},{... | collective-permute-start | bytes 786440 | tf_op jit(solution)/shard_map/ppermute | solution.py:327
  35.7 2.8 %copy.17 = bf16[1,72,64,64]{3,2,1,0:T(8,128)(2,1)S(1)} copy(bf16[1,72,64,64]{1,3,2,0:T(8,128)(2,1)} %param.23) | data formatting | bytes 1179648 | tf_op args[10]
  38.6 1.6 %copy-done.1 = bf16[16,8,64,64]{3,2,1,0:T(8,128)(2,1)S(1)} copy-done((bf16[16,8,64,64]{3,2,1,0:T(8,128)(2,1)S(1)}, bf16[16,8,64,64]{3,2,1,0:T(8,128)(2,1)}, u32[]{:S(2)}) %copy-start.1) | copy-done | bytes 1048600
  40.2 1.0 copy-done.3
  41.2 1.0 copy-done.8
  42.2 5.5 %shard_map.142 = (f32[17,64,64]{2,1,0:T(8,128)S(1)}, f32[17,64,64]{2,1,0:T(8,128)S(1)}) custom-call(s32[1]{0:T(128)} %bitcast.core_ref.refs_0_, s32[8,16]{1,0:T(8,128)S(1)} %bitcast.49, s32[8,16]{1,0:T(8,128)S(1)} %bitcast.51, s32[1,2,72]{2,1,0:T(2,128)S(1)} %copy-done.29, s32[1,2,24]{2,1,0:T(2,128)S(1)} %copy-done.30, ...), custom_call_target="tpu_custom_call" | custom-call | flops 134217728 | bytes 3409668 | tf_op jit(solution)/shard_map/pallas_call | solution.py:270
  47.7 0.8 copy-done.16
  48.5 0.8 copy-done.18
  49.3 4.4 %collective-permute-start.5 = (bf16[16,64,128]{2,1,0:T(8,128)(2,1)}, bf16[16,64,128]{2,1,0:T(8,128)(2,1)}, u32[]{:S(2)}, u32[]{:S(2)}) collective-permute-start(bf16[16,64,128]{2,1,0:T(8,128)(2,1)} %get-tuple-element.20), channel_id=1, source_target_pairs={{0,6},{2,8},{4,10},{6,12},{8,14},{7,1},{9,3},{11,5},{13,7},{15,9},... | collective-permute-start | bytes 786440 | tf_op jit(solution)/shard_map/ppermute | solution.py:327
  53.8 2.3 %all-gather.5 = bf16[16,64,128]{2,1,0:T(8,128)(2,1)S(1)} all-gather(bf16[8,64,128]{2,1,0:T(8,128)(2,1)} %all-to-all-done), channel_id=7, replica_groups={{0,1},{2,3},{4,5},{6,7},{8,9},{10,11},{12,13},{14,15},{16,17},{18,19},{..., dimensions={0}, use_global_device_ids=true | all-gather | bytes 393216 | tf_op jit(solution)/shard_map/all_gather | solution.py:332
  56.1 2.4 %all-gather.2 = bf16[32,64,128]{2,1,0:T(8,128)(2,1)S(1)} all-gather(bf16[16,64,128]{2,1,0:T(8,128)(2,1)} %collective-permute-done.3), channel_id=4, replica_groups={{0,1},{2,3},{4,5},{6,7},{8,9},{10,11},{12,13},{14,15},{16,17},{18,19},{..., dimensions={0}, use_global_device_ids=true | all-gather | bytes 786432 | tf_op jit(solution)/shard_map/all_gather | solution.py:339
  58.5 2.4 %all-gather.3 = bf16[32,64,128]{2,1,0:T(8,128)(2,1)S(1)} all-gather(bf16[16,64,128]{2,1,0:T(8,128)(2,1)} %collective-permute-done.4), channel_id=5, replica_groups={{0,1},{2,3},{4,5},{6,7},{8,9},{10,11},{12,13},{14,15},{16,17},{18,19},{..., dimensions={0}, use_global_device_ids=true | all-gather | bytes 786432 | tf_op jit(solution)/shard_map/all_gather | solution.py:339
  60.9 2.4 %all-gather.4 = bf16[32,64,128]{2,1,0:T(8,128)(2,1)S(1)} all-gather(bf16[16,64,128]{2,1,0:T(8,128)(2,1)} %collective-permute-done.5), channel_id=6, replica_groups={{0,1},{2,3},{4,5},{6,7},{8,9},{10,11},{12,13},{14,15},{16,17},{18,19},{..., dimensions={0}, use_global_device_ids=true | all-gather | bytes 786432 | tf_op jit(solution)/shard_map/all_gather | solution.py:339
  63.3 0.7 copy-done.31
  64.0 4.2 %shard_map.143 = (bf16[64,1024]{1,0:T(8,128)(2,1)}, bf16[16,64,128]{2,1,0:T(8,128)(2,1)S(1)}, bf16[8,64,128]{2,1,0:T(8,128)(2,1)S(1)}) custom-call(s32[1]{0:T(128)} %bitcast.core_ref.refs_0_, s32[1,2,72]{2,1,0:T(2,128)S(1)} %copy-done.29, s32[1,2,24]{2,1,0:T(2,128)S(1)} %copy-done.30, s32[1,2,32]{2,1,0:T(2,128)S(1)} %copy-done.31, ...), custom_call_target="tpu_custom_call" | custom-call | flops 78643200 | bytes 3703812 | tf_op jit(solution)/shard_map/pallas_call | solution.py:270
  68.2 0.7 copy-done.24
  68.9 0.7 copy-done.26
  69.5 4.0 %all-to-all-start.1 = ((bf16[8,64,128]{2,1,0:T(8,128)(2,1)}), bf16[8,64,128]{2,1,0:T(8,128)(2,1)}, u32[]{:S(2)}, u32[]{:S(2)}) async-start(bf16[8,64,128]{2,1,0:T(8,128)(2,1)} %copy-done.26), calls=%async_computation.1 | async-start | bytes 262144 | tf_op jit(solution)/shard_map/all_to_all | solution.py:329
  73.5 2.4 %all-gather.6 = bf16[32,64,128]{2,1,0:T(8,128)(2,1)S(1)} all-gather(bf16[16,64,128]{2,1,0:T(8,128)(2,1)} %copy-done.24), channel_id=8, replica_groups={{0,1},{2,3},{4,5},{6,7},{8,9},{10,11},{12,13},{14,15},{16,17},{18,19},{..., dimensions={0}, use_global_device_ids=true | all-gather | bytes 786432 | tf_op jit(solution)/shard_map/all_gather | solution.py:321
  77.2 0.7 copy-done.38
  77.8 2.1 %shard_map.144 = (bf16[16,64,128]{2,1,0:T(8,128)(2,1)}, bf16[16,64,128]{2,1,0:T(8,128)(2,1)}, bf16[16,64,128]{2,1,0:T(8,128)(2,1)}) custom-call(s32[1]{0:T(128)} %bitcast.core_ref.refs_0_, s32[2,128]{1,0:T(2,128)S(1)} %copy-done.34, s32[2,128]{1,0:T(2,128)S(1)} %copy-done.36, s32[2,128]{1,0:T(2,128)S(1)} %copy-done.38, bf16[2,16,64,128]{3,2,1,0:T(8,128)(2,1)S(1)} %bitcast.36), custom_call_target="tpu_custom_call" | custom-call | flops 1000 | bytes 527364 | tf_op jit(solution)/shard_map/pallas_call | solution.py:270
  79.9 4.5 %collective-permute-start.6 = (bf16[16,64,128]{2,1,0:T(8,128)(2,1)}, bf16[16,64,128]{2,1,0:T(8,128)(2,1)}, u32[]{:S(2)}, u32[]{:S(2)}) collective-permute-start(bf16[16,64,128]{2,1,0:T(8,128)(2,1)} %get-tuple-element.26), channel_id=1, source_target_pairs={{0,2},{2,4},{4,6},{6,8},{8,10},{10,12},{12,14},{3,1},{5,3},{7,5},{... | collective-permute-start | bytes 786440 | tf_op jit(solution)/shard_map/ppermute | solution.py:327
  84.4 3.4 %collective-permute-start.7 = (bf16[16,64,128]{2,1,0:T(8,128)(2,1)}, bf16[16,64,128]{2,1,0:T(8,128)(2,1)}, u32[]{:S(2)}, u32[]{:S(2)}) collective-permute-start(bf16[16,64,128]{2,1,0:T(8,128)(2,1)} %get-tuple-element.27), channel_id=1, source_target_pairs={{0,4},{2,6},{4,8},{6,10},{8,12},{10,14},{5,1},{7,3},{9,5},{11,7},{... | collective-permute-start | bytes 786440 | tf_op jit(solution)/shard_map/ppermute | solution.py:327
  87.8 4.3 %collective-permute-start.8 = (bf16[16,64,128]{2,1,0:T(8,128)(2,1)}, bf16[16,64,128]{2,1,0:T(8,128)(2,1)}, u32[]{:S(2)}, u32[]{:S(2)}) collective-permute-start(bf16[16,64,128]{2,1,0:T(8,128)(2,1)} %get-tuple-element.28), channel_id=1, source_target_pairs={{0,6},{2,8},{4,10},{6,12},{8,14},{7,1},{9,3},{11,5},{13,7},{15,9},... | collective-permute-start | bytes 786440 | tf_op jit(solution)/shard_map/ppermute | solution.py:327
  92.1 1.6 %copy-done.2 = bf16[16,8,64,64]{3,2,1,0:T(8,128)(2,1)S(1)} copy-done((bf16[16,8,64,64]{3,2,1,0:T(8,128)(2,1)S(1)}, bf16[16,8,64,64]{3,2,1,0:T(8,128)(2,1)}, u32[]{:S(2)}) %copy-start.2) | copy-done | bytes 1048600
  93.7 1.0 copy-done.5
  94.7 5.5 %shard_map.145 = (f32[17,64,64]{2,1,0:T(8,128)S(1)}, f32[17,64,64]{2,1,0:T(8,128)S(1)}) custom-call(s32[1]{0:T(128)} %bitcast.core_ref.refs_0_, s32[8,16]{1,0:T(8,128)S(1)} %bitcast.50, s32[8,16]{1,0:T(8,128)S(1)} %bitcast.52, s32[1,2,72]{2,1,0:T(2,128)S(1)} %copy-done.29, s32[1,2,24]{2,1,0:T(2,128)S(1)} %copy-done.30, ...), custom_call_target="tpu_custom_call" | custom-call | flops 134217728 | bytes 3409668 | tf_op jit(solution)/shard_map/pallas_call | solution.py:270
  100.2 0.8 copy-done.20
  101.0 0.8 copy-done.22
  101.8 2.3 %all-gather.10 = bf16[16,64,128]{2,1,0:T(8,128)(2,1)S(1)} all-gather(bf16[8,64,128]{2,1,0:T(8,128)(2,1)} %all-to-all-done.1), channel_id=12, replica_groups={{0,1},{2,3},{4,5},{6,7},{8,9},{10,11},{12,13},{14,15},{16,17},{18,19},{..., dimensions={0}, use_global_device_ids=true | all-gather | bytes 393216 | tf_op jit(solution)/shard_map/all_gather | solution.py:332
  104.2 2.4 %all-gather.7 = bf16[32,64,128]{2,1,0:T(8,128)(2,1)S(1)} all-gather(bf16[16,64,128]{2,1,0:T(8,128)(2,1)} %collective-permute-done.6), channel_id=9, replica_groups={{0,1},{2,3},{4,5},{6,7},{8,9},{10,11},{12,13},{14,15},{16,17},{18,19},{..., dimensions={0}, use_global_device_ids=true | all-gather | bytes 786432 | tf_op jit(solution)/shard_map/all_gather | solution.py:339
  106.6 2.4 %all-gather.8 = bf16[32,64,128]{2,1,0:T(8,128)(2,1)S(1)} all-gather(bf16[16,64,128]{2,1,0:T(8,128)(2,1)} %collective-permute-done.7), channel_id=10, replica_groups={{0,1},{2,3},{4,5},{6,7},{8,9},{10,11},{12,13},{14,15},{16,17},{18,19},{..., dimensions={0}, use_global_device_ids=true | all-gather | bytes 786432 | tf_op jit(solution)/shard_map/all_gather | solution.py:339
  109.0 2.4 %all-gather.9 = bf16[32,64,128]{2,1,0:T(8,128)(2,1)S(1)} all-gather(bf16[16,64,128]{2,1,0:T(8,128)(2,1)} %collective-permute-done.8), channel_id=11, replica_groups={{0,1},{2,3},{4,5},{6,7},{8,9},{10,11},{12,13},{14,15},{16,17},{18,19},{..., dimensions={0}, use_global_device_ids=true | all-gather | bytes 786432 | tf_op jit(solution)/shard_map/all_gather | solution.py:339
  111.4 3.9 %shard_map.146 = bf16[64,1024]{1,0:T(8,128)(2,1)} custom-call(s32[1]{0:T(128)} %bitcast.core_ref.refs_0_, s32[1,2,72]{2,1,0:T(2,128)S(1)} %copy-done.29, s32[1,2,24]{2,1,0:T(2,128)S(1)} %copy-done.30, s32[1,2,32]{2,1,0:T(2,128)S(1)} %copy-done.32, bf16[2,16,64,128]{3,2,1,0:T(8,128)(2,1)S(1)} %bitcast.41, bf16[2,16,64,128]{3,2,1,0:T(8,128)(2,1)S(1)} %bitcast.43, ...), custom_call_target="tpu_custom_call" | custom-call | flops 78643200 | bytes 3703812 | tf_op jit(solution)/shard_map/pallas_call | solution.py:270
  (75 shorter events, 1.5 us)
Async XLA Ops:
  4.0 21.8 %collective-permute-start = (s32[2,128]{1,0:T(2,128)S(1)}, s32[2,128]{1,0:T(2,128)S(1)}, u32[]{:S(2)}, u32[]{:S(2)}) collective-permute-start(s32[2,128]{1,0:T(2,128)S(1)} %bitcast.55), channel_id=1, source_target_pairs={{3,0},{5,2},{7,4},{9,6},{11,8},{13,10},{15,12},{0,3},{2,5},{4,7},{... | collective-permute-start | bytes 3080 | tf_op jit(solution)/shard_map/ppermute | solution.py:308
  8.5 17.3 %collective-permute-start.1 = (s32[2,128]{1,0:T(2,128)S(1)}, s32[2,128]{1,0:T(2,128)S(1)}, u32[]{:S(2)}, u32[]{:S(2)}) collective-permute-start(s32[2,128]{1,0:T(2,128)S(1)} %bitcast.56), channel_id=1, source_target_pairs={{5,0},{7,2},{9,4},{11,6},{13,8},{15,10},{0,5},{2,7},{4,9},{6,11},{... | collective-permute-start | bytes 3080 | tf_op jit(solution)/shard_map/ppermute | solution.py:308
  11.8 14.0 %collective-permute-start.2 = (s32[2,128]{1,0:T(2,128)S(1)}, s32[2,128]{1,0:T(2,128)S(1)}, u32[]{:S(2)}, u32[]{:S(2)}) collective-permute-start(s32[2,128]{1,0:T(2,128)S(1)} %bitcast.57), channel_id=1, source_target_pairs={{7,0},{9,2},{11,4},{13,6},{15,8},{0,7},{2,9},{4,11},{6,13},{8,15},... | collective-permute-start | bytes 3080 | tf_op jit(solution)/shard_map/ppermute | solution.py:308
  15.0 1.0 copy-start.9
  16.0 0.9 copy-start.11
  17.0 0.9 copy-start.25
  17.9 20.7 %copy-start = (bf16[16,8,64,64]{3,2,1,0:T(8,128)(2,1)S(1)}, bf16[16,8,64,64]{3,2,1,0:T(8,128)(2,1)}, u32[]{:S(2)}) copy-start(bf16[16,8,64,64]{3,2,1,0:T(8,128)(2,1)} %far_blocks.3) | copy-start | bytes 3145732
  17.9 20.7 %copy-start.27 = (s32[16,8]{0,1:T(8,128)S(1)}, s32[16,8]{0,1:T(8,128)}, u32[]{:S(2)}) copy-start(s32[16,8]{0,1:T(8,128)} %param.18) | copy-start | bytes 1540
  17.9 20.7 %copy-start.28 = (s32[16,8]{0,1:T(8,128)S(1)}, s32[16,8]{0,1:T(8,128)}, u32[]{:S(2)}) copy-start(s32[16,8]{0,1:T(8,128)} %param.16) | copy-start | bytes 1540
  17.9 20.7 %copy-start.29 = (s32[1,2,72]{2,1,0:T(2,128)S(1)}, s32[1,2,72]{2,1,0:T(2,128)}, u32[]{:S(2)}) copy-start(s32[1,2,72]{2,1,0:T(2,128)} %refs_1_.3) | copy-start | bytes 1732
  17.9 20.7 %copy-start.30 = (s32[1,2,24]{2,1,0:T(2,128)S(1)}, s32[1,2,24]{2,1,0:T(2,128)}, u32[]{:S(2)}) copy-start(s32[1,2,24]{2,1,0:T(2,128)} %refs_2_.3) | copy-start | bytes 580
  19.3 34.4 %all-to-all-start = ((bf16[8,64,128]{2,1,0:T(8,128)(2,1)}), bf16[8,64,128]{2,1,0:T(8,128)(2,1)}, u32[]{:S(2)}, u32[]{:S(2)}) async-start(bf16[8,64,128]{2,1,0:T(8,128)(2,1)} %get-tuple-element.21), calls=%async_computation | async-start | bytes 262144 | tf_op jit(solution)/shard_map/all_to_all | solution.py:329
  25.8 6.5 %copy-start.7 = (bf16[32,64,128]{2,1,0:T(8,128)(2,1)}, bf16[32,64,128]{2,1,0:T(8,128)(2,1)S(1)}, u32[]{:S(2)}) copy-start(bf16[32,64,128]{2,1,0:T(8,128)(2,1)S(1)} %all-gather.1) | copy-start | bytes 1572868
  25.8 6.5 %copy-start.33 = (s32[2,128]{1,0:T(2,128)}, s32[2,128]{1,0:T(2,128)S(1)}, u32[]{:S(2)}) copy-start(s32[2,128]{1,0:T(2,128)S(1)} %collective-permute-done.refs_0_) | copy-start | bytes 3076
  25.8 6.5 %copy-start.35 = (s32[2,128]{1,0:T(2,128)}, s32[2,128]{1,0:T(2,128)S(1)}, u32[]{:S(2)}) copy-start(s32[2,128]{1,0:T(2,128)S(1)} %collective-permute-done.1.refs_1_) | copy-start | bytes 3076
  25.8 6.5 %copy-start.37 = (s32[2,128]{1,0:T(2,128)}, s32[2,128]{1,0:T(2,128)S(1)}, u32[]{:S(2)}) copy-start(s32[2,128]{1,0:T(2,128)S(1)} %collective-permute-done.2.refs_2_) | copy-start | bytes 3076
  28.0 28.1 %collective-permute-start.3 = (bf16[16,64,128]{2,1,0:T(8,128)(2,1)}, bf16[16,64,128]{2,1,0:T(8,128)(2,1)}, u32[]{:S(2)}, u32[]{:S(2)}) collective-permute-start(bf16[16,64,128]{2,1,0:T(8,128)(2,1)} %get-tuple-element.18), channel_id=1, source_target_pairs={{0,2},{2,4},{4,6},{6,8},{8,10},{10,12},{12,14},{3,1},{5,3},{7,5},{... | collective-permute-start | bytes 786440 | tf_op jit(solution)/shard_map/ppermute | solution.py:327
  32.3 26.2 %collective-permute-start.4 = (bf16[16,64,128]{2,1,0:T(8,128)(2,1)}, bf16[16,64,128]{2,1,0:T(8,128)(2,1)}, u32[]{:S(2)}, u32[]{:S(2)}) collective-permute-start(bf16[16,64,128]{2,1,0:T(8,128)(2,1)} %get-tuple-element.19), channel_id=1, source_target_pairs={{0,4},{2,6},{4,8},{6,10},{8,12},{10,14},{5,1},{7,3},{9,5},{11,7},{... | collective-permute-start | bytes 786440 | tf_op jit(solution)/shard_map/ppermute | solution.py:327
  38.6 1.6 %copy-start.1 = (bf16[16,8,64,64]{3,2,1,0:T(8,128)(2,1)S(1)}, bf16[16,8,64,64]{3,2,1,0:T(8,128)(2,1)}, u32[]{:S(2)}) copy-start(bf16[16,8,64,64]{3,2,1,0:T(8,128)(2,1)} %near_blocks.3) | copy-start | bytes 3145732
  40.2 1.0 copy-start.3
  41.2 1.0 copy-start.8
  47.7 0.8 copy-start.16
  48.5 0.8 copy-start.18
  49.3 13.9 %copy-start.10 = (bf16[16,64,64]{2,1,0:T(8,128)(2,1)S(1)}, bf16[16,64,64]{2,1,0:T(8,128)(2,1)}, u32[]{:S(2)}) copy-start(bf16[16,64,64]{2,1,0:T(8,128)(2,1)} %refs_13_.3) | copy-start | bytes 393220
  49.3 11.5 %collective-permute-start.5 = (bf16[16,64,128]{2,1,0:T(8,128)(2,1)}, bf16[16,64,128]{2,1,0:T(8,128)(2,1)}, u32[]{:S(2)}, u32[]{:S(2)}) collective-permute-start(bf16[16,64,128]{2,1,0:T(8,128)(2,1)} %get-tuple-element.20), channel_id=1, source_target_pairs={{0,6},{2,8},{4,10},{6,12},{8,14},{7,1},{9,3},{11,5},{13,7},{15,9},... | collective-permute-start | bytes 786440 | tf_op jit(solution)/shard_map/ppermute | solution.py:327
  53.7 9.5 %copy-start.4 = (bf16[1,24,64,64]{3,2,1,0:T(8,128)(2,1)S(1)}, bf16[1,24,64,64]{3,2,1,0:T(8,128)(2,1)}, u32[]{:S(2)}) copy-start(bf16[1,24,64,64]{3,2,1,0:T(8,128)(2,1)} %param.21) | copy-start | bytes 589828
  53.7 9.5 %copy-start.12 = (bf16[16,64,64]{2,1,0:T(8,128)(2,1)S(1)}, bf16[16,64,64]{2,1,0:T(8,128)(2,1)}, u32[]{:S(2)}) copy-start(bf16[16,64,64]{2,1,0:T(8,128)(2,1)} %refs_14_.3) | copy-start | bytes 393220
  53.7 9.5 %copy-start.14 = (bf16[1,32,64,64]{3,2,1,0:T(8,128)(2,1)S(1)}, bf16[1,32,64,64]{3,2,1,0:T(8,128)(2,1)}, u32[]{:S(2)}) copy-start(bf16[1,32,64,64]{3,2,1,0:T(8,128)(2,1)} %param.25) | copy-start | bytes 786436
  53.7 9.5 %copy-start.17 = (f32[17,64,64]{2,1,0:T(8,128)S(1)}, f32[17,64,64]{2,1,0:T(8,128)}, u32[]{:S(2)}) copy-start(f32[17,64,64]{2,1,0:T(8,128)} %copy-done.16) | copy-start | bytes 835588
  53.8 9.5 %copy-start.19 = (f32[17,64,64]{2,1,0:T(8,128)S(1)}, f32[17,64,64]{2,1,0:T(8,128)}, u32[]{:S(2)}) copy-start(f32[17,64,64]{2,1,0:T(8,128)} %copy-done.18) | copy-start | bytes 835588
  63.3 0.7 copy-start.31
  68.2 0.7 copy-start.24
  68.9 0.7 copy-start.26
  69.5 32.3 %all-to-all-start.1 = ((bf16[8,64,128]{2,1,0:T(8,128)(2,1)}), bf16[8,64,128]{2,1,0:T(8,128)(2,1)}, u32[]{:S(2)}, u32[]{:S(2)}) async-start(bf16[8,64,128]{2,1,0:T(8,128)(2,1)} %copy-done.26), calls=%async_computation.1 | async-start | bytes 262144 | tf_op jit(solution)/shard_map/all_to_all | solution.py:329
  77.2 0.7 copy-start.38
  79.9 24.3 %collective-permute-start.6 = (bf16[16,64,128]{2,1,0:T(8,128)(2,1)}, bf16[16,64,128]{2,1,0:T(8,128)(2,1)}, u32[]{:S(2)}, u32[]{:S(2)}) collective-permute-start(bf16[16,64,128]{2,1,0:T(8,128)(2,1)} %get-tuple-element.26), channel_id=1, source_target_pairs={{0,2},{2,4},{4,6},{6,8},{8,10},{10,12},{12,14},{3,1},{5,3},{7,5},{... | collective-permute-start | bytes 786440 | tf_op jit(solution)/shard_map/ppermute | solution.py:327
  84.4 22.2 %collective-permute-start.7 = (bf16[16,64,128]{2,1,0:T(8,128)(2,1)}, bf16[16,64,128]{2,1,0:T(8,128)(2,1)}, u32[]{:S(2)}, u32[]{:S(2)}) collective-permute-start(bf16[16,64,128]{2,1,0:T(8,128)(2,1)} %get-tuple-element.27), channel_id=1, source_target_pairs={{0,4},{2,6},{4,8},{6,10},{8,12},{10,14},{5,1},{7,3},{9,5},{11,7},{... | collective-permute-start | bytes 786440 | tf_op jit(solution)/shard_map/ppermute | solution.py:327
  87.8 21.2 %collective-permute-start.8 = (bf16[16,64,128]{2,1,0:T(8,128)(2,1)}, bf16[16,64,128]{2,1,0:T(8,128)(2,1)}, u32[]{:S(2)}, u32[]{:S(2)}) collective-permute-start(bf16[16,64,128]{2,1,0:T(8,128)(2,1)} %get-tuple-element.28), channel_id=1, source_target_pairs={{0,6},{2,8},{4,10},{6,12},{8,14},{7,1},{9,3},{11,5},{13,7},{15,9},... | collective-permute-start | bytes 786440 | tf_op jit(solution)/shard_map/ppermute | solution.py:327
  92.1 1.6 %copy-start.2 = (bf16[16,8,64,64]{3,2,1,0:T(8,128)(2,1)S(1)}, bf16[16,8,64,64]{3,2,1,0:T(8,128)(2,1)}, u32[]{:S(2)}) copy-start(bf16[16,8,64,64]{3,2,1,0:T(8,128)(2,1)} %near_blocks.3) | copy-start | bytes 3145732
  93.7 1.0 copy-start.5
  100.2 0.8 copy-start.20
  101.0 0.8 copy-start.22
  101.8 9.5 %copy-start.6 = (bf16[1,24,64,64]{3,2,1,0:T(8,128)(2,1)S(1)}, bf16[1,24,64,64]{3,2,1,0:T(8,128)(2,1)}, u32[]{:S(2)}) copy-start(bf16[1,24,64,64]{3,2,1,0:T(8,128)(2,1)} %param.21) | copy-start | bytes 589828
  101.8 9.5 %copy-start.13 = (bf16[16,64,64]{2,1,0:T(8,128)(2,1)S(1)}, bf16[16,64,64]{2,1,0:T(8,128)(2,1)}, u32[]{:S(2)}) copy-start(bf16[16,64,64]{2,1,0:T(8,128)(2,1)} %refs_14_.3) | copy-start | bytes 393220
  101.8 9.5 %copy-start.15 = (bf16[1,32,64,64]{3,2,1,0:T(8,128)(2,1)S(1)}, bf16[1,32,64,64]{3,2,1,0:T(8,128)(2,1)}, u32[]{:S(2)}) copy-start(bf16[1,32,64,64]{3,2,1,0:T(8,128)(2,1)} %param.25) | copy-start | bytes 786436
  101.8 9.5 %copy-start.32 = (s32[1,2,32]{2,1,0:T(2,128)S(1)}, s32[1,2,32]{2,1,0:T(2,128)}, u32[]{:S(2)}) copy-start(s32[1,2,32]{2,1,0:T(2,128)} %refs_3_.3) | copy-start | bytes 772
  101.8 9.5 %copy-start.21 = (f32[17,64,64]{2,1,0:T(8,128)S(1)}, f32[17,64,64]{2,1,0:T(8,128)}, u32[]{:S(2)}) copy-start(f32[17,64,64]{2,1,0:T(8,128)} %copy-done.20) | copy-start | bytes 835588
  101.8 9.5 %copy-start.23 = (f32[17,64,64]{2,1,0:T(8,128)S(1)}, f32[17,64,64]{2,1,0:T(8,128)}, u32[]{:S(2)}) copy-start(f32[17,64,64]{2,1,0:T(8,128)} %copy-done.22) | copy-start | bytes 835588
  (2 other events, 1.2 us)

commit v2 on v1

--- a/solution.py
+++ b/solution.py
@@ -18,7 +18,7 @@
 BF16 = jnp.bfloat16
 VMEM = pl.BlockSpec(memory_space=pltpu.VMEM)
 SMEM = pl.BlockSpec(memory_space=pltpu.SMEM)
-PARAMS = pltpu.CompilerParams(vmem_limit_bytes=24 * 1024 * 1024)
+PARAMS = pltpu.CompilerParams(vmem_limit_bytes=60 * 1024 * 1024)
 
 
 def nn(a, b):
@@ -31,10 +31,6 @@
 
 def beside(a, b):
     return jnp.concatenate([a, b], axis=1)
-
-
-def chip_groups(devices):
-    return [[2 * c, 2 * c + 1] for c in range(devices // 2)]
 
 
 def outward(devices, by):
@@ -43,10 +39,8 @@
     return up + [(2 * c + 1, 2 * (c - by) + 1) for c in range(chips) if c - by >= 0]
 
 
-def asking(devices, by):
-    chips = devices // 2
-    down = [(2 * c + 1, 2 * (c - by)) for c in range(chips) if c - by >= 0]
-    return down + [(2 * c, 2 * (c + by) + 1) for c in range(chips) if c + by < chips]
+def mates(devices):
+    return [(i, i ^ 1) for i in range(devices)]
 
 
 def offset_index(off):
@@ -79,13 +73,22 @@
     lift_tiles(tiles, basis, transfer, own, up)
 
 
-def turn_tables(both, table):
-    cores, count = both.shape[0], both.shape[1]
-    for core in range(cores):
-        for i in range(count):
-            tile = both[core, i]
-            table[0, core * count + i] = tile
-            table[1, core * count + i] = beside(tile[:, 64:], tile[:, :64])
+def turn_tables(sources, table):
+    row = 0
+    for ref in sources:
+        for i in range(ref.shape[0]):
+            tile = ref[i]
+            table[0, row] = tile
+            table[1, row] = beside(tile[:, 64:], tile[:, :64])
+            row += 1
+
+
+def ask_kernel(far_plan, near_plan, out):
+    far, near = far_plan[0, 0:1, :], near_plan[0, 0:1, :]
+    blank = jnp.zeros((1, 128 - far.shape[1] - near.shape[1]), jnp.int32)
+    row = jnp.concatenate([far, near, blank], axis=1)
+    for i in range(out.shape[0]):
+        out[i] = row
 
 
 def at_left(table, base, leaf):
@@ -104,43 +107,44 @@
     return lax.broadcasted_iota(jnp.int32, (64, 128), 1) < 64
 
 
-def pack_kernel(core_ref, *refs):
-    asks = refs[:REACH]
-    both = refs[REACH]
-    outs = refs[REACH + 1 : REACH + 1 + REACH]
-    table = refs[-1]
-    core = core_ref[0]
-    turn_tables(both, table)
+def pack_kernel(place_ref, asks, own, mate, *refs):
+    outs, table = refs[:REACH], refs[REACH]
+    core, chip = place_ref[0], place_ref[1]
+    chips = asks.shape[0] // 2
+    turn_tables((own, mate), table)
     left = left_mask()
-    half = both.shape[1]
+    half = own.shape[0]
     for step in range(REACH):
-        ask, out = asks[step], outs[step]
+        out = outs[step]
         toward = jnp.where(core == 0, -2 * (step + 1), 2 * (step + 1))
-        for target in range(2):
-            for source in range(2):
+        asker = jnp.clip(chip - toward // 2, 0, chips - 1)
+        for other_target in range(2):
+            target = jnp.where(core == other_target, 0, 1)
+            for other_source in range(2):
+                source = jnp.where(core == other_source, 0, 1)
                 order = offset_index(toward + source - target)
                 for i in range(PAIR_TILES):
                     if i < FAR_TILES:
                         at = order * CAP0 + 2 * i
-                        base = source * half
+                        base = other_source * half
                     else:
                         at = OFFSETS * CAP0 + order * CAPN + 2 * (i - FAR_TILES)
-                        base = source * half + half // 2
-                    first = jnp.maximum(ask[target, at], 0)
-                    second = jnp.maximum(ask[target, at + 1], 0)
-                    out[(target * 2 + source) * PAIR_TILES + i] = pair_of(
+                        base = other_source * half + half // 2
+                    first = jnp.maximum(asks[2 * asker + target, 0, at], 0)
+                    second = jnp.maximum(asks[2 * asker + target, 0, at + 1], 0)
+                    out[(other_target * 2 + other_source) * PAIR_TILES + i] = pair_of(
                         table, base, first, second, left
                     )
 
 
 def local_kernel(
-    core_ref, far_list, near_list, far_plan, near_plan, both, far_blocks, near_blocks, far_remote,
-    near_remote, far_out, near_out, table
+    place_ref, far_list, near_list, far_plan, near_plan, own, mate, far_blocks, near_blocks,
+    far_remote, near_remote, far_out, near_out, table
 ):
-    core = core_ref[0]
-    turn_tables(both, table)
+    core = place_ref[0]
+    turn_tables((own, mate), table)
     left = left_mask()
-    half = both.shape[1]
+    half = own.shape[0]
     leaves = far_blocks.shape[0]
 
     def one_leaf(leaf, carry):
@@ -148,7 +152,7 @@
             (far_list, far_blocks, far_out, 0),
             (near_list, near_blocks, near_out, 1),
         ):
-            base = core * half + kind * (half // 2)
+            base = kind * (half // 2)
             total = jnp.zeros((64, 64), F32)
             for k in range(0, blocks.shape[1], 2):
                 x = pair_of(table, base, listed[k, leaf], listed[k + 1, leaf], left)
@@ -162,7 +166,7 @@
         (far_plan, far_remote, far_out, 0, CAP0),
         (near_plan, near_remote, near_out, 1, CAPN),
     ):
-        base = (1 - core) * half + kind * (half // 2)
+        base = half + kind * (half // 2)
         out[leaves] = jnp.zeros((64, 64), F32)
         for c in range(cap):
             slot = order * cap + c
@@ -173,21 +177,26 @@
 
 
 def combine(
-    core_ref, far_plan, near_plan, parent_plan, arrived, parents, far_in, near_in, far_remote,
-    near_remote, parent_remote, basis, transfer, far_acc, near_acc
+    place_ref, far_plan, near_plan, parent_plan, arrived, parents, swapped, far_in, near_in,
+    far_remote, near_remote, parent_remote, basis, transfer, far_acc, near_acc
 ):
-    core = core_ref[0]
+    core = place_ref[0]
     leaves = basis.shape[0]
+    per_step = 2 * PAIR_TILES
     far_acc[...] = far_in[...]
     near_acc[...] = near_in[...]
     for step in range(REACH):
         for side in range(2):
-            for source in range(2):
-                off = (2 * side - 1) * 2 * (step + 1) + source - core
+            for other in range(2):
+                sender = jnp.where(core == side, 0, 1)
+                source = jnp.where(sender == other, 0, 1)
+                away = jnp.where(sender == 0, -2 * (step + 1), 2 * (step + 1))
+                off = away + source - core
                 inside = jnp.logical_and(off >= -HOPS, off <= HOPS)
                 order = offset_index(off)
                 for i in range(PAIR_TILES):
-                    tile = arrived[step][side, (core * 2 + source) * PAIR_TILES + i]
+                    row = other * PAIR_TILES + i
+                    tile = swapped[step * per_step + row] if side else arrived[step][row]
                     if i < FAR_TILES:
                         plan, blocks, acc = far_plan, far_remote, far_acc
                         slot = order * CAP0 + 2 * i
@@ -201,12 +210,13 @@
                         x = tile[:, 64 * c : 64 * (c + 1)]
                         acc[where] = acc[where] + nt(x, blocks[slot + c])
 
-    chips = parents.shape[1]
+    chips = parents.shape[0]
     left = left_mask()
 
     def one_chip(chip, total):
-        for member in range(2):
-            tile = parents[member, chip]
+        for side in range(2):
+            tile = swapped[REACH * per_step + chip] if side else parents[chip]
+            member = jnp.where(core == side, 0, 1)
             turned = beside(tile[:, 64:], tile[:, :64])
             slot = (2 * chip + member) * 2
             s0, s1 = parent_plan[0, 0, slot], parent_plan[0, 0, slot + 1]
@@ -243,9 +253,9 @@
 
 
 def split_refs(refs):
-    core_ref, far_plan, near_plan, parent_plan = refs[:4]
+    place_ref, far_plan, near_plan, parent_plan = refs[:4]
     arrived = refs[4 : 4 + REACH]
-    return (core_ref, far_plan, near_plan, parent_plan, arrived) + tuple(refs[4 + REACH :])
+    return (place_ref, far_plan, near_plan, parent_plan, arrived) + tuple(refs[4 + REACH :])
 
 
 def middle_kernel(*refs):
@@ -274,7 +284,7 @@
         out_specs=jax.tree.map(lambda _: VMEM, outs),
         scratch_shapes=scratch,
         compiler_params=PARAMS,
-        cost_estimate=pl.CostEstimate(flops=flops, bytes_accessed=size, transcendentals=0),
+        cost_estimate=pl.CostEstimate(flops=int(flops), bytes_accessed=size, transcendentals=0),
     )(*args)
 
 
@@ -295,17 +305,12 @@
 ):
     devices = lax.axis_size("clu")
     chips = devices // 2
-    groups = chip_groups(devices)
     leaves = basis.shape[0]
-    core = (lax.axis_index("clu") % 2).astype(jnp.int32).reshape(1)
+    at = lax.axis_index("clu").astype(jnp.int32)
+    place = jnp.stack([at & 1, at >> 1])
     near_remote, far_remote, parent_remote = near_remote[0], far_remote[0], parent_remote[0]
     far_list, near_list = far_list.T, near_list.T
     same_core = [[2 * c + k for c in range(chips)] for k in range(2)]
-
-    asks = jnp.concatenate([far_plan[0, 0], near_plan[0, 0]])
-    asks = jnp.pad(asks, (0, 128 - asks.shape[0]))[None]
-    asks = lax.all_gather(asks, "clu", tiled=True, axis_index_groups=groups)
-    asked = [lax.ppermute(asks, "clu", asking(devices, d + 1)) for d in range(REACH)]
 
     shape = jax.ShapeDtypeStruct
     own_shape = shape((leaves, 64, 128), BF16)
@@ -317,42 +322,47 @@
     message = shape((4 * PAIR_TILES, 64, 128), BF16)
     block = 2 * 64**3
 
+    asks = call(
+        ask_kernel, "vv", shape((devices, 1, 128), jnp.int32), [], (far_plan, near_plan), 1000
+    )
+    asks = lax.all_to_all(asks, "clu", 0, 0, tiled=True)
+
     def exchange(own, up):
-        both = lax.all_gather(own, "clu", axis_index_groups=groups)
+        parents = lax.all_to_all(up, "clu", 0, 0, tiled=True, axis_index_groups=same_core)
+        mate = lax.ppermute(own, "clu", mates(devices))
         packed = call(
-            pack_kernel, "s" * (1 + REACH) + "v", [message] * REACH, table_scratch,
-            (core, *asked, both), 1000,
+            pack_kernel, "ssvv", [message] * REACH, table_scratch, (place, asks, own, mate), 2e9
         )
-        moved = [
+        arrived = [
             lax.ppermute(m, "clu", outward(devices, d + 1)) for d, m in enumerate(packed)
         ]
-        parents = lax.all_to_all(
-            up, "clu", 0, 0, tiled=True, axis_index_groups=same_core
+        far_acc, near_acc = call(
+            local_kernel, "sssss" + "v" * 6, [acc_shape] * 2, table_scratch,
+            (place, far_list, near_list, far_plan, near_plan, own, mate, far_blocks, near_blocks,
+             far_remote, near_remote),
+            7e9,
         )
-        parents = lax.all_gather(parents, "clu", axis_index_groups=groups)
-        far_acc, near_acc = call(
-            local_kernel, "sssssvvvvv", [acc_shape] * 2, table_scratch,
-            (core, far_list, near_list, far_plan, near_plan, both, far_blocks, near_blocks,
-             far_remote, near_remote),
-            2 * 8 * leaves * block,
+        arrived, parents, far_acc, near_acc = lax.optimization_barrier(
+            (arrived, parents, far_acc, near_acc)
         )
-        arrived = [lax.all_gather(m, "clu", axis_index_groups=groups) for m in moved]
+        swapped = jnp.concatenate([m[2 * PAIR_TILES :] for m in arrived] + [parents])
+        swapped = lax.ppermute(swapped, "clu", mates(devices))
         return (
-            core, far_plan, near_plan, parent_plan, *arrived, parents, far_acc, near_acc,
-            far_remote, near_remote, parent_remote, basis, transfer,
+            place, far_plan, near_plan, parent_plan, *arrived, parents, swapped, far_acc,
+            near_acc, far_remote, near_remote, parent_remote, basis, transfer,
         )
 
-    kinds = "ssss" + "v" * (REACH + 8)
+    kinds = "ssss" + "v" * (REACH + 9)
     own, up = call(
         lift_kernel, "vvv", [own_shape, up_shape], [], (values.T, basis, transfer),
-        2 * leaves * block,
+        1e9,
     )
     first, own, up = call(
         middle_kernel, kinds, [out_shape, own_shape, up_shape], acc_scratch, exchange(own, up),
-        150 * block,
+        4e9,
     )
     second = call(
-        last_kernel, kinds, out_shape, acc_scratch, exchange(own, up), 150 * block
+        last_kernel, kinds, out_shape, acc_scratch, exchange(own, up), 4e9
     )
     return first.T, second.T
 

time: 116 us -> 90.8 us (0.78)
  blocking collectives: 25.8 us -> 0 us
  local copies, waits for them, and re-layouts: 20.4 us -> 5.65 us
  Pallas kernels: 24.7 us -> 38.3 us
  waiting for transfers between devices: 0.03 us -> 6.93 us
  starting transfers between devices: 43.4 us -> 37.5 us
    all_gather x11 -> x0, blocking collectives: 25.8 us -> none  [the longest x6 14.3 us: exchange(): lax.all_gather(m, 'clu', axis_index_groups=groups)]
    pallas_call x7 -> x8, Pallas kernels: 24.7 us -> 38.3 us  [call(): pl.pallas_call(kernel, out_shape=outs, in_specs=[SMEM if k == 's' else VM...]
    unnamed x80 -> x29, local copies, waits for them, and re-layouts: 19 us -> 5.59 us
    ppermute x3 -> x4, starting transfers between devices: 11 us -> 0.73 us  [the longest x2 0.59 us: exchange(): mate = lax.ppermute(own, 'clu', mates(devices))]
    all_to_all x0 -> x1, starting transfers between devices: none -> 7.05 us  [on_device(): asks = lax.all_to_all(asks, 'clu', 0, 0, tiled=True)]
    ppermute x3 -> x4, waiting for transfers between devices: 0.01 us -> 3.8 us  [the longest x2 3.79 us: exchange(): swapped = lax.ppermute(swapped, 'clu', mates(devices))]
    all_to_all x0 -> x1, waiting for transfers between devices: none -> 3.11 us  [on_device(): asks = lax.all_to_all(asks, 'clu', 0, 0, tiled=True)]
    squeeze x2 -> x0, local copies, waits for them, and re-layouts: 1.36 us -> none  [on_device(): asks = jnp.concatenate([far_plan[0, 0], near_plan[0, 0]])]
  transfers between devices with their start and end apart: 11 -> 13, of which waited for: 0 -> 3; matrix products, arithmetic and copies ran while one was open for 2% -> 4% of each run, Pallas kernels for 14% -> 26%
where the time goes in v2:
time: 90.8 us; the launch traced here: 90.2 us
  Pallas kernels  38.3 us (42%)
  starting transfers between devices  37.5 us (41%)
  waiting for transfers between devices  6.93 us (8%)
  local copies, waits for them, and re-layouts  5.65 us (6%)
  between operations  0.98 us (1%)
    pallas_call x8, Pallas kernels, call(): pl.pallas_call(kernel, out_shape=outs, in_specs=[SMEM if k == 's' else VM...  38.3 us
    ppermute x6, starting transfers between devices, exchange(): lax.ppermute(m, 'clu', outward(devices, d + 1))  23 us
    all_to_all x1, starting transfers between devices, on_device(): asks = lax.all_to_all(asks, 'clu', 0, 0, tiled=True)  7.05 us
    all_to_all x2, starting transfers between devices, exchange(): lax.all_to_all(up, 'clu', 0, 0, tiled=True, axis_index_groups=same_core)  6.74 us
    unnamed x29, local copies, waits for them, and re-layouts  5.59 us
    ppermute x2, waiting for transfers between devices, exchange(): swapped = lax.ppermute(swapped, 'clu', mates(devices))  3.79 us
    all_to_all x1, waiting for transfers between devices, on_device(): asks = lax.all_to_all(asks, 'clu', 0, 0, tiled=True)  3.11 us
  transfers between devices with their start and end apart: 13, of which 3 were waited for; matrix products, arithmetic and copies ran while one was open for 4% of the time, Pallas kernels for 26%

profile of v2, /device:TPU:0, one launch (start us, length us, event | category | flops | bytes accessed | tf_op | source)
XLA Modules:
  0.0 90.2 jit_solution(11438987005637401569)
XLA Ops:
  0.6 0.0 copy-start
  0.6 2.6 %shard_map.141 = (bf16[16,64,128]{2,1,0:T(8,128)(2,1)}, bf16[8,64,128]{2,1,0:T(8,128)(2,1)}) custom-call(bf16[64,1024]{1,0:T(8,128)(2,1)} %bitcast.20, bf16[16,64,64]{2,1,0:T(8,128)(2,1)} %refs_14_.3, bf16[16,64,64]{2,1,0:T(8,128)(2,1)} %refs_15_.3), custom_call_target="tpu_custom_call" | custom-call | flops 1000000000 | bytes 393216 | tf_op jit(solution)/shard_map/pallas_call | solution.py:280
  3.2 0.5 collective-permute-start
  3.7 1.4 %shard_map.140 = s32[16,1,128]{2,1,0:T(1,128)} custom-call(s32[1,2,72]{2,1,0:T(2,128)} %refs_1_.3, s32[1,2,24]{2,1,0:T(2,128)} %refs_2_.3), custom_call_target="tpu_custom_call" | custom-call | flops 1000 | bytes 768 | tf_op jit(solution)/shard_map/pallas_call | solution.py:280
  5.0 7.0 %all-to-all-start = ((s32[16,1,128]{2,1,0:T(1,128)}), s32[16,1,128]{2,1,0:T(1,128)S(1)}, u32[]{:S(2)}, u32[]{:S(2)}) async-start(s32[16,1,128]{2,1,0:T(1,128)} %shard_map.140), calls=%async_computation | async-start | bytes 16384 | tf_op jit(solution)/shard_map/all_to_all | solution.py:328
  12.1 0.7 pad_add_fusion.place_ref.refs_0_
  12.8 2.6 %copy.15 = bf16[1,72,64,64]{3,2,1,0:T(8,128)(2,1)} copy(bf16[1,72,64,64]{1,3,2,0:T(8,128)(2,1)S(1)} %copy-done) | data formatting | bytes 1179648 | tf_op args[10]
  15.3 3.1 %all-to-all-done.asks = s32[16,1,128]{2,1,0:T(1,128)S(1)} async-done(((s32[16,1,128]{2,1,0:T(1,128)}), s32[16,1,128]{2,1,0:T(1,128)S(1)}, u32[]{:S(2)}, u32[]{:S(2)}) %all-to-all-start) | async-done | bytes 8224 | tf_op jit(solution)/shard_map/all_to_all | solution.py:328
  18.4 3.4 %all-to-all-start.1 = ((bf16[8,64,128]{2,1,0:T(8,128)(2,1)}), bf16[8,64,128]{2,1,0:T(8,128)(2,1)S(1)}, u32[]{:S(2)}, u32[]{:S(2)}) async-start(bf16[8,64,128]{2,1,0:T(8,128)(2,1)} %get-tuple-element.33), calls=%async_computation.1 | async-start | bytes 262144 | tf_op jit(solution)/shard_map/all_to_all | solution.py:331
  21.8 0.0 collective-permute-done.mate
  21.8 0.7 copy-done.12
  22.5 2.6 %shard_map.142 = (bf16[16,64,128]{2,1,0:T(8,128)(2,1)}, bf16[16,64,128]{2,1,0:T(8,128)(2,1)}, bf16[16,64,128]{2,1,0:T(8,128)(2,1)}) custom-call(s32[2]{0:T(128)} %pad_add_fusion.place_ref.refs_0_, s32[16,1,128]{2,1,0:T(1,128)} %copy-done.9, bf16[16,64,128]{2,1,0:T(8,128)(2,1)} %get-tuple-element.29.own, bf16[16,64,128]{2,1,0:T(8,128)(2,1)} %copy-done.12), custom_call_target="tpu_custom_call" | custom-call | flops 2000000000 | bytes 532488 | tf_op jit(solution)/shard_map/pallas_call | solution.py:280
  25.2 3.8 %collective-permute-start.1 = (bf16[16,64,128]{2,1,0:T(8,128)(2,1)}, bf16[16,64,128]{2,1,0:T(8,128)(2,1)S(1)}, u32[]{:S(2)}, u32[]{:S(2)}) collective-permute-start(bf16[16,64,128]{2,1,0:T(8,128)(2,1)} %get-tuple-element.30), channel_id=1, source_target_pairs={{0,2},{2,4},{4,6},{6,8},{8,10},{10,12},{12,14},{3,1},{5,3},{7,5},{... | collective-permute-start | bytes 786440 | tf_op jit(solution)/shard_map/ppermute | solution.py:337
  29.0 3.4 %collective-permute-start.2 = (bf16[16,64,128]{2,1,0:T(8,128)(2,1)}, bf16[16,64,128]{2,1,0:T(8,128)(2,1)S(1)}, u32[]{:S(2)}, u32[]{:S(2)}) collective-permute-start(bf16[16,64,128]{2,1,0:T(8,128)(2,1)} %get-tuple-element.31), channel_id=1, source_target_pairs={{0,4},{2,6},{4,8},{6,10},{8,12},{10,14},{5,1},{7,3},{9,5},{11,7},{... | collective-permute-start | bytes 786440 | tf_op jit(solution)/shard_map/ppermute | solution.py:337
  32.4 4.3 %collective-permute-start.3 = (bf16[16,64,128]{2,1,0:T(8,128)(2,1)}, bf16[16,64,128]{2,1,0:T(8,128)(2,1)S(1)}, u32[]{:S(2)}, u32[]{:S(2)}) collective-permute-start(bf16[16,64,128]{2,1,0:T(8,128)(2,1)} %get-tuple-element.32), channel_id=1, source_target_pairs={{0,6},{2,8},{4,10},{6,12},{8,14},{7,1},{9,3},{11,5},{13,7},{15,9},... | collective-permute-start | bytes 786440 | tf_op jit(solution)/shard_map/ppermute | solution.py:337
  36.7 8.5 %shard_map.143 = (f32[17,64,64]{2,1,0:T(8,128)}, f32[17,64,64]{2,1,0:T(8,128)}) custom-call(s32[2]{0:T(128)} %pad_add_fusion.place_ref.refs_0_, s32[8,16]{1,0:T(8,128)} %bitcast.21, s32[8,16]{1,0:T(8,128)} %bitcast.23, s32[1,2,72]{2,1,0:T(2,128)} %refs_1_.3, s32[1,2,24]{2,1,0:T(2,128)} %refs_2_.3, bf16[16,64,128]{2,1,0:T(8,128)(2,1)} %get-tuple-element.29.own, ...), custom_call_target="tpu_custom_call" | custom-call | flops 7000000000 | bytes 3409672 | tf_op jit(solution)/shard_map/pallas_call | solution.py:280
  45.2 0.0 all-to-all-done.1.refs_7_
  45.2 0.0 collective-permute-done.1.refs_4_
  45.2 0.0 collective-permute-done.2.refs_5_
  45.3 0.0 collective-permute-done.3.refs_6_
  45.3 0.0 copy-start.7
  45.3 0.1 pad_maximum_fusion
  45.4 0.1 collective-permute-start.4
  45.5 1.9 %collective-permute-done.4.refs_8_ = bf16[32,64,128]{2,1,0:T(8,128)(2,1)S(1)} collective-permute-done((bf16[32,64,128]{2,1,0:T(8,128)(2,1)S(1)}, bf16[32,64,128]{2,1,0:T(8,128)(2,1)S(1)}, u32[]{:S(2)}, u32[]{:S(2)}) %collective-permute-start.4) | collective-permute-done | bytes 524320 | tf_op jit(solution)/shard_map/ppermute | solution.py:349
  47.4 0.0 copy-done.5
  47.4 0.8 copy-done.10
  48.2 6.3 %shard_map.144 = (bf16[64,1024]{1,0:T(8,128)(2,1)}, bf16[16,64,128]{2,1,0:T(8,128)(2,1)}, bf16[8,64,128]{2,1,0:T(8,128)(2,1)}) custom-call(s32[2]{0:T(128)} %pad_add_fusion.place_ref.refs_0_, s32[1,2,72]{2,1,0:T(2,128)} %refs_1_.3, s32[1,2,24]{2,1,0:T(2,128)} %refs_2_.3, s32[1,2,32]{2,1,0:T(2,128)} %refs_3_.3, bf16[16,64,128]{2,1,0:T(8,128)(2,1)} %copy-done.3, ...), custom_call_target="tpu_custom_call" | custom-call | flops 4000000000 | bytes 3310600 | tf_op jit(solution)/shard_map/pallas_call | solution.py:280
  54.5 0.1 collective-permute-start.5
  54.7 3.4 %all-to-all-start.2 = ((bf16[8,64,128]{2,1,0:T(8,128)(2,1)}), bf16[8,64,128]{2,1,0:T(8,128)(2,1)S(1)}, u32[]{:S(2)}, u32[]{:S(2)}) async-start(bf16[8,64,128]{2,1,0:T(8,128)(2,1)} %get-tuple-element.47), calls=%async_computation.2 | async-start | bytes 262144 | tf_op jit(solution)/shard_map/all_to_all | solution.py:331
  58.0 0.0 collective-permute-done.5.mate
  58.0 0.0 copy-start.13
  58.0 0.7 copy-done.13
  58.8 2.6 %shard_map.145 = (bf16[16,64,128]{2,1,0:T(8,128)(2,1)}, bf16[16,64,128]{2,1,0:T(8,128)(2,1)}, bf16[16,64,128]{2,1,0:T(8,128)(2,1)}) custom-call(s32[2]{0:T(128)} %pad_add_fusion.place_ref.refs_0_, s32[16,1,128]{2,1,0:T(1,128)} %copy-done.9, bf16[16,64,128]{2,1,0:T(8,128)(2,1)} %get-tuple-element.43.own, bf16[16,64,128]{2,1,0:T(8,128)(2,1)} %copy-done.13), custom_call_target="tpu_custom_call" | custom-call | flops 2000000000 | bytes 532488 | tf_op jit(solution)/shard_map/pallas_call | solution.py:280
  61.4 3.8 %collective-permute-start.6 = (bf16[16,64,128]{2,1,0:T(8,128)(2,1)}, bf16[16,64,128]{2,1,0:T(8,128)(2,1)S(1)}, u32[]{:S(2)}, u32[]{:S(2)}) collective-permute-start(bf16[16,64,128]{2,1,0:T(8,128)(2,1)} %get-tuple-element.44), channel_id=1, source_target_pairs={{0,2},{2,4},{4,6},{6,8},{8,10},{10,12},{12,14},{3,1},{5,3},{7,5},{... | collective-permute-start | bytes 786440 | tf_op jit(solution)/shard_map/ppermute | solution.py:337
  65.2 3.4 %collective-permute-start.7 = (bf16[16,64,128]{2,1,0:T(8,128)(2,1)}, bf16[16,64,128]{2,1,0:T(8,128)(2,1)S(1)}, u32[]{:S(2)}, u32[]{:S(2)}) collective-permute-start(bf16[16,64,128]{2,1,0:T(8,128)(2,1)} %get-tuple-element.45), channel_id=1, source_target_pairs={{0,4},{2,6},{4,8},{6,10},{8,12},{10,14},{5,1},{7,3},{9,5},{11,7},{... | collective-permute-start | bytes 786440 | tf_op jit(solution)/shard_map/ppermute | solution.py:337
  68.6 4.3 %collective-permute-start.8 = (bf16[16,64,128]{2,1,0:T(8,128)(2,1)}, bf16[16,64,128]{2,1,0:T(8,128)(2,1)S(1)}, u32[]{:S(2)}, u32[]{:S(2)}) collective-permute-start(bf16[16,64,128]{2,1,0:T(8,128)(2,1)} %get-tuple-element.46), channel_id=1, source_target_pairs={{0,6},{2,8},{4,10},{6,12},{8,14},{7,1},{9,3},{11,5},{13,7},{15,9},... | collective-permute-start | bytes 786440 | tf_op jit(solution)/shard_map/ppermute | solution.py:337
  72.9 8.5 %shard_map.146 = (f32[17,64,64]{2,1,0:T(8,128)}, f32[17,64,64]{2,1,0:T(8,128)}) custom-call(s32[2]{0:T(128)} %pad_add_fusion.place_ref.refs_0_, s32[8,16]{1,0:T(8,128)} %bitcast.22, s32[8,16]{1,0:T(8,128)} %bitcast.24, s32[1,2,72]{2,1,0:T(2,128)} %refs_1_.3, s32[1,2,24]{2,1,0:T(2,128)} %refs_2_.3, bf16[16,64,128]{2,1,0:T(8,128)(2,1)} %get-tuple-element.43.own, ...), custom_call_target="tpu_custom_call" | custom-call | flops 7000000000 | bytes 3409672 | tf_op jit(solution)/shard_map/pallas_call | solution.py:280
  81.4 0.0 all-to-all-done.2.refs_7_
  81.4 0.0 collective-permute-done.6.refs_4_
  81.5 0.0 collective-permute-done.7.refs_5_
  81.5 0.0 collective-permute-done.8.refs_6_
  81.5 0.0 copy-start.8
  81.6 0.1 pad_maximum_fusion.1
  81.6 0.1 collective-permute-start.9
  81.7 1.9 %collective-permute-done.9.refs_8_ = bf16[32,64,128]{2,1,0:T(8,128)(2,1)S(1)} collective-permute-done((bf16[32,64,128]{2,1,0:T(8,128)(2,1)S(1)}, bf16[32,64,128]{2,1,0:T(8,128)(2,1)S(1)}, u32[]{:S(2)}, u32[]{:S(2)}) %collective-permute-start.9) | collective-permute-done | bytes 524320 | tf_op jit(solution)/shard_map/ppermute | solution.py:349
  83.6 0.0 copy-done.6
  83.6 0.8 copy-done.11
  84.5 5.8 %shard_map.147 = bf16[64,1024]{1,0:T(8,128)(2,1)} custom-call(s32[2]{0:T(128)} %pad_add_fusion.place_ref.refs_0_, s32[1,2,72]{2,1,0:T(2,128)} %refs_1_.3, s32[1,2,24]{2,1,0:T(2,128)} %refs_2_.3, s32[1,2,32]{2,1,0:T(2,128)} %refs_3_.3, bf16[16,64,128]{2,1,0:T(8,128)(2,1)} %copy-done.4, bf16[16,64,128]{2,1,0:T(8,128)(2,1)} %copy-done.6, ...), custom_call_target="tpu_custom_call" | custom-call | flops 4000000000 | bytes 3310600 | tf_op jit(solution)/shard_map/pallas_call | solution.py:280
  (24 shorter events, 0.1 us)
Async XLA Ops:
  0.6 12.1 %copy-start = (bf16[1,72,64,64]{1,3,2,0:T(8,128)(2,1)S(1)}, bf16[1,72,64,64]{1,3,2,0:T(8,128)(2,1)}, u32[]{:S(2)}) copy-start(bf16[1,72,64,64]{1,3,2,0:T(8,128)(2,1)} %param.23) | copy-start | bytes 1769476
  3.2 18.6 %collective-permute-start = (bf16[16,64,128]{2,1,0:T(8,128)(2,1)}, bf16[16,64,128]{2,1,0:T(8,128)(2,1)S(1)}, u32[]{:S(2)}, u32[]{:S(2)}) collective-permute-start(bf16[16,64,128]{2,1,0:T(8,128)(2,1)} %get-tuple-element.29.own), channel_id=1, source_target_pairs={{0,1},{1,0},{2,3},{3,2},{4,5},{5,4},{6,7},{7,6},{8,9},{9,8},{10,11... | collective-permute-start | bytes 786440 | tf_op jit(solution)/shard_map/ppermute | solution.py:332
  5.0 13.4 %all-to-all-start = ((s32[16,1,128]{2,1,0:T(1,128)}), s32[16,1,128]{2,1,0:T(1,128)S(1)}, u32[]{:S(2)}, u32[]{:S(2)}) async-start(s32[16,1,128]{2,1,0:T(1,128)} %shard_map.140), calls=%async_computation | async-start | bytes 16384 | tf_op jit(solution)/shard_map/all_to_all | solution.py:328
  18.4 3.4 %copy-start.9 = (s32[16,1,128]{2,1,0:T(1,128)}, s32[16,1,128]{2,1,0:T(1,128)S(1)}, u32[]{:S(2)}) copy-start(s32[16,1,128]{2,1,0:T(1,128)S(1)} %all-to-all-done.asks) | copy-start | bytes 24580
  18.4 26.8 %all-to-all-start.1 = ((bf16[8,64,128]{2,1,0:T(8,128)(2,1)}), bf16[8,64,128]{2,1,0:T(8,128)(2,1)S(1)}, u32[]{:S(2)}, u32[]{:S(2)}) async-start(bf16[8,64,128]{2,1,0:T(8,128)(2,1)} %get-tuple-element.33), calls=%async_computation.1 | async-start | bytes 262144 | tf_op jit(solution)/shard_map/all_to_all | solution.py:331
  21.8 0.7 copy-start.12
  25.2 20.1 %collective-permute-start.1 = (bf16[16,64,128]{2,1,0:T(8,128)(2,1)}, bf16[16,64,128]{2,1,0:T(8,128)(2,1)S(1)}, u32[]{:S(2)}, u32[]{:S(2)}) collective-permute-start(bf16[16,64,128]{2,1,0:T(8,128)(2,1)} %get-tuple-element.30), channel_id=1, source_target_pairs={{0,2},{2,4},{4,6},{6,8},{8,10},{10,12},{12,14},{3,1},{5,3},{7,5},{... | collective-permute-start | bytes 786440 | tf_op jit(solution)/shard_map/ppermute | solution.py:337
  29.0 16.3 %collective-permute-start.2 = (bf16[16,64,128]{2,1,0:T(8,128)(2,1)}, bf16[16,64,128]{2,1,0:T(8,128)(2,1)S(1)}, u32[]{:S(2)}, u32[]{:S(2)}) collective-permute-start(bf16[16,64,128]{2,1,0:T(8,128)(2,1)} %get-tuple-element.31), channel_id=1, source_target_pairs={{0,4},{2,6},{4,8},{6,10},{8,12},{10,14},{5,1},{7,3},{9,5},{11,7},{... | collective-permute-start | bytes 786440 | tf_op jit(solution)/shard_map/ppermute | solution.py:337
  32.4 12.9 %collective-permute-start.3 = (bf16[16,64,128]{2,1,0:T(8,128)(2,1)}, bf16[16,64,128]{2,1,0:T(8,128)(2,1)S(1)}, u32[]{:S(2)}, u32[]{:S(2)}) collective-permute-start(bf16[16,64,128]{2,1,0:T(8,128)(2,1)} %get-tuple-element.32), channel_id=1, source_target_pairs={{0,6},{2,8},{4,10},{6,12},{8,14},{7,1},{9,3},{11,5},{13,7},{15,9},... | collective-permute-start | bytes 786440 | tf_op jit(solution)/shard_map/ppermute | solution.py:337
  45.2 2.2 %copy-start.1 = (bf16[8,64,128]{2,1,0:T(8,128)(2,1)}, bf16[8,64,128]{2,1,0:T(8,128)(2,1)S(1)}, u32[]{:S(2)}) copy-start(bf16[8,64,128]{2,1,0:T(8,128)(2,1)S(1)} %all-to-all-done.1.refs_7_) | copy-start | bytes 393220
  45.2 2.2 %copy-start.3 = (bf16[16,64,128]{2,1,0:T(8,128)(2,1)}, bf16[16,64,128]{2,1,0:T(8,128)(2,1)S(1)}, u32[]{:S(2)}) copy-start(bf16[16,64,128]{2,1,0:T(8,128)(2,1)S(1)} %collective-permute-done.1.refs_4_) | copy-start | bytes 786436
  45.2 2.1 %copy-start.5 = (bf16[16,64,128]{2,1,0:T(8,128)(2,1)}, bf16[16,64,128]{2,1,0:T(8,128)(2,1)S(1)}, u32[]{:S(2)}) copy-start(bf16[16,64,128]{2,1,0:T(8,128)(2,1)S(1)} %collective-permute-done.2.refs_5_) | copy-start | bytes 786436
  45.3 2.1 %copy-start.7 = (bf16[16,64,128]{2,1,0:T(8,128)(2,1)}, bf16[16,64,128]{2,1,0:T(8,128)(2,1)S(1)}, u32[]{:S(2)}) copy-start(bf16[16,64,128]{2,1,0:T(8,128)(2,1)S(1)} %collective-permute-done.3.refs_6_) | copy-start | bytes 786436
  45.4 2.0 %collective-permute-start.4 = (bf16[32,64,128]{2,1,0:T(8,128)(2,1)S(1)}, bf16[32,64,128]{2,1,0:T(8,128)(2,1)S(1)}, u32[]{:S(2)}, u32[]{:S(2)}) collective-permute-start(bf16[32,64,128]{2,1,0:T(8,128)(2,1)S(1)} %pad_maximum_fusion), channel_id=1, source_target_pairs={{0,1},{1,0},{2,3},{3,2},{4,5},{5,4},{6,7},{7,6},{8,9},{9,8},{10,11... | collective-permute-start | bytes 1572872 | tf_op jit(solution)/shard_map/ppermute | solution.py:349
  47.4 0.8 copy-start.10
  54.5 3.5 %collective-permute-start.5 = (bf16[16,64,128]{2,1,0:T(8,128)(2,1)}, bf16[16,64,128]{2,1,0:T(8,128)(2,1)S(1)}, u32[]{:S(2)}, u32[]{:S(2)}) collective-permute-start(bf16[16,64,128]{2,1,0:T(8,128)(2,1)} %get-tuple-element.43.own), channel_id=1, source_target_pairs={{0,1},{1,0},{2,3},{3,2},{4,5},{5,4},{6,7},{7,6},{8,9},{9,8},{10,11... | collective-permute-start | bytes 786440 | tf_op jit(solution)/shard_map/ppermute | solution.py:332
  54.7 26.8 %all-to-all-start.2 = ((bf16[8,64,128]{2,1,0:T(8,128)(2,1)}), bf16[8,64,128]{2,1,0:T(8,128)(2,1)S(1)}, u32[]{:S(2)}, u32[]{:S(2)}) async-start(bf16[8,64,128]{2,1,0:T(8,128)(2,1)} %get-tuple-element.47), calls=%async_computation.2 | async-start | bytes 262144 | tf_op jit(solution)/shard_map/all_to_all | solution.py:331
  58.0 0.7 copy-start.13
  61.4 20.1 %collective-permute-start.6 = (bf16[16,64,128]{2,1,0:T(8,128)(2,1)}, bf16[16,64,128]{2,1,0:T(8,128)(2,1)S(1)}, u32[]{:S(2)}, u32[]{:S(2)}) collective-permute-start(bf16[16,64,128]{2,1,0:T(8,128)(2,1)} %get-tuple-element.44), channel_id=1, source_target_pairs={{0,2},{2,4},{4,6},{6,8},{8,10},{10,12},{12,14},{3,1},{5,3},{7,5},{... | collective-permute-start | bytes 786440 | tf_op jit(solution)/shard_map/ppermute | solution.py:337
  65.2 16.3 %collective-permute-start.7 = (bf16[16,64,128]{2,1,0:T(8,128)(2,1)}, bf16[16,64,128]{2,1,0:T(8,128)(2,1)S(1)}, u32[]{:S(2)}, u32[]{:S(2)}) collective-permute-start(bf16[16,64,128]{2,1,0:T(8,128)(2,1)} %get-tuple-element.45), channel_id=1, source_target_pairs={{0,4},{2,6},{4,8},{6,10},{8,12},{10,14},{5,1},{7,3},{9,5},{11,7},{... | collective-permute-start | bytes 786440 | tf_op jit(solution)/shard_map/ppermute | solution.py:337
  68.6 12.9 %collective-permute-start.8 = (bf16[16,64,128]{2,1,0:T(8,128)(2,1)}, bf16[16,64,128]{2,1,0:T(8,128)(2,1)S(1)}, u32[]{:S(2)}, u32[]{:S(2)}) collective-permute-start(bf16[16,64,128]{2,1,0:T(8,128)(2,1)} %get-tuple-element.46), channel_id=1, source_target_pairs={{0,6},{2,8},{4,10},{6,12},{8,14},{7,1},{9,3},{11,5},{13,7},{15,9},... | collective-permute-start | bytes 786440 | tf_op jit(solution)/shard_map/ppermute | solution.py:337
  81.4 2.2 %copy-start.2 = (bf16[8,64,128]{2,1,0:T(8,128)(2,1)}, bf16[8,64,128]{2,1,0:T(8,128)(2,1)S(1)}, u32[]{:S(2)}) copy-start(bf16[8,64,128]{2,1,0:T(8,128)(2,1)S(1)} %all-to-all-done.2.refs_7_) | copy-start | bytes 393220
  81.5 2.2 %copy-start.4 = (bf16[16,64,128]{2,1,0:T(8,128)(2,1)}, bf16[16,64,128]{2,1,0:T(8,128)(2,1)S(1)}, u32[]{:S(2)}) copy-start(bf16[16,64,128]{2,1,0:T(8,128)(2,1)S(1)} %collective-permute-done.6.refs_4_) | copy-start | bytes 786436
  81.5 2.1 %copy-start.6 = (bf16[16,64,128]{2,1,0:T(8,128)(2,1)}, bf16[16,64,128]{2,1,0:T(8,128)(2,1)S(1)}, u32[]{:S(2)}) copy-start(bf16[16,64,128]{2,1,0:T(8,128)(2,1)S(1)} %collective-permute-done.7.refs_5_) | copy-start | bytes 786436
  81.5 2.1 %copy-start.8 = (bf16[16,64,128]{2,1,0:T(8,128)(2,1)}, bf16[16,64,128]{2,1,0:T(8,128)(2,1)S(1)}, u32[]{:S(2)}) copy-start(bf16[16,64,128]{2,1,0:T(8,128)(2,1)S(1)} %collective-permute-done.8.refs_6_) | copy-start | bytes 786436
  81.6 2.0 %collective-permute-start.9 = (bf16[32,64,128]{2,1,0:T(8,128)(2,1)S(1)}, bf16[32,64,128]{2,1,0:T(8,128)(2,1)S(1)}, u32[]{:S(2)}, u32[]{:S(2)}) collective-permute-start(bf16[32,64,128]{2,1,0:T(8,128)(2,1)S(1)} %pad_maximum_fusion.1), channel_id=1, source_target_pairs={{0,1},{1,0},{2,3},{3,2},{4,5},{5,4},{6,7},{7,6},{8,9},{9,8},{10,11... | collective-permute-start | bytes 1572872 | tf_op jit(solution)/shard_map/ppermute | solution.py:349
  83.6 0.8 copy-start.11

commit v3 on v2

v3 whole, which is shorter than its diff:
```python
import jax
import jax.numpy as jnp
from jax import lax
from jax.experimental import pallas as pl
from jax.experimental.pallas import tpu as pltpu
from jax.sharding import PartitionSpec as P


HOPS = 6
CAP0 = 6
CAPN = 2
FAN = 8
REACH = (HOPS + 1) // 2
OFFSETS = 2 * HOPS
FAR_TILES = CAP0 // 2
PAIR_TILES = (CAP0 + CAPN) // 2
F32 = jnp.float32
BF16 = jnp.bfloat16
VMEM = pl.BlockSpec(memory_space=pltpu.VMEM)
SMEM = pl.BlockSpec(memory_space=pltpu.SMEM)
ANY = pl.BlockSpec(memory_space=pl.ANY)
HBM = pl.BlockSpec(memory_space=pltpu.HBM)
MIB = 1024 * 1024
SPECS = {"s": SMEM, "v": VMEM, "a": ANY, "h": HBM}
PAIRS = [[(0, 0), (0, 1), (1, 0), (1, 1)]] * (REACH - 1) + [[(0, 0), (0, 1), (1, 1)]]
MINE = 2 * PAIR_TILES
MATES = [PAIR_TILES * (len(p) - 2) for p in PAIRS]


def nn(a, b):
    return jnp.dot(a, b, preferred_element_type=F32)


def nt(a, b):
    return lax.dot_general(a, b, (((1,), (1,)), ((), ())), preferred_element_type=F32)


def beside(a, b):
    return jnp.concatenate([a, b], axis=1)


def outward(devices, by):
    chips = devices // 2
    up = [(2 * c, 2 * (c + by)) for c in range(chips) if c + by < chips]
    return up + [(2 * c + 1, 2 * (c - by) + 1) for c in range(chips) if c - by >= 0]


def mates(devices):
    return [(i, i ^ 1) for i in range(devices)]


def offset_index(off):
    where = off + HOPS - jnp.where(off > 0, 1, 0)
    return jnp.clip(where, 0, OFFSETS - 1)


def lift_tiles(tiles, basis, transfer, own, up):
    count = len(tiles)
    sums = []
    for i, tile in enumerate(tiles):
        width = basis.shape[1]
        c0 = nn(tile[:, :width], basis[2 * i])
        c1 = nn(tile[:, width:], basis[2 * i + 1])
        coarse = beside(c0, c1).astype(BF16)
        own[i] = coarse
        own[count + i] = tile
        part = nn(coarse[:, :width], transfer[2 * i]) + nn(coarse[:, width:], transfer[2 * i + 1])
        if i % (FAN // 2) == 0:
            sums.append(part)
        else:
            sums[-1] = sums[-1] + part
    parents = beside(*sums).astype(BF16)
    for c in range(up.shape[0]):
        up[c, 0:64, :] = parents


def cut(values):
    return [values[:, 128 * i : 128 * (i + 1)] for i in range(values.shape[1] // 128)]


def lift_kernel(*refs):
    inputs, (own, up), loaded, sems = refs[:5], refs[5:7], refs[7:12], refs[12]
    copies = fetch(list(zip(inputs, loaded)), sems)
    for copy in copies:
        copy.wait()
    values, basis, transfer, far_plan, near_plan = loaded
    lift_tiles(cut(values), basis, transfer, own, up)
    far, near = far_plan[0, 0:1, :], near_plan[0, 0:1, :]
    blank = jnp.zeros((1, 128 - far.shape[1] - near.shape[1]), jnp.int32)
    row = jnp.concatenate([far, near, blank], axis=1).astype(F32)
    rows = jnp.broadcast_to(row, (up.shape[1] - 64, 128)).astype(BF16)
    for c in range(up.shape[0]):
        up[c, 64:, :] = rows


def turn_tables(sources, table):
    row = 0
    for ref in sources:
        for i in range(ref.shape[0]):
            tile = ref[i]
            table[0, row] = tile
            table[1, row] = beside(tile[:, 64:], tile[:, :64])
            row += 1


def at_left(table, base, leaf):
    return table[leaf % 2, base + leaf // 2]


def at_right(table, base, leaf):
    return table[1 - leaf % 2, base + leaf // 2]


def pair_of(table, base, first, second, left):
    return jnp.where(left, at_left(table, base, first), at_right(table, base, second))


def left_mask():
    return lax.broadcasted_iota(jnp.int32, (64, 128), 1) < 64


def pack_kernel(place_ref, asks, mate_asks, own, mate, *refs):
    outs, table = refs[:REACH], refs[REACH]
    core, chip = place_ref[0], place_ref[1]
    chips = asks.shape[0]
    turn_tables((own, mate), table)
    left = left_mask()
    half = own.shape[0]
    for step in range(REACH):
        toward = jnp.where(core == 0, -2 * (step + 1), 2 * (step + 1))
        asker = jnp.clip(chip - toward // 2, 0, chips - 1)
        for place, (other_target, other_source) in enumerate(PAIRS[step]):
            target = jnp.where(core == other_target, 0, 1)
            source = jnp.where(core == other_source, 0, 1)
            order = offset_index(toward + source - target)
            asked = mate_asks if other_target else asks
            for i in range(PAIR_TILES):
                if i < FAR_TILES:
                    at = order * CAP0 + 2 * i
                    base = other_source * half
                else:
                    at = OFFSETS * CAP0 + order * CAPN + 2 * (i - FAR_TILES)
                    base = other_source * half + half // 2
                first = jnp.maximum(asked[asker, at], 0)
                second = jnp.maximum(asked[asker, at + 1], 0)
                outs[step][place * PAIR_TILES + i] = pair_of(table, base, first, second, left)


def fetch(pairs, sems):
    copies = []
    for i, (source, target) in enumerate(pairs):
        copy = pltpu.make_async_copy(source, target, sems.at[i])
        copy.start()
        copies.append(copy)
    return copies


CHUNKS = 4


def local_body(
    place_ref, far_list, near_list, far_plan, near_plan, own_in, mate_in, far_in, near_in, out,
    table, own, mate, far_blocks, near_blocks, sems, far_remote, near_remote, further, lean=False
):
    core = place_ref[0]
    leaves = far_blocks.shape[0]
    step = leaves // CHUNKS
    pairs = [(own_in, own)]
    for c in range(CHUNKS):
        rows = pl.ds(c * step, step)
        pairs += [(far_in.at[rows], far_blocks.at[rows]), (near_in.at[rows], near_blocks.at[rows])]
    order = jnp.where(core == 0, HOPS, HOPS - 1)
    if lean:
        (far_from, far_to), (near_from, near_to) = further
        further = [
            (far_from.at[pl.ds(order * CAP0, CAP0)], far_to),
            (near_from.at[pl.ds(order * CAPN, CAPN)], near_to),
        ]
    copies = fetch(pairs + [(mate_in, mate)] + further, sems)
    copies[0].wait()
    turn_tables((own,), table)
    left = left_mask()
    half = own.shape[0]
    for leaf in range(leaves):
        if leaf % step == 0:
            c = leaf // step
            copies[1 + 2 * c].wait()
            copies[2 + 2 * c].wait()
        sums = []
        for listed, blocks, base in (
            (far_list, far_blocks, 0),
            (near_list, near_blocks, half // 2),
        ):
            xs, ws = [], []
            for k in range(0, blocks.shape[1], 2):
                xs.append(pair_of(table, base, listed[k, leaf], listed[k + 1, leaf], left))
                ws.append(beside(blocks[leaf, k], blocks[leaf, k + 1]))
            sums.append(nt(jnp.concatenate(xs, axis=1), jnp.concatenate(ws, axis=1)))
        out[leaf] = beside(*sums)
    for copy in copies[1 + 2 * CHUNKS :]:
        copy.wait()
    out[leaves] = jnp.zeros((64, 128), F32)
    for plan, blocks, base, cap in (
        (far_plan, far_remote, 0, CAP0),
        (near_plan, near_remote, half // 2, CAPN),
    ):
        for c in range(cap):
            slot = order * cap + c
            target = plan[0, 1, slot]
            where = jnp.where(target < 0, leaves, target)
            leaf = jnp.maximum(plan[0, 0, slot], 0)
            tile = mate[base + leaf // 2]
            x = jnp.where(leaf % 2 == 0, tile[:, :64], tile[:, 64:])
            w = blocks[c if lean else slot]
            z = jnp.zeros_like(w)
            w = jnp.concatenate([z, w] if base else [w, z], axis=0)
            out[where] = out[where] + nt(x, w)


def local_kernel(*refs):
    ins, statics, out, held, scratch = refs[:9], refs[9:14], refs[14], refs[15:20], refs[20:]
    local_body(*ins, out, *scratch, held[0], held[1], list(zip(statics, held)))


def lean_local_kernel(*refs):
    ins, remote, out, scratch, held = refs[:9], refs[9:11], refs[11], refs[12:18], refs[18:]
    local_body(*ins, out, *scratch, *held, list(zip(remote, held)), lean=True)


def combine(
    place_ref, far_plan, near_plan, parent_plan, arrived_in, parents_in, swapped_in, sums,
    far_remote, near_remote, parent_remote, basis, transfer,
    arrived, parents, swapped, far_acc, near_acc, sems, later=()
):
    core = place_ref[0]
    leaves = basis.shape[0]
    copies = fetch(
        [(swapped_in, swapped), (parents_in.at[:, pl.ds(0, 64)], parents)]
        + [(a.at[pl.ds(0, MINE)], arrived.at[i]) for i, a in enumerate(arrived_in)]
        + list(later),
        sems,
    )
    far_acc[...] = jnp.zeros(far_acc.shape, F32)
    near_acc[...] = jnp.zeros(near_acc.shape, F32)
    first = 2 + REACH + len(later) // 3
    for copy in copies[:first]:
        copy.wait()
    row = 0
    for step in range(REACH):
        for side in range(2):
            for other_target, other in PAIRS[step]:
                if other_target != side:
                    continue
                sender = jnp.where(core == side, 0, 1)
                source = jnp.where(sender == other, 0, 1)
                away = jnp.where(sender == 0, -2 * (step + 1), 2 * (step + 1))
                order = offset_index(away + source - core)
                for i in range(PAIR_TILES):
                    if side:
                        tile = swapped[row]
                        row += 1
                    else:
                        tile = arrived[step, other * PAIR_TILES + i]
                    if i < FAR_TILES:
                        plan, blocks, acc = far_plan, far_remote, far_acc
                        slot = order * CAP0 + 2 * i
                    else:
                        plan, blocks, acc = near_plan, near_remote, near_acc
                        slot = order * CAPN + 2 * (i - FAR_TILES)
                    b0, b1 = blocks[slot], blocks[slot + 1]
                    zero = jnp.zeros_like(b0)
                    y = nt(tile, jnp.concatenate([beside(b0, zero), beside(zero, b1)], axis=0))
                    t0, t1 = plan[0, 1, slot], plan[0, 1, slot + 1]
                    t0, t1 = jnp.where(t0 < 0, leaves, t0), jnp.where(t1 < 0, leaves, t1)
                    acc[t0, :, 0:64] = acc[t0, :, 0:64] + y[:, 0:64]
                    acc[t1, :, 64:128] = acc[t1, :, 64:128] + y[:, 64:128]

    chips = parents.shape[0]
    left = left_mask()
    mates_parents = row
    for copy in copies[first:]:
        copy.wait()

    def one_chip(chip, total):
        xs, ws = [], []
        for side in range(2):
            tile = swapped[mates_parents + chip] if side else parents[chip]
            member = jnp.where(core == side, 0, 1)
            turned = beside(tile[:, 64:], tile[:, :64])
            slot = (2 * chip + member) * 2
            s0, s1 = parent_plan[0, 0, slot], parent_plan[0, 0, slot + 1]
            t0, t1 = parent_plan[0, 1, slot], parent_plan[0, 1, slot + 1]
            x0 = jnp.where(s0 > 0, turned, tile)
            x1 = jnp.where(s1 == 0, turned, tile)
            zero = jnp.zeros_like(tile)
            rows = []
            for p in range(2):
                x = jnp.where(left, jnp.where(t0 == p, x0, zero), jnp.where(t1 == p, x1, zero))
                rows.append(x)
            xs.append(jnp.concatenate(rows, axis=0))
            ws.append(beside(parent_remote[slot], parent_remote[slot + 1]))
        return total + nt(beside(*xs), beside(*ws))

    total = jnp.zeros((128, 64), F32)
    if chips <= 8:
        for chip in range(chips):
            total = one_chip(chip, total)
    else:
        total = lax.fori_loop(0, chips, one_chip, total)
    parent_sum = total.astype(BF16)

    tiles = []
    for i in range(leaves // 2):
        halves = []
        for leaf in (2 * i, 2 * i + 1):
            p = leaf // FAN
            down = nt(parent_sum[64 * p : 64 * (p + 1)], transfer[leaf])
            here, far, near = sums[leaf], far_acc[leaf], near_acc[leaf]
            summed = (here[:, :64] + far[:, :64] + far[:, 64:] + down).astype(BF16)
            rest = here[:, 64:] + near[:, :64] + near[:, 64:]
            halves.append(nt(summed, basis[leaf]) + rest)
        tiles.append(beside(*halves).astype(BF16))
    return tiles


def split_refs(refs):
    return tuple(refs[:4]) + (refs[4 : 4 + REACH],) + tuple(refs[4 + REACH :])


def middle_kernel(*refs):
    inputs, (out, own, up), scratch = refs[:-9], refs[-9:-6], refs[-6:]
    basis, transfer = inputs[-2:]
    tiles = combine(*split_refs(inputs), *scratch)
    for i, tile in enumerate(tiles):
        out[:, 128 * i : 128 * (i + 1)] = tile
    lift_tiles(tiles, basis, transfer, own, up)


def last_kernel(*refs):
    sent = 4 + REACH + 2
    inputs, statics, rest = refs[:sent], refs[sent : sent + 6], refs[sent + 6 :]
    out, scratch, held = rest[0], rest[1:7], rest[7:]
    later = [(statics[i], held[i]) for i in (1, 2, 3, 0, 4, 5)]
    tiles = combine(*split_refs(inputs + held), *scratch, later)
    for i, tile in enumerate(tiles):
        out[:, 128 * i : 128 * (i + 1)] = tile


def call(kernel, kinds, outs, scratch, args, flops, limit=24):
    size = sum(a.size * a.dtype.itemsize for a in args)
    return pl.pallas_call(
        kernel,
        out_shape=outs,
        in_specs=[SPECS[k] for k in kinds],
        out_specs=jax.tree.map(lambda _: VMEM, outs),
        scratch_shapes=scratch,
        compiler_params=pltpu.CompilerParams(vmem_limit_bytes=limit * MIB),
        cost_estimate=pl.CostEstimate(flops=int(flops), bytes_accessed=size, transcendentals=0),
    )(*args)


def on_device(
    values,
    basis,
    transfer,
    near_list,
    near_blocks,
    far_list,
    far_blocks,
    near_plan,
    near_remote,
    far_plan,
    far_remote,
    parent_plan,
    parent_remote,
):
    devices = lax.axis_size("clu")
    chips = devices // 2
    leaves = basis.shape[0]
    at = lax.axis_index("clu").astype(jnp.int32)
    place = jnp.stack([at & 1, at >> 1])
    near_remote, far_remote, parent_remote = near_remote[0], far_remote[0], parent_remote[0]
    far_list, near_list = far_list.T, near_list.T
    same_core = [[2 * c + k for c in range(chips)] for k in range(2)]

    shape = jax.ShapeDtypeStruct
    dma = pltpu.SemaphoreType.DMA
    own_shape = shape((leaves, 64, 128), BF16)
    out_shape = shape((64, values.shape[0]), BF16)
    sums_shape = shape((leaves + 1, 64, 128), F32)
    statics = (far_remote, near_remote, parent_remote, basis, transfer)
    held_shapes = [pltpu.VMEM(x.shape, x.dtype) for x in statics]
    table_scratch = [pltpu.VMEM((2, 2 * leaves, 64, 128), BF16)]
    local_scratch = [
        pltpu.VMEM((2, leaves, 64, 128), BF16),
        pltpu.VMEM(own_shape.shape, BF16),
        pltpu.VMEM(own_shape.shape, BF16),
        pltpu.VMEM(far_blocks.shape, BF16),
        pltpu.VMEM(near_blocks.shape, BF16),
    ]
    combine_scratch = [
        pltpu.VMEM((REACH, MINE, 64, 128), BF16),
        pltpu.VMEM((chips, 64, 128), BF16),
        pltpu.VMEM((sum(MATES) + chips, 64, 128), BF16),
        pltpu.VMEM((leaves + 1, 64, 128), F32),
        pltpu.VMEM((leaves + 1, 64, 128), F32),
        dma((2 + REACH,)),
    ]
    messages = [shape((PAIR_TILES * len(p), 64, 128), BF16) for p in PAIRS]

    def crosswise(x):
        return lax.ppermute(x, "clu", mates(devices))

    def exchange(own, up, asks, last):
        parents = lax.all_to_all(up, "clu", 0, 0, tiled=True, axis_index_groups=same_core)
        mate = crosswise(own)
        if asks is None:
            asks = parents[:, 64, :].astype(jnp.int32)
            asks = (asks, crosswise(asks))
        packed = call(
            pack_kernel, "sssvv", messages, table_scratch, (place, *asks, own, mate), 2e9
        )
        arrived = [
            lax.ppermute(m, "clu", outward(devices, d + 1)) for d, m in enumerate(packed)
        ]
        local = (place, far_list, near_list, far_plan, near_plan, own, mate, far_blocks,
                 near_blocks)
        if last:
            held = statics
            sums = call(
                lean_local_kernel, "sssssaahhhh", sums_shape,
                local_scratch + [dma((4 + 2 * CHUNKS,))]
                + [pltpu.VMEM((n, 64, 64), BF16) for n in (CAP0, CAPN)],
                (*local, far_remote, near_remote), 6e9, 60,
            )
        else:
            sums, *held = call(
                local_kernel, "sssssaahh" + "h" * len(statics), [sums_shape, *held_shapes],
                local_scratch + [dma((2 + 2 * CHUNKS + len(statics),))], (*local, *statics), 7e9,
            )
        arrived, parents, sums = lax.optimization_barrier((arrived, parents, sums))
        swapped = jnp.concatenate([m[MINE:] for m in arrived] + [parents[:, :64]])
        swapped = crosswise(swapped)
        inputs = (place, far_plan, near_plan, parent_plan, *arrived, parents, swapped, sums, *held)
        return inputs, asks

    kinds = "ssss" + "a" * (REACH + 2) + "v" * 6
    lifted = (values.T, basis, transfer, far_plan, near_plan)
    own, up = call(
        lift_kernel, "hhhhh", [own_shape, shape((chips, 80, 128), BF16)],
        [pltpu.VMEM(x.shape, x.dtype) for x in lifted] + [dma((len(lifted),))], lifted, 1e9,
        60,
    )
    inputs, asks = exchange(own, up, None, False)
    first, own, up = call(
        middle_kernel, kinds, [out_shape, own_shape, shape((chips, 64, 128), BF16)],
        combine_scratch, inputs, 4e9,
    )
    inputs, _ = exchange(own, up, asks, True)
    loaded = inputs[4 + REACH + 2 :]
    second = call(
        last_kernel, "ssss" + "a" * (REACH + 8), out_shape,
        combine_scratch[:-1] + [dma((2 + REACH + len(loaded),))]
        + [pltpu.VMEM(x.shape, x.dtype) for x in loaded],
        inputs, 4e9, 60,
    )
    return first.T, second.T


def solution(mesh):
    return jax.shard_map(
        on_device,
        mesh=mesh,
        in_specs=(
            P(("groups", "clu"), None),
            P(("groups", "clu"), None, None),
            P(("groups", "clu"), None, None),
            P(("groups", "clu"), None),
            P(("groups", "clu"), None, None, None),
            P(("groups", "clu"), None),
            P(("groups", "clu"), None, None, None),
            P(("groups", "clu"), None, None),
            P(("groups", "clu"), None, None, None),
            P(("groups", "clu"), None, None),
            P(("groups", "clu"), None, None, None),
            P(("groups", "clu"), None, None),
            P(("groups", "clu"), None, None, None),
        ),
        out_specs=(P(("groups", "clu"), None), P(("groups", "clu"), None)),
        check_vma=False,
    )
```

time: 90.8 us -> 78.8 us (0.87)
  Pallas kernels: 38.3 us -> 28.2 us
  starting transfers between devices: 37.5 us -> 33.5 us
  waiting for transfers between devices: 6.93 us -> 10.9 us
  local copies, waits for them, and re-layouts: 5.65 us -> 4.16 us
    pallas_call x8 -> x7, Pallas kernels: 38.3 us -> 28.2 us  [call(): pl.pallas_call(kernel, out_shape=outs, in_specs=[SPECS[k] for k in kinds]...]
    all_to_all x2, waiting for transfers between devices: 0.01 us -> 7.55 us  [exchange(): lax.all_to_all(up, 'clu', 0, 0, tiled=True, axis_index_groups=same_core)]
    all_to_all x1 -> x0, starting transfers between devices: 7.05 us -> none  [on_device(): asks = lax.all_to_all(asks, 'clu', 0, 0, tiled=True)]
    all_to_all x2, starting transfers between devices: 6.74 us -> 11.6 us  [exchange(): lax.all_to_all(up, 'clu', 0, 0, tiled=True, axis_index_groups=same_core)]
    all_to_all x1 -> x0, waiting for transfers between devices: 3.11 us -> none  [on_device(): asks = lax.all_to_all(asks, 'clu', 0, 0, tiled=True)]
    ppermute x6, starting transfers between devices: 23 us -> 20.4 us  [exchange(): lax.ppermute(m, 'clu', outward(devices, d + 1))]
    unnamed x29 -> x45, local copies, waits for them, and re-layouts: 5.59 us -> 4.09 us
    ppermute x4 -> x5, waiting for transfers between devices: 3.8 us -> 3.25 us  [crosswise(): return lax.ppermute(x, 'clu', mates(devices))]
  transfers between devices with their start and end apart: 13 -> 13, of which waited for: 3 -> 3; matrix products, arithmetic and copies ran while one was open for 4% -> 2% of each run, Pallas kernels for 26% -> 15%
where the time goes in v3:
time: 78.8 us; the launch traced here: 78.3 us
  starting transfers between devices  33.5 us (43%)
  Pallas kernels  28.2 us (36%)
  waiting for transfers between devices  10.9 us (14%)
  local copies, waits for them, and re-layouts  4.16 us (5%)
  between operations  1.33 us (2%)
    pallas_call x7, Pallas kernels, call(): pl.pallas_call(kernel, out_shape=outs, in_specs=[SPECS[k] for k in kinds]...  28.2 us
    ppermute x6, starting transfers between devices, exchange(): lax.ppermute(m, 'clu', outward(devices, d + 1))  20.4 us
    all_to_all x2, starting transfers between devices, exchange(): lax.all_to_all(up, 'clu', 0, 0, tiled=True, axis_index_groups=same_core)  11.6 us
    all_to_all x2, waiting for transfers between devices, exchange(): lax.all_to_all(up, 'clu', 0, 0, tiled=True, axis_index_groups=same_core)  7.55 us
    unnamed x45, local copies, waits for them, and re-layouts  4.09 us
    ppermute x5, waiting for transfers between devices, crosswise(): return lax.ppermute(x, 'clu', mates(devices))  3.25 us
  transfers between devices with their start and end apart: 13, of which 3 were waited for; matrix products, arithmetic and copies ran while one was open for 2% of the time, Pallas kernels for 15%

profile of v3, /device:TPU:0, one launch (start us, length us, event | category | flops | bytes accessed | tf_op | source)
XLA Modules:
  0.0 78.3 jit_solution(12633851777757503531)
XLA Ops:
  0.6 2.6 %shard_map.140 = (bf16[16,64,128]{2,1,0:T(8,128)(2,1)}, bf16[8,80,128]{2,1,0:T(8,128)(2,1)}) custom-call(bf16[64,1024]{1,0:T(8,128)(2,1)} %bitcast.27, bf16[16,64,64]{2,1,0:T(8,128)(2,1)} %refs_13_.3, bf16[16,64,64]{2,1,0:T(8,128)(2,1)} %refs_14_.1, s32[1,2,72]{2,1,0:T(2,128)} %refs_1_.5, s32[1,2,24]{2,1,0:T(2,128)} %refs_2_.5), custom_call_target="tpu_custom_call" | custom-call | flops 1000000000 | bytes 393984 | tf_op jit(solution)/shard_map/pallas_call | solution.py:351
  3.3 7.3 %all-to-all-start = ((bf16[8,80,128]{2,1,0:T(8,128)(2,1)}), bf16[8,80,128]{2,1,0:T(8,128)(2,1)S(1)}, u32[]{:S(2)}, u32[]{:S(2)}) async-start(bf16[8,80,128]{2,1,0:T(8,128)(2,1)} %get-tuple-element.29), calls=%async_computation | async-start | bytes 327680 | tf_op jit(solution)/shard_map/all_to_all | solution.py:415
  10.6 0.0 collective-permute-start.1
  10.6 7.5 %all-to-all-done.refs_7_ = bf16[8,80,128]{2,1,0:T(8,128)(2,1)S(1)} async-done(((bf16[8,80,128]{2,1,0:T(8,128)(2,1)}), bf16[8,80,128]{2,1,0:T(8,128)(2,1)S(1)}, u32[]{:S(2)}, u32[]{:S(2)}) %all-to-all-start) | async-done | bytes 163872 | tf_op jit(solution)/shard_map/all_to_all | solution.py:415
  18.2 0.1 collective-permute-start
  18.2 0.1 pad_add_fusion.place_ref.refs_0_
  18.3 0.0 copy-start.12
  18.3 0.0 copy-start.13
  18.3 1.8 %copy.26 = bf16[1,72,64,64]{3,2,1,0:T(8,128)(2,1)S(1)} copy(bf16[1,72,64,64]{1,3,2,0:T(8,128)(2,1)S(1)} %copy-done.16) | data formatting | bytes 1179648 | tf_op args[10]
  20.2 0.0 copy-start.1
  20.2 0.0 copy-start.2
  20.2 0.0 copy-start.3
  20.2 0.0 copy-start.4
  20.2 0.0 copy-start.5
  20.2 0.0 copy-start.6
  20.2 0.0 collective-permute-done.1.mate.refs_6_
  20.2 0.0 collective-permute-done.mate_asks
  20.3 1.4 %copy-done.7 = bf16[16,64,128]{2,1,0:T(8,128)(2,1)S(1)} copy-done((bf16[16,64,128]{2,1,0:T(8,128)(2,1)S(1)}, bf16[16,64,128]{2,1,0:T(8,128)(2,1)}, u32[]{:S(2)}) %copy-start.7) | copy-done | bytes 262168
  21.7 2.4 %shard_map.141 = (bf16[16,64,128]{2,1,0:T(8,128)(2,1)S(1)}, bf16[16,64,128]{2,1,0:T(8,128)(2,1)S(1)}, bf16[12,64,128]{2,1,0:T(8,128)(2,1)S(1)}) custom-call(s32[2]{0:T(128)S(1)} %pad_add_fusion.place_ref.refs_0_, s32[8,128]{1,0:T(8,128)S(1)} %fusion.asks, s32[8,128]{1,0:T(8,128)S(1)} %collective-permute-done.mate_asks, bf16[16,64,128]{2,1,0:T(8,128)(2,1)S(1)} %copy-done.7, ...), custom_call_target="tpu_custom_call" | custom-call | flops 2000000000 | bytes 532488 | tf_op jit(solution)/shard_map/pallas_call | solution.py:351
  24.1 2.7 %collective-permute-start.4 = (bf16[12,64,128]{2,1,0:T(8,128)(2,1)S(1)}, bf16[12,64,128]{2,1,0:T(8,128)(2,1)S(1)}, u32[]{:S(2)}, u32[]{:S(2)}) collective-permute-start(bf16[12,64,128]{2,1,0:T(8,128)(2,1)S(1)} %get-tuple-element.33), channel_id=1, source_target_pairs={{0,6},{2,8},{4,10},{6,12},{8,14},{7,1},{9,3},{11,5},{13,7},{15,9},... | collective-permute-start | bytes 589832 | tf_op jit(solution)/shard_map/ppermute | solution.py:424
  26.8 3.2 %collective-permute-start.2 = (bf16[16,64,128]{2,1,0:T(8,128)(2,1)S(1)}, bf16[16,64,128]{2,1,0:T(8,128)(2,1)S(1)}, u32[]{:S(2)}, u32[]{:S(2)}) collective-permute-start(bf16[16,64,128]{2,1,0:T(8,128)(2,1)S(1)} %get-tuple-element.31), channel_id=1, source_target_pairs={{0,2},{2,4},{4,6},{6,8},{8,10},{10,12},{12,14},{3,1},{5,3},{7,5},{... | collective-permute-start | bytes 786440 | tf_op jit(solution)/shard_map/ppermute | solution.py:424
  30.0 2.7 %collective-permute-start.3 = (bf16[16,64,128]{2,1,0:T(8,128)(2,1)S(1)}, bf16[16,64,128]{2,1,0:T(8,128)(2,1)S(1)}, u32[]{:S(2)}, u32[]{:S(2)}) collective-permute-start(bf16[16,64,128]{2,1,0:T(8,128)(2,1)S(1)} %get-tuple-element.32), channel_id=1, source_target_pairs={{0,4},{2,6},{4,8},{6,10},{8,12},{10,14},{5,1},{7,3},{9,5},{11,7},{... | collective-permute-start | bytes 786440 | tf_op jit(solution)/shard_map/ppermute | solution.py:424
  32.8 0.0 copy-start.14
  32.8 4.5 %shard_map.142 = (f32[17,64,128]{2,1,0:T(8,128)S(1)}, bf16[72,64,64]{2,1,0:T(8,128)(2,1)S(1)}, bf16[24,64,64]{2,1,0:T(8,128)(2,1)S(1)}, bf16[32,64,64]{2,1,0:T(8...) custom-call(s32[2]{0:T(128)S(1)} %pad_add_fusion.place_ref.refs_0_, ...), custom_call_target="tpu_custom_call" | custom-call | flops 7000000000 | bytes 3933960 | tf_op jit(solution)/shard_map/pallas_call | solution.py:351
  37.3 0.0 collective-permute-done.4.refs_6_
  37.4 0.0 collective-permute-done.2.refs_4_
  37.4 0.0 collective-permute-done.3.refs_5_
  37.5 0.1 pad_maximum_fusion
  37.5 0.9 %collective-permute-start.5 = (bf16[28,64,128]{2,1,0:T(8,128)(2,1)S(1)}, bf16[28,64,128]{2,1,0:T(8,128)(2,1)S(1)}, u32[]{:S(2)}, u32[]{:S(2)}) collective-permute-start(bf16[28,64,128]{2,1,0:T(8,128)(2,1)S(1)} %pad_maximum_fusion), channel_id=1, source_target_pairs={{0,1},{1,0},{2,3},{3,2},{4,5},{5,4},{6,7},{7,6},{8,9},{9,8},{10,11... | collective-permute-start | bytes 1376264 | tf_op jit(solution)/shard_map/ppermute | solution.py:412
  38.5 1.4 %collective-permute-done.5.refs_8_ = bf16[28,64,128]{2,1,0:T(8,128)(2,1)S(1)} collective-permute-done((bf16[28,64,128]{2,1,0:T(8,128)(2,1)S(1)}, bf16[28,64,128]{2,1,0:T(8,128)(2,1)S(1)}, u32[]{:S(2)}, u32[]{:S(2)}) %collective-permute-start.5) | collective-permute-done | bytes 458784 | tf_op jit(solution)/shard_map/ppermute | solution.py:412
  39.9 5.3 %shard_map.143 = (bf16[64,1024]{1,0:T(8,128)(2,1)}, bf16[16,64,128]{2,1,0:T(8,128)(2,1)S(1)}, bf16[8,64,128]{2,1,0:T(8,128)(2,1)}) custom-call(s32[2]{0:T(128)S(1)} %pad_add_fusion.place_ref.refs_0_, s32[1,2,72]{2,1,0:T(2,128)S(1)} %copy-done.12, s32[1,2,24]{2,1,0:T(2,128)S(1)} %copy-done.13, s32[1,2,32]{2,1,0:T(2,128)S(1)} %copy-done.14, ...), custom_call_target="tpu_custom_call" | custom-call | flops 4000000000 | bytes 3212296 | tf_op jit(solution)/shard_map/pallas_call | solution.py:351
  45.3 0.4 collective-permute-start.6
  45.7 4.3 %all-to-all-start.1 = ((bf16[8,64,128]{2,1,0:T(8,128)(2,1)}), bf16[8,64,128]{2,1,0:T(8,128)(2,1)S(1)}, u32[]{:S(2)}, u32[]{:S(2)}) async-start(bf16[8,64,128]{2,1,0:T(8,128)(2,1)} %get-tuple-element.50), calls=%async_computation.1 | async-start | bytes 262144 | tf_op jit(solution)/shard_map/all_to_all | solution.py:415
  50.0 0.0 collective-permute-done.6.mate.refs_6_
  50.0 1.5 %shard_map.144 = (bf16[16,64,128]{2,1,0:T(8,128)(2,1)S(1)}, bf16[16,64,128]{2,1,0:T(8,128)(2,1)S(1)}, bf16[12,64,128]{2,1,0:T(8,128)(2,1)S(1)}) custom-call(s32[2]{0:T(128)S(1)} %pad_add_fusion.place_ref.refs_0_, s32[8,128]{1,0:T(8,128)S(1)} %fusion.asks, s32[8,128]{1,0:T(8,128)S(1)} %collective-permute-done.mate_asks, ...), custom_call_target="tpu_custom_call" | custom-call | flops 2000000000 | bytes 532488 | tf_op jit(solution)/shard_map/pallas_call | solution.py:351
  51.5 4.8 %collective-permute-start.9 = (bf16[12,64,128]{2,1,0:T(8,128)(2,1)S(1)}, bf16[12,64,128]{2,1,0:T(8,128)(2,1)S(1)}, u32[]{:S(2)}, u32[]{:S(2)}) collective-permute-start(bf16[12,64,128]{2,1,0:T(8,128)(2,1)S(1)} %get-tuple-element.49), channel_id=1, source_target_pairs={{0,6},{2,8},{4,10},{6,12},{8,14},{7,1},{9,3},{11,5},{13,7},{15,9},... | collective-permute-start | bytes 589832 | tf_op jit(solution)/shard_map/ppermute | solution.py:424
  56.4 3.4 %collective-permute-start.7 = (bf16[16,64,128]{2,1,0:T(8,128)(2,1)S(1)}, bf16[16,64,128]{2,1,0:T(8,128)(2,1)S(1)}, u32[]{:S(2)}, u32[]{:S(2)}) collective-permute-start(bf16[16,64,128]{2,1,0:T(8,128)(2,1)S(1)} %get-tuple-element.47), channel_id=1, source_target_pairs={{0,2},{2,4},{4,6},{6,8},{8,10},{10,12},{12,14},{3,1},{5,3},{7,5},{... | collective-permute-start | bytes 786440 | tf_op jit(solution)/shard_map/ppermute | solution.py:424
  59.8 3.5 %collective-permute-start.8 = (bf16[16,64,128]{2,1,0:T(8,128)(2,1)S(1)}, bf16[16,64,128]{2,1,0:T(8,128)(2,1)S(1)}, u32[]{:S(2)}, u32[]{:S(2)}) collective-permute-start(bf16[16,64,128]{2,1,0:T(8,128)(2,1)S(1)} %get-tuple-element.48), channel_id=1, source_target_pairs={{0,4},{2,6},{4,8},{6,10},{8,12},{10,14},{5,1},{7,3},{9,5},{11,7},{... | collective-permute-start | bytes 786440 | tf_op jit(solution)/shard_map/ppermute | solution.py:424
  63.3 5.7 %shard_map.145.refs_9_ = f32[17,64,128]{2,1,0:T(8,128)} custom-call(s32[2]{0:T(128)} %copy-done.15, s32[8,16]{1,0:T(8,128)} %bitcast.23, s32[8,16]{1,0:T(8,128)} %bitcast.25, s32[1,2,72]{2,1,0:T(2,128)} %refs_1_.5, s32[1,2,24]{2,1,0:T(2,128)} %refs_2_.5, bf16[16,64,128]{2,1,0:T(8,128)(2,1)} %copy-done.8, bf16[16,64,128]{2,1,0:T(8,128)(2,1)} %copy-done.9, ...), custom_call_target="tpu_custom_call" | custom-call | flops 6000000000 | bytes 3409672 | tf_op jit(solution)/shard_map/pallas_call | solution.py:351
  69.1 0.0 all-to-all-done.1.refs_7_
  69.1 0.0 collective-permute-done.9.refs_6_
  69.1 0.0 collective-permute-done.7.refs_4_
  69.1 0.0 collective-permute-done.8.refs_5_
  69.2 0.1 pad_maximum_fusion.1
  69.3 0.1 collective-permute-start.10
  69.3 1.8 %collective-permute-done.10.refs_8_ = bf16[28,64,128]{2,1,0:T(8,128)(2,1)S(1)} collective-permute-done((bf16[28,64,128]{2,1,0:T(8,128)(2,1)S(1)}, bf16[28,64,128]{2,1,0:T(8,128)(2,1)S(1)}, u32[]{:S(2)}, u32[]{:S(2)}) %collective-permute-start.10) | collective-permute-done | bytes 458784 | tf_op jit(solution)/shard_map/ppermute | solution.py:412
  71.2 0.8 copy-done.21
  71.9 6.1 %shard_map.146 = bf16[64,1024]{1,0:T(8,128)(2,1)} custom-call(s32[2]{0:T(128)} %copy-done.15, s32[1,2,72]{2,1,0:T(2,128)} %refs_1_.5, s32[1,2,24]{2,1,0:T(2,128)} %refs_2_.5, s32[1,2,32]{2,1,0:T(2,128)} %refs_3_.9, bf16[16,64,128]{2,1,0:T(8,128)(2,1)} %copy-done.18, bf16[16,64,128]{2,1,0:T(8,128)(2,1)} %copy-done.19, bf16[12,64,128]{2,1,0:T(8,128)(2,1)} %copy-done.20, ...), custom_call_target="tpu_custom_call" | custom-call | flops 4000000000 | bytes 3179528 | tf_op jit(solution)/shard_map/pallas_call | solution.py:351
  (42 shorter events, 0.1 us)
Async XLA Ops:
  0.6 17.7 %copy-start.16 = (bf16[1,72,64,64]{1,3,2,0:T(8,128)(2,1)S(1)}, bf16[1,72,64,64]{1,3,2,0:T(8,128)(2,1)}, u32[]{:S(2)}) copy-start(bf16[1,72,64,64]{1,3,2,0:T(8,128)(2,1)} %param.23) | copy-start | bytes 1769476
  3.3 14.9 %all-to-all-start = ((bf16[8,80,128]{2,1,0:T(8,128)(2,1)}), bf16[8,80,128]{2,1,0:T(8,128)(2,1)S(1)}, u32[]{:S(2)}, u32[]{:S(2)}) async-start(bf16[8,80,128]{2,1,0:T(8,128)(2,1)} %get-tuple-element.29), calls=%async_computation | async-start | bytes 327680 | tf_op jit(solution)/shard_map/all_to_all | solution.py:415
  10.6 9.7 %collective-permute-start.1 = (bf16[16,64,128]{2,1,0:T(8,128)(2,1)}, bf16[16,64,128]{2,1,0:T(8,128)(2,1)}, u32[]{:S(2)}, u32[]{:S(2)}) collective-permute-start(bf16[16,64,128]{2,1,0:T(8,128)(2,1)} %get-tuple-element.30.own.refs_5_), channel_id=1, source_target_pairs={{0,1},{1,0},{2,3},{3,2},{4,5},{5,4},{6,7},{7,6},{8,9},{9,8},{10,11... | collective-permute-start | bytes 786440 | tf_op jit(solution)/shard_map/ppermute | solution.py:412
  18.2 2.1 %collective-permute-start = (s32[8,128]{1,0:T(8,128)S(1)}, s32[8,128]{1,0:T(8,128)S(1)}, u32[]{:S(2)}, u32[]{:S(2)}) collective-permute-start(s32[8,128]{1,0:T(8,128)S(1)} %fusion.asks), channel_id=1, source_target_pairs={{0,1},{1,0},{2,3},{3,2},{4,5},{5,4},{6,7},{7,6},{8,9},{9,8},{10,11... | collective-permute-start | bytes 12296 | tf_op jit(solution)/shard_map/ppermute | solution.py:412
  18.3 31.7 %copy-start.15 = (s32[2]{0:T(128)}, s32[2]{0:T(128)S(1)}, u32[]{:S(2)}) copy-start(s32[2]{0:T(128)S(1)} %pad_add_fusion.place_ref.refs_0_) | copy-start | bytes 28
  18.3 14.4 %copy-start.10 = (s32[16,8]{0,1:T(8,128)S(1)}, s32[16,8]{0,1:T(8,128)}, u32[]{:S(2)}) copy-start(s32[16,8]{0,1:T(8,128)} %param.18) | copy-start | bytes 1540
  18.3 14.4 %copy-start.11 = (s32[16,8]{0,1:T(8,128)S(1)}, s32[16,8]{0,1:T(8,128)}, u32[]{:S(2)}) copy-start(s32[16,8]{0,1:T(8,128)} %param.16) | copy-start | bytes 1540
  18.3 14.4 %copy-start.12 = (s32[1,2,72]{2,1,0:T(2,128)S(1)}, s32[1,2,72]{2,1,0:T(2,128)}, u32[]{:S(2)}) copy-start(s32[1,2,72]{2,1,0:T(2,128)} %refs_1_.5) | copy-start | bytes 1732
  18.3 14.4 %copy-start.13 = (s32[1,2,24]{2,1,0:T(2,128)S(1)}, s32[1,2,24]{2,1,0:T(2,128)}, u32[]{:S(2)}) copy-start(s32[1,2,24]{2,1,0:T(2,128)} %refs_2_.5) | copy-start | bytes 580
  20.2 12.6 %copy-start = (bf16[1,72,64,64]{3,2,1,0:T(8,128)(2,1)}, bf16[1,72,64,64]{3,2,1,0:T(8,128)(2,1)S(1)}, u32[]{:S(2)}) copy-start(bf16[1,72,64,64]{3,2,1,0:T(8,128)(2,1)S(1)} %copy.26) | copy-start | bytes 1769476
  20.2 12.6 %copy-start.1 = (bf16[16,8,64,64]{3,2,1,0:T(8,128)(2,1)S(1)}, bf16[16,8,64,64]{3,2,1,0:T(8,128)(2,1)}, u32[]{:S(2)}) copy-start(bf16[16,8,64,64]{3,2,1,0:T(8,128)(2,1)} %refs_7_.3) | copy-start | bytes 3145732
  20.2 12.6 %copy-start.2 = (bf16[16,8,64,64]{3,2,1,0:T(8,128)(2,1)S(1)}, bf16[16,8,64,64]{3,2,1,0:T(8,128)(2,1)}, u32[]{:S(2)}) copy-start(bf16[16,8,64,64]{3,2,1,0:T(8,128)(2,1)} %refs_8_.3) | copy-start | bytes 3145732
  20.2 12.6 %copy-start.3 = (bf16[1,32,64,64]{3,2,1,0:T(8,128)(2,1)S(1)}, bf16[1,32,64,64]{3,2,1,0:T(8,128)(2,1)}, u32[]{:S(2)}) copy-start(bf16[1,32,64,64]{3,2,1,0:T(8,128)(2,1)} %param.25) | copy-start | bytes 786436
  20.2 12.6 %copy-start.4 = (bf16[1,24,64,64]{3,2,1,0:T(8,128)(2,1)S(1)}, bf16[1,24,64,64]{3,2,1,0:T(8,128)(2,1)}, u32[]{:S(2)}) copy-start(bf16[1,24,64,64]{3,2,1,0:T(8,128)(2,1)} %param.21) | copy-start | bytes 589828
  20.2 12.6 %copy-start.5 = (bf16[16,64,64]{2,1,0:T(8,128)(2,1)S(1)}, bf16[16,64,64]{2,1,0:T(8,128)(2,1)}, u32[]{:S(2)}) copy-start(bf16[16,64,64]{2,1,0:T(8,128)(2,1)} %refs_13_.3) | copy-start | bytes 393220
  20.2 12.6 %copy-start.6 = (bf16[16,64,64]{2,1,0:T(8,128)(2,1)S(1)}, bf16[16,64,64]{2,1,0:T(8,128)(2,1)}, u32[]{:S(2)}) copy-start(bf16[16,64,64]{2,1,0:T(8,128)(2,1)} %refs_14_.1) | copy-start | bytes 393220
  20.3 1.4 %copy-start.7 = (bf16[16,64,128]{2,1,0:T(8,128)(2,1)S(1)}, bf16[16,64,128]{2,1,0:T(8,128)(2,1)}, u32[]{:S(2)}) copy-start(bf16[16,64,128]{2,1,0:T(8,128)(2,1)} %get-tuple-element.30.own.refs_5_) | copy-start | bytes 786436
  24.1 13.2 %collective-permute-start.4 = (bf16[12,64,128]{2,1,0:T(8,128)(2,1)S(1)}, bf16[12,64,128]{2,1,0:T(8,128)(2,1)S(1)}, u32[]{:S(2)}, u32[]{:S(2)}) collective-permute-start(bf16[12,64,128]{2,1,0:T(8,128)(2,1)S(1)} %get-tuple-element.33), channel_id=1, source_target_pairs={{0,6},{2,8},{4,10},{6,12},{8,14},{7,1},{9,3},{11,5},{13,7},{15,9},... | collective-permute-start | bytes 589832 | tf_op jit(solution)/shard_map/ppermute | solution.py:424
  26.8 10.6 %collective-permute-start.2 = (bf16[16,64,128]{2,1,0:T(8,128)(2,1)S(1)}, bf16[16,64,128]{2,1,0:T(8,128)(2,1)S(1)}, u32[]{:S(2)}, u32[]{:S(2)}) collective-permute-start(bf16[16,64,128]{2,1,0:T(8,128)(2,1)S(1)} %get-tuple-element.31), channel_id=1, source_target_pairs={{0,2},{2,4},{4,6},{6,8},{8,10},{10,12},{12,14},{3,1},{5,3},{7,5},{... | collective-permute-start | bytes 786440 | tf_op jit(solution)/shard_map/ppermute | solution.py:424
  30.0 7.4 %collective-permute-start.3 = (bf16[16,64,128]{2,1,0:T(8,128)(2,1)S(1)}, bf16[16,64,128]{2,1,0:T(8,128)(2,1)S(1)}, u32[]{:S(2)}, u32[]{:S(2)}) collective-permute-start(bf16[16,64,128]{2,1,0:T(8,128)(2,1)S(1)} %get-tuple-element.32), channel_id=1, source_target_pairs={{0,4},{2,6},{4,8},{6,10},{8,12},{10,14},{5,1},{7,3},{9,5},{11,7},{... | collective-permute-start | bytes 786440 | tf_op jit(solution)/shard_map/ppermute | solution.py:424
  32.8 7.1 %copy-start.14 = (s32[1,2,32]{2,1,0:T(2,128)S(1)}, s32[1,2,32]{2,1,0:T(2,128)}, u32[]{:S(2)}) copy-start(s32[1,2,32]{2,1,0:T(2,128)} %refs_3_.9) | copy-start | bytes 772
  37.5 2.4 %collective-permute-start.5 = (bf16[28,64,128]{2,1,0:T(8,128)(2,1)S(1)}, bf16[28,64,128]{2,1,0:T(8,128)(2,1)S(1)}, u32[]{:S(2)}, u32[]{:S(2)}) collective-permute-start(bf16[28,64,128]{2,1,0:T(8,128)(2,1)S(1)} %pad_maximum_fusion), channel_id=1, source_target_pairs={{0,1},{1,0},{2,3},{3,2},{4,5},{5,4},{6,7},{7,6},{8,9},{9,8},{10,11... | collective-permute-start | bytes 1376264 | tf_op jit(solution)/shard_map/ppermute | solution.py:412
  45.3 6.2 %copy-start.8 = (bf16[16,64,128]{2,1,0:T(8,128)(2,1)}, bf16[16,64,128]{2,1,0:T(8,128)(2,1)S(1)}, u32[]{:S(2)}) copy-start(bf16[16,64,128]{2,1,0:T(8,128)(2,1)S(1)} %get-tuple-element.46.own.refs_5_) | copy-start | bytes 786436
  45.3 4.7 %collective-permute-start.6 = (bf16[16,64,128]{2,1,0:T(8,128)(2,1)S(1)}, bf16[16,64,128]{2,1,0:T(8,128)(2,1)S(1)}, u32[]{:S(2)}, u32[]{:S(2)}) collective-permute-start(bf16[16,64,128]{2,1,0:T(8,128)(2,1)S(1)} %get-tuple-element.46.own.refs_5_), channel_id=1, source_target_pairs={{0,1},{1,0},{2,3},{3,2},{4,5},{5,4},{6,7},{7,6},{8,9},{9,8},{10,11... | collective-permute-start | bytes 786440 | tf_op jit(solution)/shard_map/ppermute | solution.py:412
  45.7 23.4 %all-to-all-start.1 = ((bf16[8,64,128]{2,1,0:T(8,128)(2,1)}), bf16[8,64,128]{2,1,0:T(8,128)(2,1)S(1)}, u32[]{:S(2)}, u32[]{:S(2)}) async-start(bf16[8,64,128]{2,1,0:T(8,128)(2,1)} %get-tuple-element.50), calls=%async_computation.1 | async-start | bytes 262144 | tf_op jit(solution)/shard_map/all_to_all | solution.py:415
  50.0 1.5 %copy-start.9 = (bf16[16,64,128]{2,1,0:T(8,128)(2,1)}, bf16[16,64,128]{2,1,0:T(8,128)(2,1)S(1)}, u32[]{:S(2)}) copy-start(bf16[16,64,128]{2,1,0:T(8,128)(2,1)S(1)} %collective-permute-done.6.mate.refs_6_) | copy-start | bytes 786436
  51.5 17.6 %collective-permute-start.9 = (bf16[12,64,128]{2,1,0:T(8,128)(2,1)S(1)}, bf16[12,64,128]{2,1,0:T(8,128)(2,1)S(1)}, u32[]{:S(2)}, u32[]{:S(2)}) collective-permute-start(bf16[12,64,128]{2,1,0:T(8,128)(2,1)S(1)} %get-tuple-element.49), channel_id=1, source_target_pairs={{0,6},{2,8},{4,10},{6,12},{8,14},{7,1},{9,3},{11,5},{13,7},{15,9},... | collective-permute-start | bytes 589832 | tf_op jit(solution)/shard_map/ppermute | solution.py:424
  56.4 12.7 %collective-permute-start.7 = (bf16[16,64,128]{2,1,0:T(8,128)(2,1)S(1)}, bf16[16,64,128]{2,1,0:T(8,128)(2,1)S(1)}, u32[]{:S(2)}, u32[]{:S(2)}) collective-permute-start(bf16[16,64,128]{2,1,0:T(8,128)(2,1)S(1)} %get-tuple-element.47), channel_id=1, source_target_pairs={{0,2},{2,4},{4,6},{6,8},{8,10},{10,12},{12,14},{3,1},{5,3},{7,5},{... | collective-permute-start | bytes 786440 | tf_op jit(solution)/shard_map/ppermute | solution.py:424
  59.8 9.4 %collective-permute-start.8 = (bf16[16,64,128]{2,1,0:T(8,128)(2,1)S(1)}, bf16[16,64,128]{2,1,0:T(8,128)(2,1)S(1)}, u32[]{:S(2)}, u32[]{:S(2)}) collective-permute-start(bf16[16,64,128]{2,1,0:T(8,128)(2,1)S(1)} %get-tuple-element.48), channel_id=1, source_target_pairs={{0,4},{2,6},{4,8},{6,10},{8,12},{10,14},{5,1},{7,3},{9,5},{11,7},{... | collective-permute-start | bytes 786440 | tf_op jit(solution)/shard_map/ppermute | solution.py:424
  69.1 2.1 %copy-start.17 = (bf16[8,64,128]{2,1,0:T(8,128)(2,1)}, bf16[8,64,128]{2,1,0:T(8,128)(2,1)S(1)}, u32[]{:S(2)}) copy-start(bf16[8,64,128]{2,1,0:T(8,128)(2,1)S(1)} %all-to-all-done.1.refs_7_) | copy-start | bytes 393220
  69.1 2.1 %copy-start.20 = (bf16[12,64,128]{2,1,0:T(8,128)(2,1)}, bf16[12,64,128]{2,1,0:T(8,128)(2,1)S(1)}, u32[]{:S(2)}) copy-start(bf16[12,64,128]{2,1,0:T(8,128)(2,1)S(1)} %collective-permute-done.9.refs_6_) | copy-start | bytes 589828
  69.1 2.0 %copy-start.18 = (bf16[16,64,128]{2,1,0:T(8,128)(2,1)}, bf16[16,64,128]{2,1,0:T(8,128)(2,1)S(1)}, u32[]{:S(2)}) copy-start(bf16[16,64,128]{2,1,0:T(8,128)(2,1)S(1)} %collective-permute-done.7.refs_4_) | copy-start | bytes 786436
  69.1 2.0 %copy-start.19 = (bf16[16,64,128]{2,1,0:T(8,128)(2,1)}, bf16[16,64,128]{2,1,0:T(8,128)(2,1)S(1)}, u32[]{:S(2)}) copy-start(bf16[16,64,128]{2,1,0:T(8,128)(2,1)S(1)} %collective-permute-done.8.refs_5_) | copy-start | bytes 786436
  69.3 1.9 %collective-permute-start.10 = (bf16[28,64,128]{2,1,0:T(8,128)(2,1)S(1)}, bf16[28,64,128]{2,1,0:T(8,128)(2,1)S(1)}, u32[]{:S(2)}, u32[]{:S(2)}) collective-permute-start(bf16[28,64,128]{2,1,0:T(8,128)(2,1)S(1)} %pad_maximum_fusion.1), channel_id=1, source_target_pairs={{0,1},{1,0},{2,3},{3,2},{4,5},{5,4},{6,7},{7,6},{8,9},{9,8},{10,11... | collective-permute-start | bytes 1376264 | tf_op jit(solution)/shard_map/ppermute | solution.py:412
  71.2 0.8 copy-start.21

commit v4 on v3

--- a/solution.py
+++ b/solution.py
@@ -1,6 +1,7 @@
 import jax
 import jax.numpy as jnp
 from jax import lax
+from jax.experimental.layout import Layout, with_layout_constraint
 from jax.experimental import pallas as pl
 from jax.experimental.pallas import tpu as pltpu
 from jax.sharding import PartitionSpec as P
@@ -24,7 +25,6 @@
 SPECS = {"s": SMEM, "v": VMEM, "a": ANY, "h": HBM}
 PAIRS = [[(0, 0), (0, 1), (1, 0), (1, 1)]] * (REACH - 1) + [[(0, 0), (0, 1), (1, 1)]]
 MINE = 2 * PAIR_TILES
-MATES = [PAIR_TILES * (len(p) - 2) for p in PAIRS]
 
 
 def nn(a, b):
@@ -228,23 +228,13 @@
 
 
 def combine(
-    place_ref, far_plan, near_plan, parent_plan, arrived_in, parents_in, swapped_in, sums,
-    far_remote, near_remote, parent_remote, basis, transfer,
-    arrived, parents, swapped, far_acc, near_acc, sems, later=()
+    place_ref, far_plan, near_plan, parent_plan, arrived, parents, swapped, sums,
+    far_remote, near_remote, parent_remote, basis, transfer, far_acc, near_acc
 ):
     core = place_ref[0]
     leaves = basis.shape[0]
-    copies = fetch(
-        [(swapped_in, swapped), (parents_in.at[:, pl.ds(0, 64)], parents)]
-        + [(a.at[pl.ds(0, MINE)], arrived.at[i]) for i, a in enumerate(arrived_in)]
-        + list(later),
-        sems,
-    )
     far_acc[...] = jnp.zeros(far_acc.shape, F32)
     near_acc[...] = jnp.zeros(near_acc.shape, F32)
-    first = 2 + REACH + len(later) // 3
-    for copy in copies[:first]:
-        copy.wait()
     row = 0
     for step in range(REACH):
         for side in range(2):
@@ -260,7 +250,7 @@
                         tile = swapped[row]
                         row += 1
                     else:
-                        tile = arrived[step, other * PAIR_TILES + i]
+                        tile = arrived[step][other * PAIR_TILES + i]
                     if i < FAR_TILES:
                         plan, blocks, acc = far_plan, far_remote, far_acc
                         slot = order * CAP0 + 2 * i
@@ -278,13 +268,11 @@
     chips = parents.shape[0]
     left = left_mask()
     mates_parents = row
-    for copy in copies[first:]:
-        copy.wait()
 
     def one_chip(chip, total):
         xs, ws = [], []
         for side in range(2):
-            tile = swapped[mates_parents + chip] if side else parents[chip]
+            tile = swapped[mates_parents + chip] if side else parents[chip, 0:64, :]
             member = jnp.where(core == side, 0, 1)
             turned = beside(tile[:, 64:], tile[:, :64])
             slot = (2 * chip + member) * 2
@@ -328,7 +316,7 @@
 
 
 def middle_kernel(*refs):
-    inputs, (out, own, up), scratch = refs[:-9], refs[-9:-6], refs[-6:]
+    inputs, (out, own, up), scratch = refs[:-5], refs[-5:-2], refs[-2:]
     basis, transfer = inputs[-2:]
     tiles = combine(*split_refs(inputs), *scratch)
     for i, tile in enumerate(tiles):
@@ -337,12 +325,8 @@
 
 
 def last_kernel(*refs):
-    sent = 4 + REACH + 2
-    inputs, statics, rest = refs[:sent], refs[sent : sent + 6], refs[sent + 6 :]
-    out, scratch, held = rest[0], rest[1:7], rest[7:]
-    later = [(statics[i], held[i]) for i in (1, 2, 3, 0, 4, 5)]
-    tiles = combine(*split_refs(inputs + held), *scratch, later)
-    for i, tile in enumerate(tiles):
+    inputs, out, scratch = refs[:-3], refs[-3], refs[-2:]
+    for i, tile in enumerate(combine(*split_refs(inputs), *scratch)):
         out[:, 128 * i : 128 * (i + 1)] = tile
 
 
@@ -380,6 +364,7 @@
     at = lax.axis_index("clu").astype(jnp.int32)
     place = jnp.stack([at & 1, at >> 1])
     near_remote, far_remote, parent_remote = near_remote[0], far_remote[0], parent_remote[0]
+    far_remote = with_layout_constraint(far_remote, Layout((0, 1, 2)))
     far_list, near_list = far_list.T, near_list.T
     same_core = [[2 * c + k for c in range(chips)] for k in range(2)]
 
@@ -398,23 +383,19 @@
         pltpu.VMEM(far_blocks.shape, BF16),
         pltpu.VMEM(near_blocks.shape, BF16),
     ]
-    combine_scratch = [
-        pltpu.VMEM((REACH, MINE, 64, 128), BF16),
-        pltpu.VMEM((chips, 64, 128), BF16),
-        pltpu.VMEM((sum(MATES) + chips, 64, 128), BF16),
-        pltpu.VMEM((leaves + 1, 64, 128), F32),
-        pltpu.VMEM((leaves + 1, 64, 128), F32),
-        dma((2 + REACH,)),
-    ]
+    combine_scratch = [pltpu.VMEM((leaves + 1, 64, 128), F32)] * 2
     messages = [shape((PAIR_TILES * len(p), 64, 128), BF16) for p in PAIRS]
 
     def crosswise(x):
         return lax.ppermute(x, "clu", mates(devices))
 
     def exchange(own, up, asks, last):
+        nonlocal far_remote, statics
         parents = lax.all_to_all(up, "clu", 0, 0, tiled=True, axis_index_groups=same_core)
         mate = crosswise(own)
         if asks is None:
+            parents, far_remote = lax.optimization_barrier((parents, far_remote))
+            statics = (far_remote, *statics[1:])
             asks = parents[:, 64, :].astype(jnp.int32)
             asks = (asks, crosswise(asks))
         packed = call(
@@ -444,7 +425,7 @@
         inputs = (place, far_plan, near_plan, parent_plan, *arrived, parents, swapped, sums, *held)
         return inputs, asks
 
-    kinds = "ssss" + "a" * (REACH + 2) + "v" * 6
+    kinds = "ssss" + "v" * (REACH + 8)
     lifted = (values.T, basis, transfer, far_plan, near_plan)
     own, up = call(
         lift_kernel, "hhhhh", [own_shape, shape((chips, 80, 128), BF16)],
@@ -457,13 +438,7 @@
         combine_scratch, inputs, 4e9,
     )
     inputs, _ = exchange(own, up, asks, True)
-    loaded = inputs[4 + REACH + 2 :]
-    second = call(
-        last_kernel, "ssss" + "a" * (REACH + 8), out_shape,
-        combine_scratch[:-1] + [dma((2 + REACH + len(loaded),))]
-        + [pltpu.VMEM(x.shape, x.dtype) for x in loaded],
-        inputs, 4e9, 60,
-    )
+    second = call(last_kernel, kinds, out_shape, combine_scratch, inputs, 4e9, 16)
     return first.T, second.T
 
 

time: 78.8 us -> 73.7 us (0.935)
  Pallas kernels: 28.2 us -> 25 us
  local copies, waits for them, and re-layouts: 4.16 us -> 3.1 us
  waiting for transfers between devices: 10.9 us -> 9.92 us
    pallas_call x7, Pallas kernels: 28.2 us -> 25 us  [call(): pl.pallas_call(kernel, out_shape=outs, in_specs=[SPECS[k] for k in kinds]...]
    all_to_all x2, waiting for transfers between devices: 7.55 us -> 5.69 us  [exchange(): lax.all_to_all(up, 'clu', 0, 0, tiled=True, axis_index_groups=same_core)]
    unnamed x45 -> x47, local copies, waits for them, and re-layouts: 4.09 us -> 2.99 us
    ppermute x5, waiting for transfers between devices: 3.25 us -> 4.22 us  [crosswise(): return lax.ppermute(x, 'clu', mates(devices))]
  transfers between devices with their start and end apart: 13 -> 13, of which waited for: 3 -> 4; matrix products, arithmetic and copies ran while one was open for 2% -> 3% of each run, Pallas kernels for 15% -> 17%
where the time goes in v4:
time: 73.7 us; the launch traced here: 73.2 us
  starting transfers between devices  33.7 us (46%)
  Pallas kernels  25 us (34%)
  waiting for transfers between devices  9.92 us (13%)
  local copies, waits for them, and re-layouts  3.1 us (4%)
  between operations  1.17 us (2%)
    pallas_call x7, Pallas kernels, call(): pl.pallas_call(kernel, out_shape=outs, in_specs=[SPECS[k] for k in kinds]...  25 us
    ppermute x6, starting transfers between devices, exchange(): lax.ppermute(m, 'clu', outward(devices, d + 1))  20.5 us
    all_to_all x2, starting transfers between devices, exchange(): lax.all_to_all(up, 'clu', 0, 0, tiled=True, axis_index_groups=same_core)  12.1 us
    all_to_all x2, waiting for transfers between devices, exchange(): lax.all_to_all(up, 'clu', 0, 0, tiled=True, axis_index_groups=same_core)  5.69 us
    ppermute x5, waiting for transfers between devices, crosswise(): return lax.ppermute(x, 'clu', mates(devices))  4.22 us
    unnamed x47, local copies, waits for them, and re-layouts  2.99 us
  transfers between devices with their start and end apart: 13, of which 4 were waited for; matrix products, arithmetic and copies ran while one was open for 3% of the time, Pallas kernels for 17%

profile of v4, /device:TPU:0, one launch (start us, length us, event | category | flops | bytes accessed | tf_op | source)
XLA Modules:
  0.0 73.2 jit_solution(9507150034016345399)
XLA Ops:
  0.6 2.7 %shard_map.140 = (bf16[16,64,128]{2,1,0:T(8,128)(2,1)}, bf16[8,80,128]{2,1,0:T(8,128)(2,1)}) custom-call(bf16[64,1024]{1,0:T(8,128)(2,1)} %bitcast.27, bf16[16,64,64]{2,1,0:T(8,128)(2,1)} %refs_13_.3, bf16[16,64,64]{2,1,0:T(8,128)(2,1)} %refs_14_.1, s32[1,2,72]{2,1,0:T(2,128)} %refs_1_.5, s32[1,2,24]{2,1,0:T(2,128)} %refs_2_.5), custom_call_target="tpu_custom_call" | custom-call | flops 1000000000 | bytes 393984 | tf_op jit(solution)/shard_map/pallas_call | solution.py:335
  3.3 7.4 %all-to-all-start = ((bf16[8,80,128]{2,1,0:T(8,128)(2,1)}), bf16[8,80,128]{2,1,0:T(8,128)(2,1)S(1)}, u32[]{:S(2)}, u32[]{:S(2)}) async-start(bf16[8,80,128]{2,1,0:T(8,128)(2,1)} %get-tuple-element.31), calls=%async_computation | async-start | bytes 327680 | tf_op jit(solution)/shard_map/all_to_all | solution.py:394
  10.7 0.0 collective-permute-start.1
  10.8 1.8 %copy.25 = bf16[1,72,64,64]{3,2,1,0:T(8,128)(2,1)S(1)} copy(bf16[1,72,64,64]{1,3,2,0:T(8,128)(2,1)S(1)} %copy-done.22) | data formatting | bytes 1179648 | tf_op args[10]
  12.6 5.7 %all-to-all-done.refs_7_ = bf16[8,80,128]{2,1,0:T(8,128)(2,1)S(1)} async-done(((bf16[8,80,128]{2,1,0:T(8,128)(2,1)}), bf16[8,80,128]{2,1,0:T(8,128)(2,1)S(1)}, u32[]{:S(2)}, u32[]{:S(2)}) %all-to-all-start) | async-done | bytes 163872 | tf_op jit(solution)/shard_map/all_to_all | solution.py:394
  18.4 0.1 collective-permute-start
  18.4 0.1 pad_add_fusion.place_ref.refs_0_
  18.5 0.0 copy-start.5
  18.5 0.0 copy-start.7
  18.6 0.0 copy-start.8
  18.6 0.0 copy-start.12
  18.6 0.0 copy-start.13
  18.6 0.0 copy-start.14
  18.6 0.0 copy-start.16
  18.6 0.0 collective-permute-done.1.mate.refs_6_
  18.6 1.0 %collective-permute-done.mate_asks = s32[8,128]{1,0:T(8,128)S(1)} collective-permute-done((s32[8,128]{1,0:T(8,128)S(1)}, s32[8,128]{1,0:T(8,128)S(1)}, u32[]{:S(2)}, u32[]{:S(2)}) %collective-permute-start) | collective-permute-done | bytes 4128 | tf_op jit(solution)/shard_map/ppermute | solution.py:390
  19.6 1.5 %shard_map.141 = (bf16[16,64,128]{2,1,0:T(8,128)(2,1)S(1)}, bf16[16,64,128]{2,1,0:T(8,128)(2,1)S(1)}, bf16[12,64,128]{2,1,0:T(8,128)(2,1)S(1)}) custom-call(s32[2]{0:T(128)S(1)} %pad_add_fusion.place_ref.refs_0_, s32[8,128]{1,0:T(8,128)S(1)} %fusion.asks, s32[8,128]{1,0:T(8,128)S(1)} %collective-permute-done.mate_asks, bf16[16,64,128]{2,1,0:T(8,128)(2,1)S(1)} %copy-done.9, ...), custom_call_target="tpu_custom_call" | custom-call | flops 2000000000 | bytes 532488 | tf_op jit(solution)/shard_map/pallas_call | solution.py:335
  21.1 2.7 %collective-permute-start.4 = (bf16[12,64,128]{2,1,0:T(8,128)(2,1)S(1)}, bf16[12,64,128]{2,1,0:T(8,128)(2,1)S(1)}, u32[]{:S(2)}, u32[]{:S(2)}) collective-permute-start(bf16[12,64,128]{2,1,0:T(8,128)(2,1)S(1)} %get-tuple-element.36), channel_id=1, source_target_pairs={{0,6},{2,8},{4,10},{6,12},{8,14},{7,1},{9,3},{11,5},{13,7},{15,9},... | collective-permute-start | bytes 589832 | tf_op jit(solution)/shard_map/ppermute | solution.py:405
  23.8 3.2 %collective-permute-start.2 = (bf16[16,64,128]{2,1,0:T(8,128)(2,1)S(1)}, bf16[16,64,128]{2,1,0:T(8,128)(2,1)S(1)}, u32[]{:S(2)}, u32[]{:S(2)}) collective-permute-start(bf16[16,64,128]{2,1,0:T(8,128)(2,1)S(1)} %get-tuple-element.34), channel_id=1, source_target_pairs={{0,2},{2,4},{4,6},{6,8},{8,10},{10,12},{12,14},{3,1},{5,3},{7,5},{... | collective-permute-start | bytes 786440 | tf_op jit(solution)/shard_map/ppermute | solution.py:405
  26.9 2.7 %collective-permute-start.3 = (bf16[16,64,128]{2,1,0:T(8,128)(2,1)S(1)}, bf16[16,64,128]{2,1,0:T(8,128)(2,1)S(1)}, u32[]{:S(2)}, u32[]{:S(2)}) collective-permute-start(bf16[16,64,128]{2,1,0:T(8,128)(2,1)S(1)} %get-tuple-element.35), channel_id=1, source_target_pairs={{0,4},{2,6},{4,8},{6,10},{8,12},{10,14},{5,1},{7,3},{9,5},{11,7},{... | collective-permute-start | bytes 786440 | tf_op jit(solution)/shard_map/ppermute | solution.py:405
  29.8 0.0 copy-start.18
  29.8 4.5 %shard_map.142 = (f32[17,64,128]{2,1,0:T(8,128)S(1)}, bf16[72,64,64]{2,1,0:T(8,128)(2,1)S(1)}, bf16[24,64,64]{2,1,0:T(8,128)(2,1)S(1)}, bf16[32,64,64]{2,1,0:T(8...) custom-call(s32[2]{0:T(128)S(1)} %pad_add_fusion.place_ref.refs_0_, ...), custom_call_target="tpu_custom_call" | custom-call | flops 7000000000 | bytes 3933960 | tf_op jit(solution)/shard_map/pallas_call | solution.py:335
  34.3 0.0 collective-permute-done.4.refs_6_
  34.3 0.0 collective-permute-done.2.refs_4_
  34.3 0.0 collective-permute-done.3.refs_5_
  34.4 0.1 pad_maximum_fusion
  34.5 0.6 collective-permute-start.5
  35.1 1.4 %collective-permute-done.5.refs_8_ = bf16[28,64,128]{2,1,0:T(8,128)(2,1)S(1)} collective-permute-done((bf16[28,64,128]{2,1,0:T(8,128)(2,1)S(1)}, bf16[28,64,128]{2,1,0:T(8,128)(2,1)S(1)}, u32[]{:S(2)}, u32[]{:S(2)}) %collective-permute-start.5) | collective-permute-done | bytes 458784 | tf_op jit(solution)/shard_map/ppermute | solution.py:390
  36.5 4.6 %shard_map.143 = (bf16[64,1024]{1,0:T(8,128)(2,1)}, bf16[16,64,128]{2,1,0:T(8,128)(2,1)S(1)}, bf16[8,64,128]{2,1,0:T(8,128)(2,1)}) custom-call(s32[2]{0:T(128)S(1)} %pad_add_fusion.place_ref.refs_0_, s32[1,2,72]{2,1,0:T(2,128)S(1)} %copy-done.14, s32[1,2,24]{2,1,0:T(2,128)S(1)} %copy-done.16, s32[1,2,32]{2,1,0:T(2,128)S(1)} %copy-done.18, ...), custom_call_target="tpu_custom_call" | custom-call | flops 4000000000 | bytes 3212296 | tf_op jit(solution)/shard_map/pallas_call | solution.py:335
  41.1 0.4 collective-permute-start.6
  41.5 4.7 %all-to-all-start.1 = ((bf16[8,64,128]{2,1,0:T(8,128)(2,1)}), bf16[8,64,128]{2,1,0:T(8,128)(2,1)S(1)}, u32[]{:S(2)}, u32[]{:S(2)}) async-start(bf16[8,64,128]{2,1,0:T(8,128)(2,1)} %get-tuple-element.54), calls=%async_computation.1 | async-start | bytes 262144 | tf_op jit(solution)/shard_map/all_to_all | solution.py:394
  46.2 0.0 collective-permute-done.6.mate.refs_6_
  46.2 2.1 %shard_map.144 = (bf16[16,64,128]{2,1,0:T(8,128)(2,1)}, bf16[16,64,128]{2,1,0:T(8,128)(2,1)}, bf16[12,64,128]{2,1,0:T(8,128)(2,1)}) custom-call(s32[2]{0:T(128)S(1)} %pad_add_fusion.place_ref.refs_0_, s32[8,128]{1,0:T(8,128)S(1)} %fusion.asks, s32[8,128]{1,0:T(8,128)S(1)} %collective-permute-done.mate_asks, ...), custom_call_target="tpu_custom_call" | custom-call | flops 2000000000 | bytes 532488 | tf_op jit(solution)/shard_map/pallas_call | solution.py:335
  48.3 4.8 %collective-permute-start.9 = (bf16[12,64,128]{2,1,0:T(8,128)(2,1)}, bf16[12,64,128]{2,1,0:T(8,128)(2,1)S(1)}, u32[]{:S(2)}, u32[]{:S(2)}) collective-permute-start(bf16[12,64,128]{2,1,0:T(8,128)(2,1)} %get-tuple-element.53), channel_id=1, source_target_pairs={{0,6},{2,8},{4,10},{6,12},{8,14},{7,1},{9,3},{11,5},{13,7},{15,9},... | collective-permute-start | bytes 589832 | tf_op jit(solution)/shard_map/ppermute | solution.py:405
  53.2 3.4 %collective-permute-start.7 = (bf16[16,64,128]{2,1,0:T(8,128)(2,1)}, bf16[16,64,128]{2,1,0:T(8,128)(2,1)S(1)}, u32[]{:S(2)}, u32[]{:S(2)}) collective-permute-start(bf16[16,64,128]{2,1,0:T(8,128)(2,1)} %get-tuple-element.51), channel_id=1, source_target_pairs={{0,2},{2,4},{4,6},{6,8},{8,10},{10,12},{12,14},{3,1},{5,3},{7,5},{... | collective-permute-start | bytes 786440 | tf_op jit(solution)/shard_map/ppermute | solution.py:405
  56.6 0.0 copy-start.6
  56.6 0.0 copy-start.15
  56.6 0.0 copy-start.17
  56.6 3.7 %collective-permute-start.8 = (bf16[16,64,128]{2,1,0:T(8,128)(2,1)}, bf16[16,64,128]{2,1,0:T(8,128)(2,1)S(1)}, u32[]{:S(2)}, u32[]{:S(2)}) collective-permute-start(bf16[16,64,128]{2,1,0:T(8,128)(2,1)} %get-tuple-element.52), channel_id=1, source_target_pairs={{0,4},{2,6},{4,8},{6,10},{8,12},{10,14},{5,1},{7,3},{9,5},{11,7},{... | collective-permute-start | bytes 786440 | tf_op jit(solution)/shard_map/ppermute | solution.py:405
  60.3 5.7 %shard_map.145.refs_9_ = f32[17,64,128]{2,1,0:T(8,128)} custom-call(s32[2]{0:T(128)} %copy-done.19, s32[8,16]{1,0:T(8,128)} %bitcast.23, s32[8,16]{1,0:T(8,128)} %bitcast.25, s32[1,2,72]{2,1,0:T(2,128)} %refs_1_.5, s32[1,2,24]{2,1,0:T(2,128)} %refs_2_.5, bf16[16,64,128]{2,1,0:T(8,128)(2,1)} %copy-done.10, bf16[16,64,128]{2,1,0:T(8,128)(2,1)} %copy-done.11, ...), custom_call_target="tpu_custom_call" | custom-call | flops 6000000000 | bytes 3409672 | tf_op jit(solution)/shard_map/pallas_call | solution.py:335
  66.0 0.0 all-to-all-done.1.refs_7_
  66.1 0.0 collective-permute-done.9.refs_6_
  66.1 0.0 collective-permute-done.7.refs_4_
  66.1 0.1 pad_maximum_fusion.1
  66.2 0.1 collective-permute-start.10
  66.3 1.8 %collective-permute-done.10.refs_8_ = bf16[28,64,128]{2,1,0:T(8,128)(2,1)S(1)} collective-permute-done((bf16[28,64,128]{2,1,0:T(8,128)(2,1)S(1)}, bf16[28,64,128]{2,1,0:T(8,128)(2,1)S(1)}, u32[]{:S(2)}, u32[]{:S(2)}) %collective-permute-start.10) | collective-permute-done | bytes 458784 | tf_op jit(solution)/shard_map/ppermute | solution.py:390
  68.1 1.0 %copy-done.21 = f32[17,64,128]{2,1,0:T(8,128)S(1)} copy-done((f32[17,64,128]{2,1,0:T(8,128)S(1)}, f32[17,64,128]{2,1,0:T(8,128)}, u32[]{:S(2)}) %copy-start.21) | copy-done | bytes 557080
  69.2 4.0 %shard_map.146 = bf16[64,1024]{1,0:T(8,128)(2,1)} custom-call(s32[2]{0:T(128)S(1)} %copy-done.20, s32[1,2,72]{2,1,0:T(2,128)S(1)} %copy-done.15, s32[1,2,24]{2,1,0:T(2,128)S(1)} %copy-done.17, s32[1,2,32]{2,1,0:T(2,128)S(1)} %copy-done.18, bf16[16,64,128]{2,1,0:T(8,128)(2,1)S(1)} %collective-permute-done.7.refs_4_, ...), custom_call_target="tpu_custom_call" | custom-call | flops 4000000000 | bytes 3179528 | tf_op jit(solution)/shard_map/pallas_call | solution.py:335
  (44 shorter events, 0.2 us)
Async XLA Ops:
  0.6 10.1 %copy-start.22 = (bf16[1,72,64,64]{1,3,2,0:T(8,128)(2,1)S(1)}, bf16[1,72,64,64]{1,3,2,0:T(8,128)(2,1)}, u32[]{:S(2)}) copy-start(bf16[1,72,64,64]{1,3,2,0:T(8,128)(2,1)} %param.23) | copy-start | bytes 1769476
  3.3 16.3 %copy-start.9 = (bf16[16,64,128]{2,1,0:T(8,128)(2,1)S(1)}, bf16[16,64,128]{2,1,0:T(8,128)(2,1)}, u32[]{:S(2)}) copy-start(bf16[16,64,128]{2,1,0:T(8,128)(2,1)} %get-tuple-element.33.own.refs_5_) | copy-start | bytes 786436
  3.3 15.0 %all-to-all-start = ((bf16[8,80,128]{2,1,0:T(8,128)(2,1)}), bf16[8,80,128]{2,1,0:T(8,128)(2,1)S(1)}, u32[]{:S(2)}, u32[]{:S(2)}) async-start(bf16[8,80,128]{2,1,0:T(8,128)(2,1)} %get-tuple-element.31), calls=%async_computation | async-start | bytes 327680 | tf_op jit(solution)/shard_map/all_to_all | solution.py:394
  10.7 7.9 %collective-permute-start.1 = (bf16[16,64,128]{2,1,0:T(8,128)(2,1)}, bf16[16,64,128]{2,1,0:T(8,128)(2,1)S(1)}, u32[]{:S(2)}, u32[]{:S(2)}) collective-permute-start(bf16[16,64,128]{2,1,0:T(8,128)(2,1)} %get-tuple-element.33.own.refs_5_), channel_id=1, source_target_pairs={{0,1},{1,0},{2,3},{3,2},{4,5},{5,4},{6,7},{7,6},{8,9},{9,8},{10,11... | collective-permute-start | bytes 786440 | tf_op jit(solution)/shard_map/ppermute | solution.py:390
  12.6 17.1 %copy-start = (bf16[1,72,64,64]{3,2,1,0:T(8,128)(2,1)}, bf16[1,72,64,64]{3,2,1,0:T(8,128)(2,1)S(1)}, u32[]{:S(2)}) copy-start(bf16[1,72,64,64]{3,2,1,0:T(8,128)(2,1)S(1)} %copy.25) | copy-start | bytes 1769476
  18.4 1.2 %collective-permute-start = (s32[8,128]{1,0:T(8,128)S(1)}, s32[8,128]{1,0:T(8,128)S(1)}, u32[]{:S(2)}, u32[]{:S(2)}) collective-permute-start(s32[8,128]{1,0:T(8,128)S(1)} %fusion.asks), channel_id=1, source_target_pairs={{0,1},{1,0},{2,3},{3,2},{4,5},{5,4},{6,7},{7,6},{8,9},{9,8},{10,11... | collective-permute-start | bytes 12296 | tf_op jit(solution)/shard_map/ppermute | solution.py:390
  18.5 27.7 %copy-start.19 = (s32[2]{0:T(128)}, s32[2]{0:T(128)S(1)}, u32[]{:S(2)}) copy-start(s32[2]{0:T(128)S(1)} %pad_add_fusion.place_ref.refs_0_) | copy-start | bytes 28
  18.5 11.2 %copy-start.2 = (bf16[16,8,64,64]{3,2,1,0:T(8,128)(2,1)S(1)}, bf16[16,8,64,64]{3,2,1,0:T(8,128)(2,1)}, u32[]{:S(2)}) copy-start(bf16[16,8,64,64]{3,2,1,0:T(8,128)(2,1)} %refs_7_.3) | copy-start | bytes 3145732
  18.5 11.2 %copy-start.3 = (bf16[16,8,64,64]{3,2,1,0:T(8,128)(2,1)S(1)}, bf16[16,8,64,64]{3,2,1,0:T(8,128)(2,1)}, u32[]{:S(2)}) copy-start(bf16[16,8,64,64]{3,2,1,0:T(8,128)(2,1)} %refs_8_.3) | copy-start | bytes 3145732
  18.5 11.2 %copy-start.4 = (bf16[1,32,64,64]{3,2,1,0:T(8,128)(2,1)S(1)}, bf16[1,32,64,64]{3,2,1,0:T(8,128)(2,1)}, u32[]{:S(2)}) copy-start(bf16[1,32,64,64]{3,2,1,0:T(8,128)(2,1)} %param.25) | copy-start | bytes 786436
  18.5 11.2 %copy-start.5 = (bf16[1,24,64,64]{3,2,1,0:T(8,128)(2,1)S(1)}, bf16[1,24,64,64]{3,2,1,0:T(8,128)(2,1)}, u32[]{:S(2)}) copy-start(bf16[1,24,64,64]{3,2,1,0:T(8,128)(2,1)} %param.21) | copy-start | bytes 589828
  18.5 11.2 %copy-start.7 = (bf16[16,64,64]{2,1,0:T(8,128)(2,1)S(1)}, bf16[16,64,64]{2,1,0:T(8,128)(2,1)}, u32[]{:S(2)}) copy-start(bf16[16,64,64]{2,1,0:T(8,128)(2,1)} %refs_13_.3) | copy-start | bytes 393220
  18.6 11.2 %copy-start.8 = (bf16[16,64,64]{2,1,0:T(8,128)(2,1)S(1)}, bf16[16,64,64]{2,1,0:T(8,128)(2,1)}, u32[]{:S(2)}) copy-start(bf16[16,64,64]{2,1,0:T(8,128)(2,1)} %refs_14_.1) | copy-start | bytes 393220
  18.6 11.2 %copy-start.12 = (s32[16,8]{0,1:T(8,128)S(1)}, s32[16,8]{0,1:T(8,128)}, u32[]{:S(2)}) copy-start(s32[16,8]{0,1:T(8,128)} %param.18) | copy-start | bytes 1540
  18.6 11.2 %copy-start.13 = (s32[16,8]{0,1:T(8,128)S(1)}, s32[16,8]{0,1:T(8,128)}, u32[]{:S(2)}) copy-start(s32[16,8]{0,1:T(8,128)} %param.16) | copy-start | bytes 1540
  18.6 11.2 %copy-start.14 = (s32[1,2,72]{2,1,0:T(2,128)S(1)}, s32[1,2,72]{2,1,0:T(2,128)}, u32[]{:S(2)}) copy-start(s32[1,2,72]{2,1,0:T(2,128)} %refs_1_.5) | copy-start | bytes 1732
  18.6 11.2 %copy-start.16 = (s32[1,2,24]{2,1,0:T(2,128)S(1)}, s32[1,2,24]{2,1,0:T(2,128)}, u32[]{:S(2)}) copy-start(s32[1,2,24]{2,1,0:T(2,128)} %refs_2_.5) | copy-start | bytes 580
  21.1 13.3 %collective-permute-start.4 = (bf16[12,64,128]{2,1,0:T(8,128)(2,1)S(1)}, bf16[12,64,128]{2,1,0:T(8,128)(2,1)S(1)}, u32[]{:S(2)}, u32[]{:S(2)}) collective-permute-start(bf16[12,64,128]{2,1,0:T(8,128)(2,1)S(1)} %get-tuple-element.36), channel_id=1, source_target_pairs={{0,6},{2,8},{4,10},{6,12},{8,14},{7,1},{9,3},{11,5},{13,7},{15,9},... | collective-permute-start | bytes 589832 | tf_op jit(solution)/shard_map/ppermute | solution.py:405
  23.8 10.6 %collective-permute-start.2 = (bf16[16,64,128]{2,1,0:T(8,128)(2,1)S(1)}, bf16[16,64,128]{2,1,0:T(8,128)(2,1)S(1)}, u32[]{:S(2)}, u32[]{:S(2)}) collective-permute-start(bf16[16,64,128]{2,1,0:T(8,128)(2,1)S(1)} %get-tuple-element.34), channel_id=1, source_target_pairs={{0,2},{2,4},{4,6},{6,8},{8,10},{10,12},{12,14},{3,1},{5,3},{7,5},{... | collective-permute-start | bytes 786440 | tf_op jit(solution)/shard_map/ppermute | solution.py:405
  26.9 7.4 %collective-permute-start.3 = (bf16[16,64,128]{2,1,0:T(8,128)(2,1)S(1)}, bf16[16,64,128]{2,1,0:T(8,128)(2,1)S(1)}, u32[]{:S(2)}, u32[]{:S(2)}) collective-permute-start(bf16[16,64,128]{2,1,0:T(8,128)(2,1)S(1)} %get-tuple-element.35), channel_id=1, source_target_pairs={{0,4},{2,6},{4,8},{6,10},{8,12},{10,14},{5,1},{7,3},{9,5},{11,7},{... | collective-permute-start | bytes 786440 | tf_op jit(solution)/shard_map/ppermute | solution.py:405
  29.8 6.8 %copy-start.18 = (s32[1,2,32]{2,1,0:T(2,128)S(1)}, s32[1,2,32]{2,1,0:T(2,128)}, u32[]{:S(2)}) copy-start(s32[1,2,32]{2,1,0:T(2,128)} %refs_3_.9) | copy-start | bytes 772
  34.5 2.1 %collective-permute-start.5 = (bf16[28,64,128]{2,1,0:T(8,128)(2,1)S(1)}, bf16[28,64,128]{2,1,0:T(8,128)(2,1)S(1)}, u32[]{:S(2)}, u32[]{:S(2)}) collective-permute-start(bf16[28,64,128]{2,1,0:T(8,128)(2,1)S(1)} %pad_maximum_fusion), channel_id=1, source_target_pairs={{0,1},{1,0},{2,3},{3,2},{4,5},{5,4},{6,7},{7,6},{8,9},{9,8},{10,11... | collective-permute-start | bytes 1376264 | tf_op jit(solution)/shard_map/ppermute | solution.py:390
  41.1 7.2 %copy-start.10 = (bf16[16,64,128]{2,1,0:T(8,128)(2,1)}, bf16[16,64,128]{2,1,0:T(8,128)(2,1)S(1)}, u32[]{:S(2)}) copy-start(bf16[16,64,128]{2,1,0:T(8,128)(2,1)S(1)} %get-tuple-element.50.own.refs_5_) | copy-start | bytes 786436
  41.1 5.1 %collective-permute-start.6 = (bf16[16,64,128]{2,1,0:T(8,128)(2,1)S(1)}, bf16[16,64,128]{2,1,0:T(8,128)(2,1)S(1)}, u32[]{:S(2)}, u32[]{:S(2)}) collective-permute-start(bf16[16,64,128]{2,1,0:T(8,128)(2,1)S(1)} %get-tuple-element.50.own.refs_5_), channel_id=1, source_target_pairs={{0,1},{1,0},{2,3},{3,2},{4,5},{5,4},{6,7},{7,6},{8,9},{9,8},{10,11... | collective-permute-start | bytes 786440 | tf_op jit(solution)/shard_map/ppermute | solution.py:390
  41.5 24.6 %all-to-all-start.1 = ((bf16[8,64,128]{2,1,0:T(8,128)(2,1)}), bf16[8,64,128]{2,1,0:T(8,128)(2,1)S(1)}, u32[]{:S(2)}, u32[]{:S(2)}) async-start(bf16[8,64,128]{2,1,0:T(8,128)(2,1)} %get-tuple-element.54), calls=%async_computation.1 | async-start | bytes 262144 | tf_op jit(solution)/shard_map/all_to_all | solution.py:394
  46.2 2.2 %copy-start.11 = (bf16[16,64,128]{2,1,0:T(8,128)(2,1)}, bf16[16,64,128]{2,1,0:T(8,128)(2,1)S(1)}, u32[]{:S(2)}) copy-start(bf16[16,64,128]{2,1,0:T(8,128)(2,1)S(1)} %collective-permute-done.6.mate.refs_6_) | copy-start | bytes 786436
  48.3 17.7 %collective-permute-start.9 = (bf16[12,64,128]{2,1,0:T(8,128)(2,1)}, bf16[12,64,128]{2,1,0:T(8,128)(2,1)S(1)}, u32[]{:S(2)}, u32[]{:S(2)}) collective-permute-start(bf16[12,64,128]{2,1,0:T(8,128)(2,1)} %get-tuple-element.53), channel_id=1, source_target_pairs={{0,6},{2,8},{4,10},{6,12},{8,14},{7,1},{9,3},{11,5},{13,7},{15,9},... | collective-permute-start | bytes 589832 | tf_op jit(solution)/shard_map/ppermute | solution.py:405
  53.2 12.9 %collective-permute-start.7 = (bf16[16,64,128]{2,1,0:T(8,128)(2,1)}, bf16[16,64,128]{2,1,0:T(8,128)(2,1)S(1)}, u32[]{:S(2)}, u32[]{:S(2)}) collective-permute-start(bf16[16,64,128]{2,1,0:T(8,128)(2,1)} %get-tuple-element.51), channel_id=1, source_target_pairs={{0,2},{2,4},{4,6},{6,8},{8,10},{10,12},{12,14},{3,1},{5,3},{7,5},{... | collective-permute-start | bytes 786440 | tf_op jit(solution)/shard_map/ppermute | solution.py:405
  56.6 11.5 %copy-start.1 = (bf16[1,72,64,64]{3,2,1,0:T(8,128)(2,1)S(1)}, bf16[1,72,64,64]{3,2,1,0:T(8,128)(2,1)}, u32[]{:S(2)}) copy-start(bf16[1,72,64,64]{3,2,1,0:T(8,128)(2,1)} %copy-done) | copy-start | bytes 1769476
  56.6 11.5 %copy-start.6 = (bf16[1,24,64,64]{3,2,1,0:T(8,128)(2,1)S(1)}, bf16[1,24,64,64]{3,2,1,0:T(8,128)(2,1)}, u32[]{:S(2)}) copy-start(bf16[1,24,64,64]{3,2,1,0:T(8,128)(2,1)} %param.21) | copy-start | bytes 589828
  56.6 11.5 %copy-start.15 = (s32[1,2,72]{2,1,0:T(2,128)S(1)}, s32[1,2,72]{2,1,0:T(2,128)}, u32[]{:S(2)}) copy-start(s32[1,2,72]{2,1,0:T(2,128)} %refs_1_.5) | copy-start | bytes 1732
  56.6 11.5 %copy-start.17 = (s32[1,2,24]{2,1,0:T(2,128)S(1)}, s32[1,2,24]{2,1,0:T(2,128)}, u32[]{:S(2)}) copy-start(s32[1,2,24]{2,1,0:T(2,128)} %refs_2_.5) | copy-start | bytes 580
  56.6 11.5 %copy-start.20 = (s32[2]{0:T(128)S(1)}, s32[2]{0:T(128)}, u32[]{:S(2)}) copy-start(s32[2]{0:T(128)} %copy-done.19) | copy-start | bytes 28
  56.6 9.5 %collective-permute-start.8 = (bf16[16,64,128]{2,1,0:T(8,128)(2,1)}, bf16[16,64,128]{2,1,0:T(8,128)(2,1)S(1)}, u32[]{:S(2)}, u32[]{:S(2)}) collective-permute-start(bf16[16,64,128]{2,1,0:T(8,128)(2,1)} %get-tuple-element.52), channel_id=1, source_target_pairs={{0,4},{2,6},{4,8},{6,10},{8,12},{10,14},{5,1},{7,3},{9,5},{11,7},{... | collective-permute-start | bytes 786440 | tf_op jit(solution)/shard_map/ppermute | solution.py:405
  66.2 1.9 %collective-permute-start.10 = (bf16[28,64,128]{2,1,0:T(8,128)(2,1)S(1)}, bf16[28,64,128]{2,1,0:T(8,128)(2,1)S(1)}, u32[]{:S(2)}, u32[]{:S(2)}) collective-permute-start(bf16[28,64,128]{2,1,0:T(8,128)(2,1)S(1)} %pad_maximum_fusion.1), channel_id=1, source_target_pairs={{0,1},{1,0},{2,3},{3,2},{4,5},{5,4},{6,7},{7,6},{8,9},{9,8},{10,11... | collective-permute-start | bytes 1376264 | tf_op jit(solution)/shard_map/ppermute | solution.py:390
  68.1 1.1 %copy-start.21 = (f32[17,64,128]{2,1,0:T(8,128)S(1)}, f32[17,64,128]{2,1,0:T(8,128)}, u32[]{:S(2)}) copy-start(f32[17,64,128]{2,1,0:T(8,128)} %shard_map.145.refs_9_) | copy-start | bytes 1671172

commit v5 on v4

--- a/solution.py
+++ b/solution.py
@@ -195,14 +195,15 @@
             for k in range(0, blocks.shape[1], 2):
                 xs.append(pair_of(table, base, listed[k, leaf], listed[k + 1, leaf], left))
                 ws.append(beside(blocks[leaf, k], blocks[leaf, k + 1]))
-            sums.append(nt(jnp.concatenate(xs, axis=1), jnp.concatenate(ws, axis=1)))
-        out[leaf] = beside(*sums)
+            total = nt(jnp.concatenate(xs, axis=1), jnp.concatenate(ws, axis=1))
+            sums.append(beside(total, jnp.zeros_like(total)))
+        out[0, leaf], out[1, leaf] = sums
     for copy in copies[1 + 2 * CHUNKS :]:
         copy.wait()
-    out[leaves] = jnp.zeros((64, 128), F32)
-    for plan, blocks, base, cap in (
-        (far_plan, far_remote, 0, CAP0),
-        (near_plan, near_remote, half // 2, CAPN),
+    out[:, leaves] = jnp.zeros((2, 64, 128), F32)
+    for kind, plan, blocks, base, cap in (
+        (0, far_plan, far_remote, 0, CAP0),
+        (1, near_plan, near_remote, half // 2, CAPN),
     ):
         for c in range(cap):
             slot = order * cap + c
@@ -212,9 +213,7 @@
             tile = mate[base + leaf // 2]
             x = jnp.where(leaf % 2 == 0, tile[:, :64], tile[:, 64:])
             w = blocks[c if lean else slot]
-            z = jnp.zeros_like(w)
-            w = jnp.concatenate([z, w] if base else [w, z], axis=0)
-            out[where] = out[where] + nt(x, w)
+            out[kind, where, :, 0:64] = out[kind, where, :, 0:64] + nt(x, w)
 
 
 def local_kernel(*refs):
@@ -227,110 +226,136 @@
     local_body(*ins, out, *scratch, *held, list(zip(remote, held)), lean=True)
 
 
-def combine(
-    place_ref, far_plan, near_plan, parent_plan, arrived, parents, swapped, sums,
-    far_remote, near_remote, parent_remote, basis, transfer, far_acc, near_acc
+def diagonal(b0, b1):
+    zero = jnp.zeros_like(b0)
+    return jnp.concatenate([beside(b0, zero), beside(zero, b1)], axis=0)
+
+
+def add_slots(core, side, tile_at, far_plan, near_plan, far_remote, near_remote, acc):
+    leaves = acc.shape[1] - 1
+    for step in range(REACH):
+        for other_target, other in PAIRS[step]:
+            if other_target != side:
+                continue
+            sender = jnp.where(core == side, 0, 1)
+            source = jnp.where(sender == other, 0, 1)
+            away = jnp.where(sender == 0, -2 * (step + 1), 2 * (step + 1))
+            order = offset_index(away + source - core)
+            for i in range(PAIR_TILES):
+                if i < FAR_TILES:
+                    kind, plan, blocks = 0, far_plan, far_remote
+                    slot = order * CAP0 + 2 * i
+                else:
+                    kind, plan, blocks = 1, near_plan, near_remote
+                    slot = order * CAPN + 2 * (i - FAR_TILES)
+                y = nt(tile_at(step, other, i), diagonal(blocks[slot], blocks[slot + 1]))
+                t0, t1 = plan[0, 1, slot], plan[0, 1, slot + 1]
+                t0, t1 = jnp.where(t0 < 0, leaves, t0), jnp.where(t1 < 0, leaves, t1)
+                acc[kind, t0, :, 0:64] = acc[kind, t0, :, 0:64] + y[:, 0:64]
+                acc[kind, t1, :, 64:128] = acc[kind, t1, :, 64:128] + y[:, 64:128]
+
+
+def add_parents(core, side, chips, tile_at, parent_plan, parent_remote, total):
+    left = left_mask()
+    member = jnp.where(core == side, 0, 1)
+
+    def one_chip(chip):
+        tile = tile_at(chip)
+        turned = beside(tile[:, 64:], tile[:, :64])
+        slot = (2 * chip + member) * 2
+        s0, s1 = parent_plan[0, 0, slot], parent_plan[0, 0, slot + 1]
+        t0, t1 = parent_plan[0, 1, slot], parent_plan[0, 1, slot + 1]
+        x0 = jnp.where(s0 > 0, turned, tile)
+        x1 = jnp.where(s1 == 0, turned, tile)
+        zero = jnp.zeros_like(tile)
+        rows = []
+        for p in range(2):
+            x = jnp.where(left, jnp.where(t0 == p, x0, zero), jnp.where(t1 == p, x1, zero))
+            rows.append(x)
+        return jnp.concatenate(rows, axis=0), beside(parent_remote[slot], parent_remote[slot + 1])
+
+    def two_chips(index, total):
+        (x0, w0), (x1, w1) = one_chip(2 * index), one_chip(2 * index + 1)
+        return total + nt(beside(x0, x1), beside(w0, w1))
+
+    if chips % 2:
+        total = total + nt(*one_chip(chips - 1))
+    if chips <= 8:
+        for index in range(chips // 2):
+            total = two_chips(index, total)
+        return total
+    return lax.fori_loop(0, chips // 2, two_chips, total)
+
+
+def arrived_kernel(*refs):
+    place_ref, far_plan, near_plan, parent_plan = refs[:4]
+    arrived = refs[4 : 4 + REACH]
+    parents, _, far_remote, near_remote, parent_remote, acc, total = refs[4 + REACH :]
+    core = place_ref[0]
+    add_slots(
+        core, 0, lambda step, other, i: arrived[step][other * PAIR_TILES + i],
+        far_plan, near_plan, far_remote, near_remote, acc,
+    )
+    total[...] = add_parents(
+        core, 0, parents.shape[0], lambda chip: parents[chip, 0:64, :],
+        parent_plan, parent_remote, jnp.zeros((128, 64), F32),
+    )
+
+
+def swapped_body(
+    place_ref, far_plan, near_plan, parent_plan, swapped, _, total, far_remote, near_remote,
+    parent_remote, basis, transfer, acc
 ):
     core = place_ref[0]
     leaves = basis.shape[0]
-    far_acc[...] = jnp.zeros(far_acc.shape, F32)
-    near_acc[...] = jnp.zeros(near_acc.shape, F32)
-    row = 0
-    for step in range(REACH):
-        for side in range(2):
-            for other_target, other in PAIRS[step]:
-                if other_target != side:
-                    continue
-                sender = jnp.where(core == side, 0, 1)
-                source = jnp.where(sender == other, 0, 1)
-                away = jnp.where(sender == 0, -2 * (step + 1), 2 * (step + 1))
-                order = offset_index(away + source - core)
-                for i in range(PAIR_TILES):
-                    if side:
-                        tile = swapped[row]
-                        row += 1
-                    else:
-                        tile = arrived[step][other * PAIR_TILES + i]
-                    if i < FAR_TILES:
-                        plan, blocks, acc = far_plan, far_remote, far_acc
-                        slot = order * CAP0 + 2 * i
-                    else:
-                        plan, blocks, acc = near_plan, near_remote, near_acc
-                        slot = order * CAPN + 2 * (i - FAR_TILES)
-                    b0, b1 = blocks[slot], blocks[slot + 1]
-                    zero = jnp.zeros_like(b0)
-                    y = nt(tile, jnp.concatenate([beside(b0, zero), beside(zero, b1)], axis=0))
-                    t0, t1 = plan[0, 1, slot], plan[0, 1, slot + 1]
-                    t0, t1 = jnp.where(t0 < 0, leaves, t0), jnp.where(t1 < 0, leaves, t1)
-                    acc[t0, :, 0:64] = acc[t0, :, 0:64] + y[:, 0:64]
-                    acc[t1, :, 64:128] = acc[t1, :, 64:128] + y[:, 64:128]
-
-    chips = parents.shape[0]
+    starts, rows = [], 0
+    for pairs in PAIRS:
+        starts.append(rows)
+        rows += PAIR_TILES * (len(pairs) - 2)
+
+    def tile_at(step, other, i):
+        order = [o for t, o in PAIRS[step] if t == 1].index(other)
+        return swapped[starts[step] + order * PAIR_TILES + i]
+
+    add_slots(core, 1, tile_at, far_plan, near_plan, far_remote, near_remote, acc)
+    parent_sum = add_parents(
+        core, 1, swapped.shape[0] - rows, lambda chip: swapped[rows + chip],
+        parent_plan, parent_remote, total[...],
+    ).astype(BF16)
     left = left_mask()
-    mates_parents = row
-
-    def one_chip(chip, total):
-        xs, ws = [], []
-        for side in range(2):
-            tile = swapped[mates_parents + chip] if side else parents[chip, 0:64, :]
-            member = jnp.where(core == side, 0, 1)
-            turned = beside(tile[:, 64:], tile[:, :64])
-            slot = (2 * chip + member) * 2
-            s0, s1 = parent_plan[0, 0, slot], parent_plan[0, 0, slot + 1]
-            t0, t1 = parent_plan[0, 1, slot], parent_plan[0, 1, slot + 1]
-            x0 = jnp.where(s0 > 0, turned, tile)
-            x1 = jnp.where(s1 == 0, turned, tile)
-            zero = jnp.zeros_like(tile)
-            rows = []
-            for p in range(2):
-                x = jnp.where(left, jnp.where(t0 == p, x0, zero), jnp.where(t1 == p, x1, zero))
-                rows.append(x)
-            xs.append(jnp.concatenate(rows, axis=0))
-            ws.append(beside(parent_remote[slot], parent_remote[slot + 1]))
-        return total + nt(beside(*xs), beside(*ws))
-
-    total = jnp.zeros((128, 64), F32)
-    if chips <= 8:
-        for chip in range(chips):
-            total = one_chip(chip, total)
-    else:
-        total = lax.fori_loop(0, chips, one_chip, total)
-    parent_sum = total.astype(BF16)
+
+    def leaf_pair(kind, i):
+        a, b = acc[kind, 2 * i], acc[kind, 2 * i + 1]
+        crossed = jnp.where(left, b, a)
+        return jnp.where(left, a, b) + beside(crossed[:, 64:], crossed[:, :64])
 
     tiles = []
     for i in range(leaves // 2):
-        halves = []
-        for leaf in (2 * i, 2 * i + 1):
-            p = leaf // FAN
-            down = nt(parent_sum[64 * p : 64 * (p + 1)], transfer[leaf])
-            here, far, near = sums[leaf], far_acc[leaf], near_acc[leaf]
-            summed = (here[:, :64] + far[:, :64] + far[:, 64:] + down).astype(BF16)
-            rest = here[:, 64:] + near[:, :64] + near[:, 64:]
-            halves.append(nt(summed, basis[leaf]) + rest)
-        tiles.append(beside(*halves).astype(BF16))
+        p = 2 * i // FAN
+        both = jnp.concatenate([transfer[2 * i], transfer[2 * i + 1]], axis=0)
+        down = nt(parent_sum[64 * p : 64 * (p + 1)], both)
+        summed = (leaf_pair(0, i) + down).astype(BF16)
+        y = nt(summed, diagonal(basis[2 * i], basis[2 * i + 1])) + leaf_pair(1, i)
+        tiles.append(y.astype(BF16))
     return tiles
 
 
-def split_refs(refs):
-    return tuple(refs[:4]) + (refs[4 : 4 + REACH],) + tuple(refs[4 + REACH :])
-
-
 def middle_kernel(*refs):
-    inputs, (out, own, up), scratch = refs[:-5], refs[-5:-2], refs[-2:]
+    inputs, (acc, out, own, up) = refs[:-4], refs[-4:]
     basis, transfer = inputs[-2:]
-    tiles = combine(*split_refs(inputs), *scratch)
+    tiles = swapped_body(*inputs, acc)
     for i, tile in enumerate(tiles):
         out[:, 128 * i : 128 * (i + 1)] = tile
     lift_tiles(tiles, basis, transfer, own, up)
 
 
 def last_kernel(*refs):
-    inputs, out, scratch = refs[:-3], refs[-3], refs[-2:]
-    for i, tile in enumerate(combine(*split_refs(inputs), *scratch)):
+    inputs, (acc, out) = refs[:-2], refs[-2:]
+    for i, tile in enumerate(swapped_body(*inputs, acc)):
         out[:, 128 * i : 128 * (i + 1)] = tile
 
 
-def call(kernel, kinds, outs, scratch, args, flops, limit=24):
+def call(kernel, kinds, outs, scratch, args, flops, limit=24, aliases=None):
     size = sum(a.size * a.dtype.itemsize for a in args)
     return pl.pallas_call(
         kernel,
@@ -338,6 +363,7 @@
         in_specs=[SPECS[k] for k in kinds],
         out_specs=jax.tree.map(lambda _: VMEM, outs),
         scratch_shapes=scratch,
+        input_output_aliases=aliases or {},
         compiler_params=pltpu.CompilerParams(vmem_limit_bytes=limit * MIB),
         cost_estimate=pl.CostEstimate(flops=int(flops), bytes_accessed=size, transcendentals=0),
     )(*args)
@@ -372,7 +398,7 @@
     dma = pltpu.SemaphoreType.DMA
     own_shape = shape((leaves, 64, 128), BF16)
     out_shape = shape((64, values.shape[0]), BF16)
-    sums_shape = shape((leaves + 1, 64, 128), F32)
+    sums_shape = shape((2, leaves + 1, 64, 128), F32)
     statics = (far_remote, near_remote, parent_remote, basis, transfer)
     held_shapes = [pltpu.VMEM(x.shape, x.dtype) for x in statics]
     table_scratch = [pltpu.VMEM((2, 2 * leaves, 64, 128), BF16)]
@@ -383,7 +409,6 @@
         pltpu.VMEM(far_blocks.shape, BF16),
         pltpu.VMEM(near_blocks.shape, BF16),
     ]
-    combine_scratch = [pltpu.VMEM((leaves + 1, 64, 128), F32)] * 2
     messages = [shape((PAIR_TILES * len(p), 64, 128), BF16) for p in PAIRS]
 
     def crosswise(x):
@@ -412,7 +437,7 @@
                 lean_local_kernel, "sssssaahhhh", sums_shape,
                 local_scratch + [dma((4 + 2 * CHUNKS,))]
                 + [pltpu.VMEM((n, 64, 64), BF16) for n in (CAP0, CAPN)],
-                (*local, far_remote, near_remote), 6e9, 60,
+                (*local, far_remote, near_remote), 6e9, 12,
             )
         else:
             sums, *held = call(
@@ -422,10 +447,14 @@
         arrived, parents, sums = lax.optimization_barrier((arrived, parents, sums))
         swapped = jnp.concatenate([m[MINE:] for m in arrived] + [parents[:, :64]])
         swapped = crosswise(swapped)
-        inputs = (place, far_plan, near_plan, parent_plan, *arrived, parents, swapped, sums, *held)
-        return inputs, asks
-
-    kinds = "ssss" + "v" * (REACH + 8)
+        plans = (place, far_plan, near_plan, parent_plan)
+        sums, total = call(
+            arrived_kernel, "ssss" + "v" * (REACH + 5), [sums_shape, shape((128, 64), F32)], [],
+            (*plans, *arrived, parents, sums, *held[:3]), 2e9, 16, {4 + REACH + 1: 0},
+        )
+        return (*plans, swapped, sums, total, *held), asks
+
+    kinds = "ssss" + "v" * 8
     lifted = (values.T, basis, transfer, far_plan, near_plan)
     own, up = call(
         lift_kernel, "hhhhh", [own_shape, shape((chips, 80, 128), BF16)],
@@ -433,12 +462,14 @@
         60,
     )
     inputs, asks = exchange(own, up, None, False)
-    first, own, up = call(
-        middle_kernel, kinds, [out_shape, own_shape, shape((chips, 64, 128), BF16)],
-        combine_scratch, inputs, 4e9,
+    _, first, own, up = call(
+        middle_kernel, kinds, [sums_shape, out_shape, own_shape, shape((chips, 64, 128), BF16)],
+        [], inputs, 3e9, 16, {5: 0},
     )
     inputs, _ = exchange(own, up, asks, True)
-    second = call(last_kernel, kinds, out_shape, combine_scratch, inputs, 4e9, 16)
+    _, second = call(
+        last_kernel, kinds, [sums_shape, out_shape], [], inputs, 2e9, 16, {5: 0}
+    )
     return first.T, second.T
 
 

time: 73.7 us -> 71.4 us (0.969)
  waiting for transfers between devices: 9.92 us -> 6.77 us
  local copies, waits for them, and re-layouts: 3.1 us -> 5 us
    ppermute x5, waiting for transfers between devices: 4.22 us -> 1.06 us  [crosswise(): return lax.ppermute(x, 'clu', mates(devices))]
    unnamed x47 -> x39, local copies, waits for them, and re-layouts: 2.99 us -> 4.89 us
    pallas_call x7 -> x9, Pallas kernels: 25 us -> 24.3 us  [call(): pl.pallas_call(kernel, out_shape=outs, in_specs=[SPECS[k] for k in kinds]...]
  transfers between devices with their start and end apart: 13 -> 13, of which waited for: 4 -> 3; matrix products, arithmetic and copies ran while one was open for 3% -> 3% of each run, Pallas kernels for 17% -> 20%
where the time goes in v5:
time: 71.4 us; the launch traced here: 70.8 us
  starting transfers between devices  33.4 us (47%)
  Pallas kernels  24.3 us (34%)
  waiting for transfers between devices  6.77 us (9%)
  local copies, waits for them, and re-layouts  5 us (7%)
  between operations  1.12 us (2%)
    pallas_call x9, Pallas kernels, call(): pl.pallas_call(kernel, out_shape=outs, in_specs=[SPECS[k] for k in kinds]...  24.3 us
    ppermute x6, starting transfers between devices, exchange(): lax.ppermute(m, 'clu', outward(devices, d + 1))  20.3 us
    all_to_all x2, starting transfers between devices, exchange(): lax.all_to_all(up, 'clu', 0, 0, tiled=True, axis_index_groups=same_core)  12 us
    all_to_all x2, waiting for transfers between devices, exchange(): lax.all_to_all(up, 'clu', 0, 0, tiled=True, axis_index_groups=same_core)  5.69 us
    unnamed x39, local copies, waits for them, and re-layouts  4.89 us
  transfers between devices with their start and end apart: 13, of which 3 were waited for; matrix products, arithmetic and copies ran while one was open for 3% of the time, Pallas kernels for 20%

profile of v5, /device:TPU:0, one launch (start us, length us, event | category | flops | bytes accessed | tf_op | source)
XLA Modules:
  0.0 70.8 jit_solution(1813644899929628688)
XLA Ops:
  0.6 2.6 %shard_map.140 = (bf16[16,64,128]{2,1,0:T(8,128)(2,1)}, bf16[8,80,128]{2,1,0:T(8,128)(2,1)}) custom-call(bf16[64,1024]{1,0:T(8,128)(2,1)} %bitcast.30, bf16[16,64,64]{2,1,0:T(8,128)(2,1)} %refs_10_.1, bf16[16,64,64]{2,1,0:T(8,128)(2,1)} %refs_11_.1, s32[1,2,72]{2,1,0:T(2,128)} %refs_1_.9, s32[1,2,24]{2,1,0:T(2,128)} %refs_2_.9), custom_call_target="tpu_custom_call" | custom-call | flops 1000000000 | bytes 393984 | tf_op jit(solution)/shard_map/pallas_call | solution.py:360
  3.3 7.3 %all-to-all-start = ((bf16[8,80,128]{2,1,0:T(8,128)(2,1)}), bf16[8,80,128]{2,1,0:T(8,128)(2,1)S(1)}, u32[]{:S(2)}, u32[]{:S(2)}) async-start(bf16[8,80,128]{2,1,0:T(8,128)(2,1)} %get-tuple-element.36), calls=%async_computation | async-start | bytes 327680 | tf_op jit(solution)/shard_map/all_to_all | solution.py:419
  10.6 0.0 collective-permute-start.1
  10.6 1.8 %copy.29 = bf16[1,72,64,64]{3,2,1,0:T(8,128)(2,1)S(1)} copy(bf16[1,72,64,64]{1,3,2,0:T(8,128)(2,1)S(1)} %copy-done.18) | data formatting | bytes 1179648 | tf_op args[10]
  12.5 5.7 %all-to-all-done.refs_7_ = bf16[8,80,128]{2,1,0:T(8,128)(2,1)S(1)} async-done(((bf16[8,80,128]{2,1,0:T(8,128)(2,1)}), bf16[8,80,128]{2,1,0:T(8,128)(2,1)S(1)}, u32[]{:S(2)}, u32[]{:S(2)}) %all-to-all-start) | async-done | bytes 163872 | tf_op jit(solution)/shard_map/all_to_all | solution.py:419
  18.2 0.1 collective-permute-start
  18.3 0.1 pad_add_fusion.place_ref.refs_0_
  18.4 0.0 copy-start.6
  18.4 0.0 copy-start.7
  18.4 0.0 copy-start.11
  18.4 0.0 copy-start.12
  18.4 0.0 copy-start.13
  18.4 0.0 copy-start.14
  18.4 0.0 collective-permute-done.1.mate.refs_6_
  18.5 1.0 %collective-permute-done.mate_asks = s32[8,128]{1,0:T(8,128)S(1)} collective-permute-done((s32[8,128]{1,0:T(8,128)S(1)}, s32[8,128]{1,0:T(8,128)S(1)}, u32[]{:S(2)}, u32[]{:S(2)}) %collective-permute-start) | collective-permute-done | bytes 4128 | tf_op jit(solution)/shard_map/ppermute | solution.py:415
  19.4 1.5 %shard_map.141 = (bf16[16,64,128]{2,1,0:T(8,128)(2,1)S(1)}, bf16[16,64,128]{2,1,0:T(8,128)(2,1)S(1)}, bf16[12,64,128]{2,1,0:T(8,128)(2,1)S(1)}) custom-call(s32[2]{0:T(128)S(1)} %pad_add_fusion.place_ref.refs_0_, s32[8,128]{1,0:T(8,128)S(1)} %fusion.asks, s32[8,128]{1,0:T(8,128)S(1)} %collective-permute-done.mate_asks, bf16[16,64,128]{2,1,0:T(8,128)(2,1)S(1)} %copy-done.8, ...), custom_call_target="tpu_custom_call" | custom-call | flops 2000000000 | bytes 532488 | tf_op jit(solution)/shard_map/pallas_call | solution.py:360
  20.9 2.7 %collective-permute-start.4 = (bf16[12,64,128]{2,1,0:T(8,128)(2,1)S(1)}, bf16[12,64,128]{2,1,0:T(8,128)(2,1)S(1)}, u32[]{:S(2)}, u32[]{:S(2)}) collective-permute-start(bf16[12,64,128]{2,1,0:T(8,128)(2,1)S(1)} %get-tuple-element.41), channel_id=1, source_target_pairs={{0,6},{2,8},{4,10},{6,12},{8,14},{7,1},{9,3},{11,5},{13,7},{15,9},... | collective-permute-start | bytes 589832 | tf_op jit(solution)/shard_map/ppermute | solution.py:430
  23.6 3.2 %collective-permute-start.2 = (bf16[16,64,128]{2,1,0:T(8,128)(2,1)S(1)}, bf16[16,64,128]{2,1,0:T(8,128)(2,1)S(1)}, u32[]{:S(2)}, u32[]{:S(2)}) collective-permute-start(bf16[16,64,128]{2,1,0:T(8,128)(2,1)S(1)} %get-tuple-element.39), channel_id=1, source_target_pairs={{0,2},{2,4},{4,6},{6,8},{8,10},{10,12},{12,14},{3,1},{5,3},{7,5},{... | collective-permute-start | bytes 786440 | tf_op jit(solution)/shard_map/ppermute | solution.py:430
  26.8 2.7 %collective-permute-start.3 = (bf16[16,64,128]{2,1,0:T(8,128)(2,1)S(1)}, bf16[16,64,128]{2,1,0:T(8,128)(2,1)S(1)}, u32[]{:S(2)}, u32[]{:S(2)}) collective-permute-start(bf16[16,64,128]{2,1,0:T(8,128)(2,1)S(1)} %get-tuple-element.40), channel_id=1, source_target_pairs={{0,4},{2,6},{4,8},{6,10},{8,12},{10,14},{5,1},{7,3},{9,5},{11,7},{... | collective-permute-start | bytes 786440 | tf_op jit(solution)/shard_map/ppermute | solution.py:430
  29.6 4.6 %shard_map.142 = (f32[2,17,64,128]{3,2,1,0:T(8,128)S(1)}, bf16[72,64,64]{2,1,0:T(8,128)(2,1)S(1)}, bf16[24,64,64]{2,1,0:T(8,128)(2,1)S(1)}, bf16[32,64,64]{2,1,0...) custom-call(s32[2]{0:T(128)S(1)} %pad_add_fusion.place_ref.refs_0_, ...), custom_call_target="tpu_custom_call" | custom-call | flops 7000000000 | bytes 3933960 | tf_op jit(solution)/shard_map/pallas_call | solution.py:360
  34.2 0.0 copy-start.15
  34.2 0.0 collective-permute-done.4.refs_6_
  34.2 0.0 collective-permute-done.2.refs_4_
  34.3 0.1 pad_maximum_fusion
  34.4 0.6 collective-permute-start.5
  34.9 1.4 %shard_map.143 = (f32[2,17,64,128]{3,2,1,0:T(8,128)S(1)}, f32[128,64]{1,0:T(8,128)S(1)}) custom-call(s32[2]{0:T(128)S(1)} %pad_add_fusion.place_ref.refs_0_, s32[1,2,72]{2,1,0:T(2,128)S(1)} %copy-done.13, s32[1,2,24]{2,1,0:T(2,128)S(1)} %copy-done.14, s32[1,2,32]{2,1,0:T(2,128)S(1)} %copy-done.15, ...), custom_call_target="tpu_custom_call", output_to_operand_aliasing={{0}: (8, {})} | custom-call | flops 2000000000 | bytes 3048456 | tf_op jit(solution)/shard_map/pallas_call | solution.py:360
  36.3 0.1 collective-permute-done.5.refs_4_
  36.4 3.1 %shard_map.144 = (f32[2,17,64,128]{3,2,1,0:T(8,128)S(1)}, bf16[64,1024]{1,0:T(8,128)(2,1)}, bf16[16,64,128]{2,1,0:T(8,128)(2,1)}, bf16[8,64,128]{2,1,0:T(8,128)(2,1)}) custom-call(s32[2]{0:T(128)S(1)} %pad_add_fusion.place_ref.refs_0_, s32[1,2,72]{2,1,0:T(2,128)S(1)} %copy-done.13, s32[1,2,24]{2,1,0:T(2,128)S(1)} %copy-done.14, ...), custom_call_target="tpu_custom_call", output_to_operand_aliasing={{0}: (5, {})} | custom-call | flops 3000000000 | bytes 2917384 | tf_op jit(solution)/shard_map/pallas_call | solution.py:360
  39.5 0.4 collective-permute-start.6
  39.9 4.7 %all-to-all-start.1 = ((bf16[8,64,128]{2,1,0:T(8,128)(2,1)}), bf16[8,64,128]{2,1,0:T(8,128)(2,1)S(1)}, u32[]{:S(2)}, u32[]{:S(2)}) async-start(bf16[8,64,128]{2,1,0:T(8,128)(2,1)} %get-tuple-element.61), calls=%async_computation.1 | async-start | bytes 262144 | tf_op jit(solution)/shard_map/all_to_all | solution.py:419
  44.6 0.0 copy-start.3
  44.6 0.0 collective-permute-done.6.mate.refs_6_
  44.6 2.6 %shard_map.145 = (bf16[16,64,128]{2,1,0:T(8,128)(2,1)}, bf16[16,64,128]{2,1,0:T(8,128)(2,1)}, bf16[12,64,128]{2,1,0:T(8,128)(2,1)}) custom-call(s32[2]{0:T(128)S(1)} %pad_add_fusion.place_ref.refs_0_, s32[8,128]{1,0:T(8,128)S(1)} %fusion.asks, s32[8,128]{1,0:T(8,128)S(1)} %collective-permute-done.mate_asks, ...), custom_call_target="tpu_custom_call" | custom-call | flops 2000000000 | bytes 532488 | tf_op jit(solution)/shard_map/pallas_call | solution.py:360
  47.2 4.8 %collective-permute-start.9 = (bf16[12,64,128]{2,1,0:T(8,128)(2,1)}, bf16[12,64,128]{2,1,0:T(8,128)(2,1)S(1)}, u32[]{:S(2)}, u32[]{:S(2)}) collective-permute-start(bf16[12,64,128]{2,1,0:T(8,128)(2,1)} %get-tuple-element.60), channel_id=1, source_target_pairs={{0,6},{2,8},{4,10},{6,12},{8,14},{7,1},{9,3},{11,5},{13,7},{15,9},... | collective-permute-start | bytes 589832 | tf_op jit(solution)/shard_map/ppermute | solution.py:430
  52.0 3.4 %collective-permute-start.7 = (bf16[16,64,128]{2,1,0:T(8,128)(2,1)}, bf16[16,64,128]{2,1,0:T(8,128)(2,1)S(1)}, u32[]{:S(2)}, u32[]{:S(2)}) collective-permute-start(bf16[16,64,128]{2,1,0:T(8,128)(2,1)} %get-tuple-element.58), channel_id=1, source_target_pairs={{0,2},{2,4},{4,6},{6,8},{8,10},{10,12},{12,14},{3,1},{5,3},{7,5},{... | collective-permute-start | bytes 786440 | tf_op jit(solution)/shard_map/ppermute | solution.py:430
  55.4 3.5 %collective-permute-start.8 = (bf16[16,64,128]{2,1,0:T(8,128)(2,1)}, bf16[16,64,128]{2,1,0:T(8,128)(2,1)S(1)}, u32[]{:S(2)}, u32[]{:S(2)}) collective-permute-start(bf16[16,64,128]{2,1,0:T(8,128)(2,1)} %get-tuple-element.59), channel_id=1, source_target_pairs={{0,4},{2,6},{4,8},{6,10},{8,12},{10,14},{5,1},{7,3},{9,5},{11,7},{... | collective-permute-start | bytes 786440 | tf_op jit(solution)/shard_map/ppermute | solution.py:430
  59.0 0.9 %copy-done.10 = bf16[16,64,128]{2,1,0:T(8,128)(2,1)S(1)} copy-done((bf16[16,64,128]{2,1,0:T(8,128)(2,1)S(1)}, bf16[16,64,128]{2,1,0:T(8,128)(2,1)}, u32[]{:S(2)}) %copy-start.10) | copy-done | bytes 262168
  59.9 4.6 %shard_map.146.refs_8_ = f32[2,17,64,128]{3,2,1,0:T(8,128)S(1)} custom-call(s32[2]{0:T(128)S(1)} %pad_add_fusion.place_ref.refs_0_, s32[8,16]{1,0:T(8,128)S(1)} %bitcast.27, s32[8,16]{1,0:T(8,128)S(1)} %bitcast.29, s32[1,2,72]{2,1,0:T(2,128)S(1)} %copy-done.13, s32[1,2,24]{2,1,0:T(2,128)S(1)} %copy-done.14, ...), custom_call_target="tpu_custom_call" | custom-call | flops 6000000000 | bytes 3409672 | tf_op jit(solution)/shard_map/pallas_call | solution.py:360
  64.6 1.0 %copy-done.16 = f32[2,17,64,128]{3,2,1,0:T(8,128)} copy-done((f32[2,17,64,128]{3,2,1,0:T(8,128)}, f32[2,17,64,128]{3,2,1,0:T(8,128)S(1)}, u32[]{:S(2)}) %copy-start.16) | copy-done | bytes 1114136
  65.6 0.0 all-to-all-done.1.refs_7_
  65.6 0.0 collective-permute-done.9.refs_6_
  65.6 0.0 collective-permute-done.8.refs_5_
  65.7 0.1 pad_maximum_fusion.1
  65.8 0.1 collective-permute-start.10
  65.8 1.0 %copy-done.17 = f32[2,17,64,128]{3,2,1,0:T(8,128)S(1)} copy-done((f32[2,17,64,128]{3,2,1,0:T(8,128)S(1)}, f32[2,17,64,128]{3,2,1,0:T(8,128)}, u32[]{:S(2)}) %copy-start.17) | copy-done | bytes 1114136
  66.9 1.4 %shard_map.147 = (f32[2,17,64,128]{3,2,1,0:T(8,128)S(1)}, f32[128,64]{1,0:T(8,128)S(1)}) custom-call(s32[2]{0:T(128)S(1)} %pad_add_fusion.place_ref.refs_0_, s32[1,2,72]{2,1,0:T(2,128)S(1)} %copy-done.13, s32[1,2,24]{2,1,0:T(2,128)S(1)} %copy-done.14, s32[1,2,32]{2,1,0:T(2,128)S(1)} %copy-done.15, ...), custom_call_target="tpu_custom_call", output_to_operand_aliasing={{0}: (8, {})} | custom-call | flops 2000000000 | bytes 3015688 | tf_op jit(solution)/shard_map/pallas_call | solution.py:360
  68.2 0.0 collective-permute-done.10.refs_4_
  68.2 2.6 %shard_map.148 = (f32[2,17,64,128]{3,2,1,0:T(8,128)S(1)}, bf16[64,1024]{1,0:T(8,128)(2,1)}) custom-call(s32[2]{0:T(128)S(1)} %pad_add_fusion.place_ref.refs_0_, s32[1,2,72]{2,1,0:T(2,128)S(1)} %copy-done.13, s32[1,2,24]{2,1,0:T(2,128)S(1)} %copy-done.14, s32[1,2,32]{2,1,0:T(2,128)S(1)} %copy-done.15, ...), custom_call_target="tpu_custom_call", output_to_operand_aliasing={{0}: (5, {})} | custom-call | flops 2000000000 | bytes 2917384 | tf_op jit(solution)/shard_map/pallas_call | solution.py:360
  (38 shorter events, 0.2 us)
Async XLA Ops:
  0.6 10.0 %copy-start.18 = (bf16[1,72,64,64]{1,3,2,0:T(8,128)(2,1)S(1)}, bf16[1,72,64,64]{1,3,2,0:T(8,128)(2,1)}, u32[]{:S(2)}) copy-start(bf16[1,72,64,64]{1,3,2,0:T(8,128)(2,1)} %param.23) | copy-start | bytes 1769476
  3.3 14.9 %all-to-all-start = ((bf16[8,80,128]{2,1,0:T(8,128)(2,1)}), bf16[8,80,128]{2,1,0:T(8,128)(2,1)S(1)}, u32[]{:S(2)}, u32[]{:S(2)}) async-start(bf16[8,80,128]{2,1,0:T(8,128)(2,1)} %get-tuple-element.36), calls=%async_computation | async-start | bytes 327680 | tf_op jit(solution)/shard_map/all_to_all | solution.py:419
  10.6 7.9 %collective-permute-start.1 = (bf16[16,64,128]{2,1,0:T(8,128)(2,1)}, bf16[16,64,128]{2,1,0:T(8,128)(2,1)S(1)}, u32[]{:S(2)}, u32[]{:S(2)}) collective-permute-start(bf16[16,64,128]{2,1,0:T(8,128)(2,1)} %get-tuple-element.38.own.refs_5_), channel_id=1, source_target_pairs={{0,1},{1,0},{2,3},{3,2},{4,5},{5,4},{6,7},{7,6},{8,9},{9,8},{10,11... | collective-permute-start | bytes 786440 | tf_op jit(solution)/shard_map/ppermute | solution.py:415
  10.6 8.8 %copy-start.8 = (bf16[16,64,128]{2,1,0:T(8,128)(2,1)S(1)}, bf16[16,64,128]{2,1,0:T(8,128)(2,1)}, u32[]{:S(2)}) copy-start(bf16[16,64,128]{2,1,0:T(8,128)(2,1)} %get-tuple-element.38.own.refs_5_) | copy-start | bytes 786436
  18.2 1.2 %collective-permute-start = (s32[8,128]{1,0:T(8,128)S(1)}, s32[8,128]{1,0:T(8,128)S(1)}, u32[]{:S(2)}, u32[]{:S(2)}) collective-permute-start(s32[8,128]{1,0:T(8,128)S(1)} %fusion.asks), channel_id=1, source_target_pairs={{0,1},{1,0},{2,3},{3,2},{4,5},{5,4},{6,7},{7,6},{8,9},{9,8},{10,11... | collective-permute-start | bytes 12296 | tf_op jit(solution)/shard_map/ppermute | solution.py:415
  18.4 11.2 %copy-start = (bf16[16,8,64,64]{3,2,1,0:T(8,128)(2,1)S(1)}, bf16[16,8,64,64]{3,2,1,0:T(8,128)(2,1)}, u32[]{:S(2)}) copy-start(bf16[16,8,64,64]{3,2,1,0:T(8,128)(2,1)} %refs_7_.3) | copy-start | bytes 3145732
  18.4 11.2 %copy-start.2 = (bf16[16,8,64,64]{3,2,1,0:T(8,128)(2,1)S(1)}, bf16[16,8,64,64]{3,2,1,0:T(8,128)(2,1)}, u32[]{:S(2)}) copy-start(bf16[16,8,64,64]{3,2,1,0:T(8,128)(2,1)} %refs_8_.3) | copy-start | bytes 3145732
  18.4 11.2 %copy-start.4 = (bf16[1,32,64,64]{3,2,1,0:T(8,128)(2,1)S(1)}, bf16[1,32,64,64]{3,2,1,0:T(8,128)(2,1)}, u32[]{:S(2)}) copy-start(bf16[1,32,64,64]{3,2,1,0:T(8,128)(2,1)} %param.25) | copy-start | bytes 786436
  18.4 11.2 %copy-start.5 = (bf16[1,24,64,64]{3,2,1,0:T(8,128)(2,1)S(1)}, bf16[1,24,64,64]{3,2,1,0:T(8,128)(2,1)}, u32[]{:S(2)}) copy-start(bf16[1,24,64,64]{3,2,1,0:T(8,128)(2,1)} %param.21) | copy-start | bytes 589828
  18.4 11.2 %copy-start.6 = (bf16[16,64,64]{2,1,0:T(8,128)(2,1)S(1)}, bf16[16,64,64]{2,1,0:T(8,128)(2,1)}, u32[]{:S(2)}) copy-start(bf16[16,64,64]{2,1,0:T(8,128)(2,1)} %refs_10_.1) | copy-start | bytes 393220
  18.4 11.2 %copy-start.7 = (bf16[16,64,64]{2,1,0:T(8,128)(2,1)S(1)}, bf16[16,64,64]{2,1,0:T(8,128)(2,1)}, u32[]{:S(2)}) copy-start(bf16[16,64,64]{2,1,0:T(8,128)(2,1)} %refs_11_.1) | copy-start | bytes 393220
  18.4 11.2 %copy-start.11 = (s32[16,8]{0,1:T(8,128)S(1)}, s32[16,8]{0,1:T(8,128)}, u32[]{:S(2)}) copy-start(s32[16,8]{0,1:T(8,128)} %param.18) | copy-start | bytes 1540
  18.4 11.2 %copy-start.12 = (s32[16,8]{0,1:T(8,128)S(1)}, s32[16,8]{0,1:T(8,128)}, u32[]{:S(2)}) copy-start(s32[16,8]{0,1:T(8,128)} %param.16) | copy-start | bytes 1540
  18.4 11.2 %copy-start.13 = (s32[1,2,72]{2,1,0:T(2,128)S(1)}, s32[1,2,72]{2,1,0:T(2,128)}, u32[]{:S(2)}) copy-start(s32[1,2,72]{2,1,0:T(2,128)} %refs_1_.9) | copy-start | bytes 1732
  18.4 11.2 %copy-start.14 = (s32[1,2,24]{2,1,0:T(2,128)S(1)}, s32[1,2,24]{2,1,0:T(2,128)}, u32[]{:S(2)}) copy-start(s32[1,2,24]{2,1,0:T(2,128)} %refs_2_.9) | copy-start | bytes 580
  20.9 13.3 %collective-permute-start.4 = (bf16[12,64,128]{2,1,0:T(8,128)(2,1)S(1)}, bf16[12,64,128]{2,1,0:T(8,128)(2,1)S(1)}, u32[]{:S(2)}, u32[]{:S(2)}) collective-permute-start(bf16[12,64,128]{2,1,0:T(8,128)(2,1)S(1)} %get-tuple-element.41), channel_id=1, source_target_pairs={{0,6},{2,8},{4,10},{6,12},{8,14},{7,1},{9,3},{11,5},{13,7},{15,9},... | collective-permute-start | bytes 589832 | tf_op jit(solution)/shard_map/ppermute | solution.py:430
  23.6 10.6 %collective-permute-start.2 = (bf16[16,64,128]{2,1,0:T(8,128)(2,1)S(1)}, bf16[16,64,128]{2,1,0:T(8,128)(2,1)S(1)}, u32[]{:S(2)}, u32[]{:S(2)}) collective-permute-start(bf16[16,64,128]{2,1,0:T(8,128)(2,1)S(1)} %get-tuple-element.39), channel_id=1, source_target_pairs={{0,2},{2,4},{4,6},{6,8},{8,10},{10,12},{12,14},{3,1},{5,3},{7,5},{... | collective-permute-start | bytes 786440 | tf_op jit(solution)/shard_map/ppermute | solution.py:430
  26.8 7.4 %collective-permute-start.3 = (bf16[16,64,128]{2,1,0:T(8,128)(2,1)S(1)}, bf16[16,64,128]{2,1,0:T(8,128)(2,1)S(1)}, u32[]{:S(2)}, u32[]{:S(2)}) collective-permute-start(bf16[16,64,128]{2,1,0:T(8,128)(2,1)S(1)} %get-tuple-element.40), channel_id=1, source_target_pairs={{0,4},{2,6},{4,8},{6,10},{8,12},{10,14},{5,1},{7,3},{9,5},{11,7},{... | collective-permute-start | bytes 786440 | tf_op jit(solution)/shard_map/ppermute | solution.py:430
  34.2 0.8 %copy-start.15 = (s32[1,2,32]{2,1,0:T(2,128)S(1)}, s32[1,2,32]{2,1,0:T(2,128)}, u32[]{:S(2)}) copy-start(s32[1,2,32]{2,1,0:T(2,128)} %refs_3_.13) | copy-start | bytes 772
  34.4 2.0 %collective-permute-start.5 = (bf16[28,64,128]{2,1,0:T(8,128)(2,1)S(1)}, bf16[28,64,128]{2,1,0:T(8,128)(2,1)S(1)}, u32[]{:S(2)}, u32[]{:S(2)}) collective-permute-start(bf16[28,64,128]{2,1,0:T(8,128)(2,1)S(1)} %pad_maximum_fusion), channel_id=1, source_target_pairs={{0,1},{1,0},{2,3},{3,2},{4,5},{5,4},{6,7},{7,6},{8,9},{9,8},{10,11... | collective-permute-start | bytes 1376264 | tf_op jit(solution)/shard_map/ppermute | solution.py:415
  39.5 5.1 %collective-permute-start.6 = (bf16[16,64,128]{2,1,0:T(8,128)(2,1)}, bf16[16,64,128]{2,1,0:T(8,128)(2,1)S(1)}, u32[]{:S(2)}, u32[]{:S(2)}) collective-permute-start(bf16[16,64,128]{2,1,0:T(8,128)(2,1)} %get-tuple-element.57.own.refs_5_), channel_id=1, source_target_pairs={{0,1},{1,0},{2,3},{3,2},{4,5},{5,4},{6,7},{7,6},{8,9},{9,8},{10,11... | collective-permute-start | bytes 786440 | tf_op jit(solution)/shard_map/ppermute | solution.py:415
  39.9 25.7 %all-to-all-start.1 = ((bf16[8,64,128]{2,1,0:T(8,128)(2,1)}), bf16[8,64,128]{2,1,0:T(8,128)(2,1)S(1)}, u32[]{:S(2)}, u32[]{:S(2)}) async-start(bf16[8,64,128]{2,1,0:T(8,128)(2,1)} %get-tuple-element.61), calls=%async_computation.1 | async-start | bytes 262144 | tf_op jit(solution)/shard_map/all_to_all | solution.py:419
  44.6 14.4 %copy-start.1 = (bf16[16,8,64,64]{3,2,1,0:T(8,128)(2,1)S(1)}, bf16[16,8,64,64]{3,2,1,0:T(8,128)(2,1)}, u32[]{:S(2)}) copy-start(bf16[16,8,64,64]{3,2,1,0:T(8,128)(2,1)} %refs_7_.3) | copy-start | bytes 3145732
  44.6 14.4 %copy-start.3 = (bf16[16,8,64,64]{3,2,1,0:T(8,128)(2,1)S(1)}, bf16[16,8,64,64]{3,2,1,0:T(8,128)(2,1)}, u32[]{:S(2)}) copy-start(bf16[16,8,64,64]{3,2,1,0:T(8,128)(2,1)} %refs_8_.3) | copy-start | bytes 3145732
  44.6 2.6 %copy-start.9 = (bf16[16,64,128]{2,1,0:T(8,128)(2,1)}, bf16[16,64,128]{2,1,0:T(8,128)(2,1)S(1)}, u32[]{:S(2)}) copy-start(bf16[16,64,128]{2,1,0:T(8,128)(2,1)S(1)} %collective-permute-done.6.mate.refs_6_) | copy-start | bytes 786436
  47.2 18.4 %collective-permute-start.9 = (bf16[12,64,128]{2,1,0:T(8,128)(2,1)}, bf16[12,64,128]{2,1,0:T(8,128)(2,1)S(1)}, u32[]{:S(2)}, u32[]{:S(2)}) collective-permute-start(bf16[12,64,128]{2,1,0:T(8,128)(2,1)} %get-tuple-element.60), channel_id=1, source_target_pairs={{0,6},{2,8},{4,10},{6,12},{8,14},{7,1},{9,3},{11,5},{13,7},{15,9},... | collective-permute-start | bytes 589832 | tf_op jit(solution)/shard_map/ppermute | solution.py:430
  52.0 13.6 %collective-permute-start.7 = (bf16[16,64,128]{2,1,0:T(8,128)(2,1)}, bf16[16,64,128]{2,1,0:T(8,128)(2,1)S(1)}, u32[]{:S(2)}, u32[]{:S(2)}) collective-permute-start(bf16[16,64,128]{2,1,0:T(8,128)(2,1)} %get-tuple-element.58), channel_id=1, source_target_pairs={{0,2},{2,4},{4,6},{6,8},{8,10},{10,12},{12,14},{3,1},{5,3},{7,5},{... | collective-permute-start | bytes 786440 | tf_op jit(solution)/shard_map/ppermute | solution.py:430
  55.4 10.2 %collective-permute-start.8 = (bf16[16,64,128]{2,1,0:T(8,128)(2,1)}, bf16[16,64,128]{2,1,0:T(8,128)(2,1)S(1)}, u32[]{:S(2)}, u32[]{:S(2)}) collective-permute-start(bf16[16,64,128]{2,1,0:T(8,128)(2,1)} %get-tuple-element.59), channel_id=1, source_target_pairs={{0,4},{2,6},{4,8},{6,10},{8,12},{10,14},{5,1},{7,3},{9,5},{11,7},{... | collective-permute-start | bytes 786440 | tf_op jit(solution)/shard_map/ppermute | solution.py:430
  59.0 1.0 %copy-start.10 = (bf16[16,64,128]{2,1,0:T(8,128)(2,1)S(1)}, bf16[16,64,128]{2,1,0:T(8,128)(2,1)}, u32[]{:S(2)}) copy-start(bf16[16,64,128]{2,1,0:T(8,128)(2,1)} %copy-done.9) | copy-start | bytes 786436
  64.6 1.0 %copy-start.16 = (f32[2,17,64,128]{3,2,1,0:T(8,128)}, f32[2,17,64,128]{3,2,1,0:T(8,128)S(1)}, u32[]{:S(2)}) copy-start(f32[2,17,64,128]{3,2,1,0:T(8,128)S(1)} %shard_map.146.refs_8_) | copy-start | bytes 3342340
  65.6 1.2 %copy-start.17 = (f32[2,17,64,128]{3,2,1,0:T(8,128)S(1)}, f32[2,17,64,128]{3,2,1,0:T(8,128)}, u32[]{:S(2)}) copy-start(f32[2,17,64,128]{3,2,1,0:T(8,128)} %copy-done.16) | copy-start | bytes 3342340
  65.8 2.5 %collective-permute-start.10 = (bf16[28,64,128]{2,1,0:T(8,128)(2,1)S(1)}, bf16[28,64,128]{2,1,0:T(8,128)(2,1)S(1)}, u32[]{:S(2)}, u32[]{:S(2)}) collective-permute-start(bf16[28,64,128]{2,1,0:T(8,128)(2,1)S(1)} %pad_maximum_fusion.1), channel_id=1, source_target_pairs={{0,1},{1,0},{2,3},{3,2},{4,5},{5,4},{6,7},{7,6},{8,9},{9,8},{10,11... | collective-permute-start | bytes 1376264 | tf_op jit(solution)/shard_map/ppermute | solution.py:415

commit v6 on v5

--- a/solution.py
+++ b/solution.py
@@ -119,13 +119,26 @@
     return lax.broadcasted_iota(jnp.int32, (64, 128), 1) < 64
 
 
-def pack_kernel(place_ref, asks, mate_asks, own, mate, *refs):
-    outs, table = refs[:REACH], refs[REACH]
+def mate_offset(core):
+    return jnp.where(core == 0, HOPS, HOPS - 1)
+
+
+def pack_kernel(place_ref, asks, mate_asks, far_plan, near_plan, own, mate, *refs):
+    outs, beyond, table = refs[:REACH], refs[REACH], refs[REACH + 1]
     core, chip = place_ref[0], place_ref[1]
     chips = asks.shape[0]
     turn_tables((own, mate), table)
     left = left_mask()
     half = own.shape[0]
+    order = mate_offset(core)
+    for i in range(PAIR_TILES):
+        if i < FAR_TILES:
+            plan, at, base = far_plan, order * CAP0 + 2 * i, half
+        else:
+            plan, at, base = near_plan, order * CAPN + 2 * (i - FAR_TILES), half + half // 2
+        first = jnp.maximum(plan[0, 0, at], 0)
+        second = jnp.maximum(plan[0, 0, at + 1], 0)
+        beyond[i] = pair_of(table, base, first, second, left)
     for step in range(REACH):
         toward = jnp.where(core == 0, -2 * (step + 1), 2 * (step + 1))
         asker = jnp.clip(chip - toward // 2, 0, chips - 1)
@@ -159,8 +172,8 @@
 
 
 def local_body(
-    place_ref, far_list, near_list, far_plan, near_plan, own_in, mate_in, far_in, near_in, out,
-    table, own, mate, far_blocks, near_blocks, sems, far_remote, near_remote, further, lean=False
+    place_ref, far_list, near_list, far_plan, near_plan, own_in, beyond_in, far_in, near_in, out,
+    table, own, beyond, far_blocks, near_blocks, sems, far_remote, near_remote, further, lean=False
 ):
     core = place_ref[0]
     leaves = far_blocks.shape[0]
@@ -169,14 +182,14 @@
     for c in range(CHUNKS):
         rows = pl.ds(c * step, step)
         pairs += [(far_in.at[rows], far_blocks.at[rows]), (near_in.at[rows], near_blocks.at[rows])]
-    order = jnp.where(core == 0, HOPS, HOPS - 1)
+    order = mate_offset(core)
     if lean:
         (far_from, far_to), (near_from, near_to) = further
         further = [
             (far_from.at[pl.ds(order * CAP0, CAP0)], far_to),
             (near_from.at[pl.ds(order * CAPN, CAPN)], near_to),
         ]
-    copies = fetch(pairs + [(mate_in, mate)] + further, sems)
+    copies = fetch(pairs + [(beyond_in, beyond)] + further, sems)
     copies[0].wait()
     turn_tables((own,), table)
     left = left_mask()
@@ -201,19 +214,18 @@
     for copy in copies[1 + 2 * CHUNKS :]:
         copy.wait()
     out[:, leaves] = jnp.zeros((2, 64, 128), F32)
-    for kind, plan, blocks, base, cap in (
-        (0, far_plan, far_remote, 0, CAP0),
-        (1, near_plan, near_remote, half // 2, CAPN),
-    ):
-        for c in range(cap):
-            slot = order * cap + c
-            target = plan[0, 1, slot]
-            where = jnp.where(target < 0, leaves, target)
-            leaf = jnp.maximum(plan[0, 0, slot], 0)
-            tile = mate[base + leaf // 2]
-            x = jnp.where(leaf % 2 == 0, tile[:, :64], tile[:, 64:])
-            w = blocks[c if lean else slot]
-            out[kind, where, :, 0:64] = out[kind, where, :, 0:64] + nt(x, w)
+    for i in range(PAIR_TILES):
+        if i < FAR_TILES:
+            kind, plan, blocks, at, cap = 0, far_plan, far_remote, 2 * i, CAP0
+        else:
+            kind, plan, blocks, at, cap = 1, near_plan, near_remote, 2 * (i - FAR_TILES), CAPN
+        slot = order * cap + at
+        first = at if lean else slot
+        y = nt(beyond[i], diagonal(blocks[first], blocks[first + 1]))
+        t0, t1 = plan[0, 1, slot], plan[0, 1, slot + 1]
+        t0, t1 = jnp.where(t0 < 0, leaves, t0), jnp.where(t1 < 0, leaves, t1)
+        out[kind, t0, :, 0:64] = out[kind, t0, :, 0:64] + y[:, 0:64]
+        out[kind, t1, :, 64:128] = out[kind, t1, :, 64:128] + y[:, 64:128]
 
 
 def local_kernel(*refs):
@@ -397,6 +409,7 @@
     shape = jax.ShapeDtypeStruct
     dma = pltpu.SemaphoreType.DMA
     own_shape = shape((leaves, 64, 128), BF16)
+    beyond_shape = shape((PAIR_TILES, 64, 128), BF16)
     out_shape = shape((64, values.shape[0]), BF16)
     sums_shape = shape((2, leaves + 1, 64, 128), F32)
     statics = (far_remote, near_remote, parent_remote, basis, transfer)
@@ -405,7 +418,7 @@
     local_scratch = [
         pltpu.VMEM((2, leaves, 64, 128), BF16),
         pltpu.VMEM(own_shape.shape, BF16),
-        pltpu.VMEM(own_shape.shape, BF16),
+        pltpu.VMEM(beyond_shape.shape, BF16),
         pltpu.VMEM(far_blocks.shape, BF16),
         pltpu.VMEM(near_blocks.shape, BF16),
     ]
@@ -423,13 +436,14 @@
             statics = (far_remote, *statics[1:])
             asks = parents[:, 64, :].astype(jnp.int32)
             asks = (asks, crosswise(asks))
-        packed = call(
-            pack_kernel, "sssvv", messages, table_scratch, (place, *asks, own, mate), 2e9
+        *packed, beyond = call(
+            pack_kernel, "sssssvv", [*messages, beyond_shape], table_scratch,
+            (place, *asks, far_plan, near_plan, own, mate), 2e9,
         )
         arrived = [
             lax.ppermute(m, "clu", outward(devices, d + 1)) for d, m in enumerate(packed)
         ]
-        local = (place, far_list, near_list, far_plan, near_plan, own, mate, far_blocks,
+        local = (place, far_list, near_list, far_plan, near_plan, own, beyond, far_blocks,
                  near_blocks)
         if last:
             held = statics

time: 71.4 us -> 70.5 us (0.987)
  local copies, waits for them, and re-layouts: 5 us -> 4.04 us
    unnamed x39 -> x35, local copies, waits for them, and re-layouts: 4.89 us -> 3.93 us
  transfers between devices with their start and end apart: 13 -> 13, of which waited for: 3 -> 3; matrix products, arithmetic and copies ran while one was open for 3% -> 3% of each run, Pallas kernels for 20% -> 21%
where the time goes in v6:
time: 70.5 us; the launch traced here: 70 us
  starting transfers between devices  33.4 us (47%)
  Pallas kernels  24.5 us (35%)
  waiting for transfers between devices  6.76 us (10%)
  local copies, waits for them, and re-layouts  4.04 us (6%)
  between operations  1.09 us (2%)
    pallas_call x9, Pallas kernels, call(): pl.pallas_call(kernel, out_shape=outs, in_specs=[SPECS[k] for k in kinds]...  24.5 us
    ppermute x6, starting transfers between devices, exchange(): lax.ppermute(m, 'clu', outward(devices, d + 1))  20.3 us
    all_to_all x2, starting transfers between devices, exchange(): lax.all_to_all(up, 'clu', 0, 0, tiled=True, axis_index_groups=same_core)  12 us
    all_to_all x2, waiting for transfers between devices, exchange(): lax.all_to_all(up, 'clu', 0, 0, tiled=True, axis_index_groups=same_core)  5.67 us
    unnamed x35, local copies, waits for them, and re-layouts  3.93 us
  transfers between devices with their start and end apart: 13, of which 3 were waited for; matrix products, arithmetic and copies ran while one was open for 3% of the time, Pallas kernels for 21%

profile of v6, /device:TPU:0, one launch (start us, length us, event | category | flops | bytes accessed | tf_op | source)
XLA Modules:
  0.0 70.0 jit_solution(8293437475338033614)
XLA Ops:
  0.6 2.6 %shard_map.140 = (bf16[16,64,128]{2,1,0:T(8,128)(2,1)}, bf16[8,80,128]{2,1,0:T(8,128)(2,1)}) custom-call(bf16[64,1024]{1,0:T(8,128)(2,1)} %bitcast.30, bf16[16,64,64]{2,1,0:T(8,128)(2,1)} %refs_10_.1, bf16[16,64,64]{2,1,0:T(8,128)(2,1)} %refs_11_.1, s32[1,2,72]{2,1,0:T(2,128)} %refs_1_.9, s32[1,2,24]{2,1,0:T(2,128)} %refs_2_.9), custom_call_target="tpu_custom_call" | custom-call | flops 1000000000 | bytes 393984 | tf_op jit(solution)/shard_map/pallas_call | solution.py:372
  3.3 7.3 %all-to-all-start = ((bf16[8,80,128]{2,1,0:T(8,128)(2,1)}), bf16[8,80,128]{2,1,0:T(8,128)(2,1)S(1)}, u32[]{:S(2)}, u32[]{:S(2)}) async-start(bf16[8,80,128]{2,1,0:T(8,128)(2,1)} %get-tuple-element.38), calls=%async_computation | async-start | bytes 327680 | tf_op jit(solution)/shard_map/all_to_all | solution.py:432
  10.6 0.0 collective-permute-start.1
  10.6 0.0 copy-start.11
  10.6 0.0 copy-start.12
  10.6 1.8 %copy.29 = bf16[1,72,64,64]{3,2,1,0:T(8,128)(2,1)S(1)} copy(bf16[1,72,64,64]{1,3,2,0:T(8,128)(2,1)S(1)} %copy-done.16) | data formatting | bytes 1179648 | tf_op args[10]
  12.5 5.7 %all-to-all-done.refs_7_ = bf16[8,80,128]{2,1,0:T(8,128)(2,1)S(1)} async-done(((bf16[8,80,128]{2,1,0:T(8,128)(2,1)}), bf16[8,80,128]{2,1,0:T(8,128)(2,1)S(1)}, u32[]{:S(2)}, u32[]{:S(2)}) %all-to-all-start) | async-done | bytes 163872 | tf_op jit(solution)/shard_map/all_to_all | solution.py:432
  18.2 0.1 collective-permute-start
  18.3 0.1 pad_add_fusion.place_ref.refs_0_
  18.4 0.0 copy-start.6
  18.4 0.0 copy-start.7
  18.4 0.0 copy-start.9
  18.4 0.0 copy-start.10
  18.4 0.0 collective-permute-done.1.mate
  18.4 1.0 %collective-permute-done.mate_asks = s32[8,128]{1,0:T(8,128)S(1)} collective-permute-done((s32[8,128]{1,0:T(8,128)S(1)}, s32[8,128]{1,0:T(8,128)S(1)}, u32[]{:S(2)}, u32[]{:S(2)}) %collective-permute-start) | collective-permute-done | bytes 4128 | tf_op jit(solution)/shard_map/ppermute | solution.py:428
  19.4 1.5 %shard_map.141 = (bf16[16,64,128]{2,1,0:T(8,128)(2,1)S(1)}, bf16[16,64,128]{2,1,0:T(8,128)(2,1)S(1)}, bf16[12,64,128]{2,1,0:T(8,128)(2,1)S(1)}, bf16[4,64,128]{2,1,0:T(8,128)(2,1)S(1)}) custom-call(s32[2]{0:T(128)S(1)} %pad_add_fusion.place_ref.refs_0_, s32[8,128]{1,0:T(8,128)S(1)} %fusion.asks, s32[8,128]{1,0:T(8,128)S(1)} %collective-permute-done.mate_asks, ...), custom_call_target="tpu_custom_call" | custom-call | flops 2000000000 | bytes 533256 | tf_op jit(solution)/shard_map/pallas_call | solution.py:372
  21.0 2.7 %collective-permute-start.4 = (bf16[12,64,128]{2,1,0:T(8,128)(2,1)S(1)}, bf16[12,64,128]{2,1,0:T(8,128)(2,1)S(1)}, u32[]{:S(2)}, u32[]{:S(2)}) collective-permute-start(bf16[12,64,128]{2,1,0:T(8,128)(2,1)S(1)} %get-tuple-element.43), channel_id=1, source_target_pairs={{0,6},{2,8},{4,10},{6,12},{8,14},{7,1},{9,3},{11,5},{13,7},{15,9},... | collective-permute-start | bytes 589832 | tf_op jit(solution)/shard_map/ppermute | solution.py:444
  23.7 3.2 %collective-permute-start.2 = (bf16[16,64,128]{2,1,0:T(8,128)(2,1)S(1)}, bf16[16,64,128]{2,1,0:T(8,128)(2,1)S(1)}, u32[]{:S(2)}, u32[]{:S(2)}) collective-permute-start(bf16[16,64,128]{2,1,0:T(8,128)(2,1)S(1)} %get-tuple-element.41), channel_id=1, source_target_pairs={{0,2},{2,4},{4,6},{6,8},{8,10},{10,12},{12,14},{3,1},{5,3},{7,5},{... | collective-permute-start | bytes 786440 | tf_op jit(solution)/shard_map/ppermute | solution.py:444
  26.9 2.7 %collective-permute-start.3 = (bf16[16,64,128]{2,1,0:T(8,128)(2,1)S(1)}, bf16[16,64,128]{2,1,0:T(8,128)(2,1)S(1)}, u32[]{:S(2)}, u32[]{:S(2)}) collective-permute-start(bf16[16,64,128]{2,1,0:T(8,128)(2,1)S(1)} %get-tuple-element.42), channel_id=1, source_target_pairs={{0,4},{2,6},{4,8},{6,10},{8,12},{10,14},{5,1},{7,3},{9,5},{11,7},{... | collective-permute-start | bytes 786440 | tf_op jit(solution)/shard_map/ppermute | solution.py:444
  29.7 4.6 %shard_map.142 = (f32[2,17,64,128]{3,2,1,0:T(8,128)S(1)}, bf16[72,64,64]{2,1,0:T(8,128)(2,1)S(1)}, bf16[24,64,64]{2,1,0:T(8,128)(2,1)S(1)}, bf16[32,64,64]{2,1,0...) custom-call(s32[2]{0:T(128)S(1)} %pad_add_fusion.place_ref.refs_0_, ...), custom_call_target="tpu_custom_call" | custom-call | flops 7000000000 | bytes 3737352 | tf_op jit(solution)/shard_map/pallas_call | solution.py:372
  34.3 0.0 copy-start.13
  34.3 0.0 collective-permute-done.4.refs_6_
  34.4 0.0 collective-permute-done.3.refs_5_
  34.4 0.1 pad_maximum_fusion
  34.5 0.5 collective-permute-start.5
  35.0 1.4 %shard_map.143 = (f32[2,17,64,128]{3,2,1,0:T(8,128)S(1)}, f32[128,64]{1,0:T(8,128)S(1)}) custom-call(s32[2]{0:T(128)S(1)} %pad_add_fusion.place_ref.refs_0_, s32[1,2,72]{2,1,0:T(2,128)S(1)} %copy-done.11, s32[1,2,24]{2,1,0:T(2,128)S(1)} %copy-done.12, s32[1,2,32]{2,1,0:T(2,128)S(1)} %copy-done.13, ...), custom_call_target="tpu_custom_call", output_to_operand_aliasing={{0}: (8, {})} | custom-call | flops 2000000000 | bytes 3048456 | tf_op jit(solution)/shard_map/pallas_call | solution.py:372
  36.4 0.1 collective-permute-done.5.refs_4_
  36.5 3.1 %shard_map.144 = (f32[2,17,64,128]{3,2,1,0:T(8,128)S(1)}, bf16[64,1024]{1,0:T(8,128)(2,1)}, bf16[16,64,128]{2,1,0:T(8,128)(2,1)}, bf16[8,64,128]{2,1,0:T(8,128)(2,1)}) custom-call(s32[2]{0:T(128)S(1)} %pad_add_fusion.place_ref.refs_0_, s32[1,2,72]{2,1,0:T(2,128)S(1)} %copy-done.11, s32[1,2,24]{2,1,0:T(2,128)S(1)} %copy-done.12, ...), custom_call_target="tpu_custom_call", output_to_operand_aliasing={{0}: (5, {})} | custom-call | flops 3000000000 | bytes 2917384 | tf_op jit(solution)/shard_map/pallas_call | solution.py:372
  39.6 0.4 collective-permute-start.6
  40.0 4.7 %all-to-all-start.1 = ((bf16[8,64,128]{2,1,0:T(8,128)(2,1)}), bf16[8,64,128]{2,1,0:T(8,128)(2,1)S(1)}, u32[]{:S(2)}, u32[]{:S(2)}) async-start(bf16[8,64,128]{2,1,0:T(8,128)(2,1)} %get-tuple-element.64), calls=%async_computation.1 | async-start | bytes 262144 | tf_op jit(solution)/shard_map/all_to_all | solution.py:432
  44.7 0.0 copy-start.3
  44.7 0.0 collective-permute-done.6.mate
  44.7 2.6 %shard_map.145 = (bf16[16,64,128]{2,1,0:T(8,128)(2,1)}, bf16[16,64,128]{2,1,0:T(8,128)(2,1)}, bf16[12,64,128]{2,1,0:T(8,128)(2,1)}, bf16[4,64,128]{2,1,0:T(8,128)(2,1)S(1)}) custom-call(s32[2]{0:T(128)S(1)} %pad_add_fusion.place_ref.refs_0_, s32[8,128]{1,0:T(8,128)S(1)} %fusion.asks, s32[8,128]{1,0:T(8,128)S(1)} %collective-permute-done.mate_asks, ...), custom_call_target="tpu_custom_call" | custom-call | flops 2000000000 | bytes 533256 | tf_op jit(solution)/shard_map/pallas_call | solution.py:372
  47.4 4.8 %collective-permute-start.9 = (bf16[12,64,128]{2,1,0:T(8,128)(2,1)}, bf16[12,64,128]{2,1,0:T(8,128)(2,1)S(1)}, u32[]{:S(2)}, u32[]{:S(2)}) collective-permute-start(bf16[12,64,128]{2,1,0:T(8,128)(2,1)} %get-tuple-element.63), channel_id=1, source_target_pairs={{0,6},{2,8},{4,10},{6,12},{8,14},{7,1},{9,3},{11,5},{13,7},{15,9},... | collective-permute-start | bytes 589832 | tf_op jit(solution)/shard_map/ppermute | solution.py:444
  52.2 3.4 %collective-permute-start.7 = (bf16[16,64,128]{2,1,0:T(8,128)(2,1)}, bf16[16,64,128]{2,1,0:T(8,128)(2,1)S(1)}, u32[]{:S(2)}, u32[]{:S(2)}) collective-permute-start(bf16[16,64,128]{2,1,0:T(8,128)(2,1)} %get-tuple-element.61), channel_id=1, source_target_pairs={{0,2},{2,4},{4,6},{6,8},{8,10},{10,12},{12,14},{3,1},{5,3},{7,5},{... | collective-permute-start | bytes 786440 | tf_op jit(solution)/shard_map/ppermute | solution.py:444
  55.6 3.5 %collective-permute-start.8 = (bf16[16,64,128]{2,1,0:T(8,128)(2,1)}, bf16[16,64,128]{2,1,0:T(8,128)(2,1)S(1)}, u32[]{:S(2)}, u32[]{:S(2)}) collective-permute-start(bf16[16,64,128]{2,1,0:T(8,128)(2,1)} %get-tuple-element.62), channel_id=1, source_target_pairs={{0,4},{2,6},{4,8},{6,10},{8,12},{10,14},{5,1},{7,3},{9,5},{11,7},{... | collective-permute-start | bytes 786440 | tf_op jit(solution)/shard_map/ppermute | solution.py:444
  59.1 4.6 %shard_map.146.refs_8_ = f32[2,17,64,128]{3,2,1,0:T(8,128)S(1)} custom-call(s32[2]{0:T(128)S(1)} %pad_add_fusion.place_ref.refs_0_, s32[8,16]{1,0:T(8,128)S(1)} %bitcast.27, s32[8,16]{1,0:T(8,128)S(1)} %bitcast.29, s32[1,2,72]{2,1,0:T(2,128)S(1)} %copy-done.11, s32[1,2,24]{2,1,0:T(2,128)S(1)} %copy-done.12, ...), custom_call_target="tpu_custom_call" | custom-call | flops 6000000000 | bytes 3213064 | tf_op jit(solution)/shard_map/pallas_call | solution.py:372
  63.8 1.0 %copy-done.14 = f32[2,17,64,128]{3,2,1,0:T(8,128)} copy-done((f32[2,17,64,128]{3,2,1,0:T(8,128)}, f32[2,17,64,128]{3,2,1,0:T(8,128)S(1)}, u32[]{:S(2)}) %copy-start.14) | copy-done | bytes 1114136
  64.8 0.0 all-to-all-done.1.refs_7_
  64.8 0.0 collective-permute-done.9.refs_6_
  64.8 0.0 collective-permute-done.7.refs_4_
  64.8 0.0 collective-permute-done.8.refs_5_
  64.9 0.1 pad_maximum_fusion.1
  65.0 0.1 collective-permute-start.10
  65.0 1.0 %copy-done.15 = f32[2,17,64,128]{3,2,1,0:T(8,128)S(1)} copy-done((f32[2,17,64,128]{3,2,1,0:T(8,128)S(1)}, f32[2,17,64,128]{3,2,1,0:T(8,128)}, u32[]{:S(2)}) %copy-start.15) | copy-done | bytes 1114136
  66.1 1.4 %shard_map.147 = (f32[2,17,64,128]{3,2,1,0:T(8,128)S(1)}, f32[128,64]{1,0:T(8,128)S(1)}) custom-call(s32[2]{0:T(128)S(1)} %pad_add_fusion.place_ref.refs_0_, s32[1,2,72]{2,1,0:T(2,128)S(1)} %copy-done.11, s32[1,2,24]{2,1,0:T(2,128)S(1)} %copy-done.12, s32[1,2,32]{2,1,0:T(2,128)S(1)} %copy-done.13, ...), custom_call_target="tpu_custom_call", output_to_operand_aliasing={{0}: (8, {})} | custom-call | flops 2000000000 | bytes 3015688 | tf_op jit(solution)/shard_map/pallas_call | solution.py:372
  67.4 0.0 collective-permute-done.10.refs_4_
  67.4 2.6 %shard_map.148 = (f32[2,17,64,128]{3,2,1,0:T(8,128)S(1)}, bf16[64,1024]{1,0:T(8,128)(2,1)}) custom-call(s32[2]{0:T(128)S(1)} %pad_add_fusion.place_ref.refs_0_, s32[1,2,72]{2,1,0:T(2,128)S(1)} %copy-done.11, s32[1,2,24]{2,1,0:T(2,128)S(1)} %copy-done.12, s32[1,2,32]{2,1,0:T(2,128)S(1)} %copy-done.13, ...), custom_call_target="tpu_custom_call", output_to_operand_aliasing={{0}: (5, {})} | custom-call | flops 2000000000 | bytes 2917384 | tf_op jit(solution)/shard_map/pallas_call | solution.py:372
  (34 shorter events, 0.2 us)
Async XLA Ops:
  0.6 10.0 %copy-start.16 = (bf16[1,72,64,64]{1,3,2,0:T(8,128)(2,1)S(1)}, bf16[1,72,64,64]{1,3,2,0:T(8,128)(2,1)}, u32[]{:S(2)}) copy-start(bf16[1,72,64,64]{1,3,2,0:T(8,128)(2,1)} %param.23) | copy-start | bytes 1769476
  3.3 14.9 %all-to-all-start = ((bf16[8,80,128]{2,1,0:T(8,128)(2,1)}), bf16[8,80,128]{2,1,0:T(8,128)(2,1)S(1)}, u32[]{:S(2)}, u32[]{:S(2)}) async-start(bf16[8,80,128]{2,1,0:T(8,128)(2,1)} %get-tuple-element.38), calls=%async_computation | async-start | bytes 327680 | tf_op jit(solution)/shard_map/all_to_all | solution.py:432
  10.6 7.8 %collective-permute-start.1 = (bf16[16,64,128]{2,1,0:T(8,128)(2,1)}, bf16[16,64,128]{2,1,0:T(8,128)(2,1)S(1)}, u32[]{:S(2)}, u32[]{:S(2)}) collective-permute-start(bf16[16,64,128]{2,1,0:T(8,128)(2,1)} %get-tuple-element.40.own.refs_5_), channel_id=1, source_target_pairs={{0,1},{1,0},{2,3},{3,2},{4,5},{5,4},{6,7},{7,6},{8,9},{9,8},{10,11... | collective-permute-start | bytes 786440 | tf_op jit(solution)/shard_map/ppermute | solution.py:428
  10.6 8.8 %copy-start.8 = (bf16[16,64,128]{2,1,0:T(8,128)(2,1)S(1)}, bf16[16,64,128]{2,1,0:T(8,128)(2,1)}, u32[]{:S(2)}) copy-start(bf16[16,64,128]{2,1,0:T(8,128)(2,1)} %get-tuple-element.40.own.refs_5_) | copy-start | bytes 786436
  10.6 8.8 %copy-start.11 = (s32[1,2,72]{2,1,0:T(2,128)S(1)}, s32[1,2,72]{2,1,0:T(2,128)}, u32[]{:S(2)}) copy-start(s32[1,2,72]{2,1,0:T(2,128)} %refs_1_.9) | copy-start | bytes 1732
  10.6 8.8 %copy-start.12 = (s32[1,2,24]{2,1,0:T(2,128)S(1)}, s32[1,2,24]{2,1,0:T(2,128)}, u32[]{:S(2)}) copy-start(s32[1,2,24]{2,1,0:T(2,128)} %refs_2_.9) | copy-start | bytes 580
  18.2 1.2 %collective-permute-start = (s32[8,128]{1,0:T(8,128)S(1)}, s32[8,128]{1,0:T(8,128)S(1)}, u32[]{:S(2)}, u32[]{:S(2)}) collective-permute-start(s32[8,128]{1,0:T(8,128)S(1)} %fusion.asks), channel_id=1, source_target_pairs={{0,1},{1,0},{2,3},{3,2},{4,5},{5,4},{6,7},{7,6},{8,9},{9,8},{10,11... | collective-permute-start | bytes 12296 | tf_op jit(solution)/shard_map/ppermute | solution.py:428
  18.4 11.3 %copy-start = (bf16[16,8,64,64]{3,2,1,0:T(8,128)(2,1)S(1)}, bf16[16,8,64,64]{3,2,1,0:T(8,128)(2,1)}, u32[]{:S(2)}) copy-start(bf16[16,8,64,64]{3,2,1,0:T(8,128)(2,1)} %refs_7_.3) | copy-start | bytes 3145732
  18.4 11.3 %copy-start.2 = (bf16[16,8,64,64]{3,2,1,0:T(8,128)(2,1)S(1)}, bf16[16,8,64,64]{3,2,1,0:T(8,128)(2,1)}, u32[]{:S(2)}) copy-start(bf16[16,8,64,64]{3,2,1,0:T(8,128)(2,1)} %refs_8_.3) | copy-start | bytes 3145732
  18.4 11.3 %copy-start.4 = (bf16[1,32,64,64]{3,2,1,0:T(8,128)(2,1)S(1)}, bf16[1,32,64,64]{3,2,1,0:T(8,128)(2,1)}, u32[]{:S(2)}) copy-start(bf16[1,32,64,64]{3,2,1,0:T(8,128)(2,1)} %param.25) | copy-start | bytes 786436
  18.4 11.3 %copy-start.5 = (bf16[1,24,64,64]{3,2,1,0:T(8,128)(2,1)S(1)}, bf16[1,24,64,64]{3,2,1,0:T(8,128)(2,1)}, u32[]{:S(2)}) copy-start(bf16[1,24,64,64]{3,2,1,0:T(8,128)(2,1)} %param.21) | copy-start | bytes 589828
  18.4 11.3 %copy-start.6 = (bf16[16,64,64]{2,1,0:T(8,128)(2,1)S(1)}, bf16[16,64,64]{2,1,0:T(8,128)(2,1)}, u32[]{:S(2)}) copy-start(bf16[16,64,64]{2,1,0:T(8,128)(2,1)} %refs_10_.1) | copy-start | bytes 393220
  18.4 11.3 %copy-start.7 = (bf16[16,64,64]{2,1,0:T(8,128)(2,1)S(1)}, bf16[16,64,64]{2,1,0:T(8,128)(2,1)}, u32[]{:S(2)}) copy-start(bf16[16,64,64]{2,1,0:T(8,128)(2,1)} %refs_11_.1) | copy-start | bytes 393220
  18.4 11.3 %copy-start.9 = (s32[16,8]{0,1:T(8,128)S(1)}, s32[16,8]{0,1:T(8,128)}, u32[]{:S(2)}) copy-start(s32[16,8]{0,1:T(8,128)} %param.18) | copy-start | bytes 1540
  18.4 11.3 %copy-start.10 = (s32[16,8]{0,1:T(8,128)S(1)}, s32[16,8]{0,1:T(8,128)}, u32[]{:S(2)}) copy-start(s32[16,8]{0,1:T(8,128)} %param.16) | copy-start | bytes 1540
  21.0 13.3 %collective-permute-start.4 = (bf16[12,64,128]{2,1,0:T(8,128)(2,1)S(1)}, bf16[12,64,128]{2,1,0:T(8,128)(2,1)S(1)}, u32[]{:S(2)}, u32[]{:S(2)}) collective-permute-start(bf16[12,64,128]{2,1,0:T(8,128)(2,1)S(1)} %get-tuple-element.43), channel_id=1, source_target_pairs={{0,6},{2,8},{4,10},{6,12},{8,14},{7,1},{9,3},{11,5},{13,7},{15,9},... | collective-permute-start | bytes 589832 | tf_op jit(solution)/shard_map/ppermute | solution.py:444
  23.7 10.7 %collective-permute-start.2 = (bf16[16,64,128]{2,1,0:T(8,128)(2,1)S(1)}, bf16[16,64,128]{2,1,0:T(8,128)(2,1)S(1)}, u32[]{:S(2)}, u32[]{:S(2)}) collective-permute-start(bf16[16,64,128]{2,1,0:T(8,128)(2,1)S(1)} %get-tuple-element.41), channel_id=1, source_target_pairs={{0,2},{2,4},{4,6},{6,8},{8,10},{10,12},{12,14},{3,1},{5,3},{7,5},{... | collective-permute-start | bytes 786440 | tf_op jit(solution)/shard_map/ppermute | solution.py:444
  26.9 7.5 %collective-permute-start.3 = (bf16[16,64,128]{2,1,0:T(8,128)(2,1)S(1)}, bf16[16,64,128]{2,1,0:T(8,128)(2,1)S(1)}, u32[]{:S(2)}, u32[]{:S(2)}) collective-permute-start(bf16[16,64,128]{2,1,0:T(8,128)(2,1)S(1)} %get-tuple-element.42), channel_id=1, source_target_pairs={{0,4},{2,6},{4,8},{6,10},{8,12},{10,14},{5,1},{7,3},{9,5},{11,7},{... | collective-permute-start | bytes 786440 | tf_op jit(solution)/shard_map/ppermute | solution.py:444
  34.3 0.7 copy-start.13
  34.5 2.0 %collective-permute-start.5 = (bf16[28,64,128]{2,1,0:T(8,128)(2,1)S(1)}, bf16[28,64,128]{2,1,0:T(8,128)(2,1)S(1)}, u32[]{:S(2)}, u32[]{:S(2)}) collective-permute-start(bf16[28,64,128]{2,1,0:T(8,128)(2,1)S(1)} %pad_maximum_fusion), channel_id=1, source_target_pairs={{0,1},{1,0},{2,3},{3,2},{4,5},{5,4},{6,7},{7,6},{8,9},{9,8},{10,11... | collective-permute-start | bytes 1376264 | tf_op jit(solution)/shard_map/ppermute | solution.py:428
  39.6 5.1 %collective-permute-start.6 = (bf16[16,64,128]{2,1,0:T(8,128)(2,1)}, bf16[16,64,128]{2,1,0:T(8,128)(2,1)S(1)}, u32[]{:S(2)}, u32[]{:S(2)}) collective-permute-start(bf16[16,64,128]{2,1,0:T(8,128)(2,1)} %get-tuple-element.60.own.refs_5_), channel_id=1, source_target_pairs={{0,1},{1,0},{2,3},{3,2},{4,5},{5,4},{6,7},{7,6},{8,9},{9,8},{10,11... | collective-permute-start | bytes 786440 | tf_op jit(solution)/shard_map/ppermute | solution.py:428
  40.0 24.8 %all-to-all-start.1 = ((bf16[8,64,128]{2,1,0:T(8,128)(2,1)}), bf16[8,64,128]{2,1,0:T(8,128)(2,1)S(1)}, u32[]{:S(2)}, u32[]{:S(2)}) async-start(bf16[8,64,128]{2,1,0:T(8,128)(2,1)} %get-tuple-element.64), calls=%async_computation.1 | async-start | bytes 262144 | tf_op jit(solution)/shard_map/all_to_all | solution.py:432
  44.7 14.4 %copy-start.1 = (bf16[16,8,64,64]{3,2,1,0:T(8,128)(2,1)S(1)}, bf16[16,8,64,64]{3,2,1,0:T(8,128)(2,1)}, u32[]{:S(2)}) copy-start(bf16[16,8,64,64]{3,2,1,0:T(8,128)(2,1)} %refs_7_.3) | copy-start | bytes 3145732
  44.7 14.4 %copy-start.3 = (bf16[16,8,64,64]{3,2,1,0:T(8,128)(2,1)S(1)}, bf16[16,8,64,64]{3,2,1,0:T(8,128)(2,1)}, u32[]{:S(2)}) copy-start(bf16[16,8,64,64]{3,2,1,0:T(8,128)(2,1)} %refs_8_.3) | copy-start | bytes 3145732
  47.4 17.4 %collective-permute-start.9 = (bf16[12,64,128]{2,1,0:T(8,128)(2,1)}, bf16[12,64,128]{2,1,0:T(8,128)(2,1)S(1)}, u32[]{:S(2)}, u32[]{:S(2)}) collective-permute-start(bf16[12,64,128]{2,1,0:T(8,128)(2,1)} %get-tuple-element.63), channel_id=1, source_target_pairs={{0,6},{2,8},{4,10},{6,12},{8,14},{7,1},{9,3},{11,5},{13,7},{15,9},... | collective-permute-start | bytes 589832 | tf_op jit(solution)/shard_map/ppermute | solution.py:444
  52.2 12.6 %collective-permute-start.7 = (bf16[16,64,128]{2,1,0:T(8,128)(2,1)}, bf16[16,64,128]{2,1,0:T(8,128)(2,1)S(1)}, u32[]{:S(2)}, u32[]{:S(2)}) collective-permute-start(bf16[16,64,128]{2,1,0:T(8,128)(2,1)} %get-tuple-element.61), channel_id=1, source_target_pairs={{0,2},{2,4},{4,6},{6,8},{8,10},{10,12},{12,14},{3,1},{5,3},{7,5},{... | collective-permute-start | bytes 786440 | tf_op jit(solution)/shard_map/ppermute | solution.py:444
  55.6 9.3 %collective-permute-start.8 = (bf16[16,64,128]{2,1,0:T(8,128)(2,1)}, bf16[16,64,128]{2,1,0:T(8,128)(2,1)S(1)}, u32[]{:S(2)}, u32[]{:S(2)}) collective-permute-start(bf16[16,64,128]{2,1,0:T(8,128)(2,1)} %get-tuple-element.62), channel_id=1, source_target_pairs={{0,4},{2,6},{4,8},{6,10},{8,12},{10,14},{5,1},{7,3},{9,5},{11,7},{... | collective-permute-start | bytes 786440 | tf_op jit(solution)/shard_map/ppermute | solution.py:444
  63.8 1.0 %copy-start.14 = (f32[2,17,64,128]{3,2,1,0:T(8,128)}, f32[2,17,64,128]{3,2,1,0:T(8,128)S(1)}, u32[]{:S(2)}) copy-start(f32[2,17,64,128]{3,2,1,0:T(8,128)S(1)} %shard_map.146.refs_8_) | copy-start | bytes 3342340
  64.8 1.2 %copy-start.15 = (f32[2,17,64,128]{3,2,1,0:T(8,128)S(1)}, f32[2,17,64,128]{3,2,1,0:T(8,128)}, u32[]{:S(2)}) copy-start(f32[2,17,64,128]{3,2,1,0:T(8,128)} %copy-done.14) | copy-start | bytes 3342340
  65.0 2.5 %collective-permute-start.10 = (bf16[28,64,128]{2,1,0:T(8,128)(2,1)S(1)}, bf16[28,64,128]{2,1,0:T(8,128)(2,1)S(1)}, u32[]{:S(2)}, u32[]{:S(2)}) collective-permute-start(bf16[28,64,128]{2,1,0:T(8,128)(2,1)S(1)} %pad_maximum_fusion.1), channel_id=1, source_target_pairs={{0,1},{1,0},{2,3},{3,2},{4,5},{5,4},{6,7},{7,6},{8,9},{9,8},{10,11... | collective-permute-start | bytes 1376264 | tf_op jit(solution)/shard_map/ppermute | solution.py:428

commit v7 on v6

--- a/solution.py
+++ b/solution.py
@@ -54,16 +54,20 @@
     return jnp.clip(where, 0, OFFSETS - 1)
 
 
-def lift_tiles(tiles, basis, transfer, own, up):
+def lift_tiles(tiles, basis, transfer, own, up, pending=()):
     count = len(tiles)
-    sums = []
+    sums, lifted = [], []
+    width = basis.shape[1]
     for i, tile in enumerate(tiles):
-        width = basis.shape[1]
         c0 = nn(tile[:, :width], basis[2 * i])
         c1 = nn(tile[:, width:], basis[2 * i + 1])
         coarse = beside(c0, c1).astype(BF16)
         own[i] = coarse
         own[count + i] = tile
+        lifted.append(coarse)
+    for copy in pending:
+        copy.wait()
+    for i, coarse in enumerate(lifted):
         part = nn(coarse[:, :width], transfer[2 * i]) + nn(coarse[:, width:], transfer[2 * i + 1])
         if i % (FAN // 2) == 0:
             sums.append(part)
@@ -81,10 +85,10 @@
 def lift_kernel(*refs):
     inputs, (own, up), loaded, sems = refs[:5], refs[5:7], refs[7:12], refs[12]
     copies = fetch(list(zip(inputs, loaded)), sems)
-    for copy in copies:
+    for copy in copies[:2]:
         copy.wait()
     values, basis, transfer, far_plan, near_plan = loaded
-    lift_tiles(cut(values), basis, transfer, own, up)
+    lift_tiles(cut(values), basis, transfer, own, up, copies[2:])
     far, near = far_plan[0, 0:1, :], near_plan[0, 0:1, :]
     blank = jnp.zeros((1, 128 - far.shape[1] - near.shape[1]), jnp.int32)
     row = jnp.concatenate([far, near, blank], axis=1).astype(F32)

time: 70.5 us -> 70.3 us (level)
  no operation moved by 1% of the time
where the time goes in v7:
time: 70.3 us; the launch traced here: 69.8 us
  starting transfers between devices  33.4 us (48%)
  Pallas kernels  24.4 us (35%)
  waiting for transfers between devices  6.77 us (10%)
  local copies, waits for them, and re-layouts  4.04 us (6%)
  between operations  1.09 us (2%)
    pallas_call x9, Pallas kernels, call(): pl.pallas_call(kernel, out_shape=outs, in_specs=[SPECS[k] for k in kinds]...  24.4 us
    ppermute x6, starting transfers between devices, exchange(): lax.ppermute(m, 'clu', outward(devices, d + 1))  20.3 us
    all_to_all x2, starting transfers between devices, exchange(): lax.all_to_all(up, 'clu', 0, 0, tiled=True, axis_index_groups=same_core)  12 us
    all_to_all x2, waiting for transfers between devices, exchange(): lax.all_to_all(up, 'clu', 0, 0, tiled=True, axis_index_groups=same_core)  5.67 us
    unnamed x35, local copies, waits for them, and re-layouts  3.93 us
  transfers between devices with their start and end apart: 13, of which 3 were waited for; matrix products, arithmetic and copies ran while one was open for 3% of the time, Pallas kernels for 21%

profile of v7, /device:TPU:0, one launch (start us, length us, event | category | flops | bytes accessed | tf_op | source)
XLA Modules:
  0.0 69.8 jit_solution(16129981925905478465)
XLA Ops:
  0.6 2.5 %shard_map.140 = (bf16[16,64,128]{2,1,0:T(8,128)(2,1)}, bf16[8,80,128]{2,1,0:T(8,128)(2,1)}) custom-call(bf16[64,1024]{1,0:T(8,128)(2,1)} %bitcast.30, bf16[16,64,64]{2,1,0:T(8,128)(2,1)} %refs_10_.1, bf16[16,64,64]{2,1,0:T(8,128)(2,1)} %refs_11_.1, s32[1,2,72]{2,1,0:T(2,128)} %refs_1_.9, s32[1,2,24]{2,1,0:T(2,128)} %refs_2_.9), custom_call_target="tpu_custom_call" | custom-call | flops 1000000000 | bytes 393984 | tf_op jit(solution)/shard_map/pallas_call | solution.py:376
  3.1 7.3 %all-to-all-start = ((bf16[8,80,128]{2,1,0:T(8,128)(2,1)}), bf16[8,80,128]{2,1,0:T(8,128)(2,1)S(1)}, u32[]{:S(2)}, u32[]{:S(2)}) async-start(bf16[8,80,128]{2,1,0:T(8,128)(2,1)} %get-tuple-element.38), calls=%async_computation | async-start | bytes 327680 | tf_op jit(solution)/shard_map/all_to_all | solution.py:436
  10.4 0.0 collective-permute-start.1
  10.5 0.0 copy-start.11
  10.5 0.0 copy-start.12
  10.5 1.8 %copy.29 = bf16[1,72,64,64]{3,2,1,0:T(8,128)(2,1)S(1)} copy(bf16[1,72,64,64]{1,3,2,0:T(8,128)(2,1)S(1)} %copy-done.16) | data formatting | bytes 1179648 | tf_op args[10]
  12.3 5.7 %all-to-all-done.refs_7_ = bf16[8,80,128]{2,1,0:T(8,128)(2,1)S(1)} async-done(((bf16[8,80,128]{2,1,0:T(8,128)(2,1)}), bf16[8,80,128]{2,1,0:T(8,128)(2,1)S(1)}, u32[]{:S(2)}, u32[]{:S(2)}) %all-to-all-start) | async-done | bytes 163872 | tf_op jit(solution)/shard_map/all_to_all | solution.py:436
  18.0 0.1 collective-permute-start
  18.1 0.1 pad_add_fusion.place_ref.refs_0_
  18.2 0.0 copy-start.6
  18.2 0.0 copy-start.7
  18.2 0.0 copy-start.9
  18.3 0.0 copy-start.10
  18.3 0.0 collective-permute-done.1.mate
  18.3 1.0 %collective-permute-done.mate_asks = s32[8,128]{1,0:T(8,128)S(1)} collective-permute-done((s32[8,128]{1,0:T(8,128)S(1)}, s32[8,128]{1,0:T(8,128)S(1)}, u32[]{:S(2)}, u32[]{:S(2)}) %collective-permute-start) | collective-permute-done | bytes 4128 | tf_op jit(solution)/shard_map/ppermute | solution.py:432
  19.3 1.5 %shard_map.141 = (bf16[16,64,128]{2,1,0:T(8,128)(2,1)S(1)}, bf16[16,64,128]{2,1,0:T(8,128)(2,1)S(1)}, bf16[12,64,128]{2,1,0:T(8,128)(2,1)S(1)}, bf16[4,64,128]{2,1,0:T(8,128)(2,1)S(1)}) custom-call(s32[2]{0:T(128)S(1)} %pad_add_fusion.place_ref.refs_0_, s32[8,128]{1,0:T(8,128)S(1)} %fusion.asks, s32[8,128]{1,0:T(8,128)S(1)} %collective-permute-done.mate_asks, ...), custom_call_target="tpu_custom_call" | custom-call | flops 2000000000 | bytes 533256 | tf_op jit(solution)/shard_map/pallas_call | solution.py:376
  20.8 2.7 %collective-permute-start.4 = (bf16[12,64,128]{2,1,0:T(8,128)(2,1)S(1)}, bf16[12,64,128]{2,1,0:T(8,128)(2,1)S(1)}, u32[]{:S(2)}, u32[]{:S(2)}) collective-permute-start(bf16[12,64,128]{2,1,0:T(8,128)(2,1)S(1)} %get-tuple-element.43), channel_id=1, source_target_pairs={{0,6},{2,8},{4,10},{6,12},{8,14},{7,1},{9,3},{11,5},{13,7},{15,9},... | collective-permute-start | bytes 589832 | tf_op jit(solution)/shard_map/ppermute | solution.py:448
  23.6 3.2 %collective-permute-start.2 = (bf16[16,64,128]{2,1,0:T(8,128)(2,1)S(1)}, bf16[16,64,128]{2,1,0:T(8,128)(2,1)S(1)}, u32[]{:S(2)}, u32[]{:S(2)}) collective-permute-start(bf16[16,64,128]{2,1,0:T(8,128)(2,1)S(1)} %get-tuple-element.41), channel_id=1, source_target_pairs={{0,2},{2,4},{4,6},{6,8},{8,10},{10,12},{12,14},{3,1},{5,3},{7,5},{... | collective-permute-start | bytes 786440 | tf_op jit(solution)/shard_map/ppermute | solution.py:448
  26.7 2.7 %collective-permute-start.3 = (bf16[16,64,128]{2,1,0:T(8,128)(2,1)S(1)}, bf16[16,64,128]{2,1,0:T(8,128)(2,1)S(1)}, u32[]{:S(2)}, u32[]{:S(2)}) collective-permute-start(bf16[16,64,128]{2,1,0:T(8,128)(2,1)S(1)} %get-tuple-element.42), channel_id=1, source_target_pairs={{0,4},{2,6},{4,8},{6,10},{8,12},{10,14},{5,1},{7,3},{9,5},{11,7},{... | collective-permute-start | bytes 786440 | tf_op jit(solution)/shard_map/ppermute | solution.py:448
  29.5 4.6 %shard_map.142 = (f32[2,17,64,128]{3,2,1,0:T(8,128)S(1)}, bf16[72,64,64]{2,1,0:T(8,128)(2,1)S(1)}, bf16[24,64,64]{2,1,0:T(8,128)(2,1)S(1)}, bf16[32,64,64]{2,1,0...) custom-call(s32[2]{0:T(128)S(1)} %pad_add_fusion.place_ref.refs_0_, ...), custom_call_target="tpu_custom_call" | custom-call | flops 7000000000 | bytes 3737352 | tf_op jit(solution)/shard_map/pallas_call | solution.py:376
  34.2 0.0 copy-start.13
  34.2 0.0 collective-permute-done.4.refs_6_
  34.2 0.0 collective-permute-done.2.refs_4_
  34.2 0.0 collective-permute-done.3.refs_5_
  34.3 0.1 pad_maximum_fusion
  34.4 0.5 collective-permute-start.5
  34.9 1.4 %shard_map.143 = (f32[2,17,64,128]{3,2,1,0:T(8,128)S(1)}, f32[128,64]{1,0:T(8,128)S(1)}) custom-call(s32[2]{0:T(128)S(1)} %pad_add_fusion.place_ref.refs_0_, s32[1,2,72]{2,1,0:T(2,128)S(1)} %copy-done.11, s32[1,2,24]{2,1,0:T(2,128)S(1)} %copy-done.12, s32[1,2,32]{2,1,0:T(2,128)S(1)} %copy-done.13, ...), custom_call_target="tpu_custom_call", output_to_operand_aliasing={{0}: (8, {})} | custom-call | flops 2000000000 | bytes 3048456 | tf_op jit(solution)/shard_map/pallas_call | solution.py:376
  36.3 0.1 collective-permute-done.5.refs_4_
  36.3 3.1 %shard_map.144 = (f32[2,17,64,128]{3,2,1,0:T(8,128)S(1)}, bf16[64,1024]{1,0:T(8,128)(2,1)}, bf16[16,64,128]{2,1,0:T(8,128)(2,1)}, bf16[8,64,128]{2,1,0:T(8,128)(2,1)}) custom-call(s32[2]{0:T(128)S(1)} %pad_add_fusion.place_ref.refs_0_, s32[1,2,72]{2,1,0:T(2,128)S(1)} %copy-done.11, s32[1,2,24]{2,1,0:T(2,128)S(1)} %copy-done.12, ...), custom_call_target="tpu_custom_call", output_to_operand_aliasing={{0}: (5, {})} | custom-call | flops 3000000000 | bytes 2917384 | tf_op jit(solution)/shard_map/pallas_call | solution.py:376
  39.4 0.4 collective-permute-start.6
  39.8 4.7 %all-to-all-start.1 = ((bf16[8,64,128]{2,1,0:T(8,128)(2,1)}), bf16[8,64,128]{2,1,0:T(8,128)(2,1)S(1)}, u32[]{:S(2)}, u32[]{:S(2)}) async-start(bf16[8,64,128]{2,1,0:T(8,128)(2,1)} %get-tuple-element.64), calls=%async_computation.1 | async-start | bytes 262144 | tf_op jit(solution)/shard_map/all_to_all | solution.py:436
  44.5 0.0 copy-start.3
  44.5 0.0 collective-permute-done.6.mate
  44.6 2.6 %shard_map.145 = (bf16[16,64,128]{2,1,0:T(8,128)(2,1)}, bf16[16,64,128]{2,1,0:T(8,128)(2,1)}, bf16[12,64,128]{2,1,0:T(8,128)(2,1)}, bf16[4,64,128]{2,1,0:T(8,128)(2,1)S(1)}) custom-call(s32[2]{0:T(128)S(1)} %pad_add_fusion.place_ref.refs_0_, s32[8,128]{1,0:T(8,128)S(1)} %fusion.asks, s32[8,128]{1,0:T(8,128)S(1)} %collective-permute-done.mate_asks, ...), custom_call_target="tpu_custom_call" | custom-call | flops 2000000000 | bytes 533256 | tf_op jit(solution)/shard_map/pallas_call | solution.py:376
  47.2 4.8 %collective-permute-start.9 = (bf16[12,64,128]{2,1,0:T(8,128)(2,1)}, bf16[12,64,128]{2,1,0:T(8,128)(2,1)S(1)}, u32[]{:S(2)}, u32[]{:S(2)}) collective-permute-start(bf16[12,64,128]{2,1,0:T(8,128)(2,1)} %get-tuple-element.63), channel_id=1, source_target_pairs={{0,6},{2,8},{4,10},{6,12},{8,14},{7,1},{9,3},{11,5},{13,7},{15,9},... | collective-permute-start | bytes 589832 | tf_op jit(solution)/shard_map/ppermute | solution.py:448
  52.0 3.4 %collective-permute-start.7 = (bf16[16,64,128]{2,1,0:T(8,128)(2,1)}, bf16[16,64,128]{2,1,0:T(8,128)(2,1)S(1)}, u32[]{:S(2)}, u32[]{:S(2)}) collective-permute-start(bf16[16,64,128]{2,1,0:T(8,128)(2,1)} %get-tuple-element.61), channel_id=1, source_target_pairs={{0,2},{2,4},{4,6},{6,8},{8,10},{10,12},{12,14},{3,1},{5,3},{7,5},{... | collective-permute-start | bytes 786440 | tf_op jit(solution)/shard_map/ppermute | solution.py:448
  55.4 3.5 %collective-permute-start.8 = (bf16[16,64,128]{2,1,0:T(8,128)(2,1)}, bf16[16,64,128]{2,1,0:T(8,128)(2,1)S(1)}, u32[]{:S(2)}, u32[]{:S(2)}) collective-permute-start(bf16[16,64,128]{2,1,0:T(8,128)(2,1)} %get-tuple-element.62), channel_id=1, source_target_pairs={{0,4},{2,6},{4,8},{6,10},{8,12},{10,14},{5,1},{7,3},{9,5},{11,7},{... | collective-permute-start | bytes 786440 | tf_op jit(solution)/shard_map/ppermute | solution.py:448
  59.0 4.6 %shard_map.146.refs_8_ = f32[2,17,64,128]{3,2,1,0:T(8,128)S(1)} custom-call(s32[2]{0:T(128)S(1)} %pad_add_fusion.place_ref.refs_0_, s32[8,16]{1,0:T(8,128)S(1)} %bitcast.27, s32[8,16]{1,0:T(8,128)S(1)} %bitcast.29, s32[1,2,72]{2,1,0:T(2,128)S(1)} %copy-done.11, s32[1,2,24]{2,1,0:T(2,128)S(1)} %copy-done.12, ...), custom_call_target="tpu_custom_call" | custom-call | flops 6000000000 | bytes 3213064 | tf_op jit(solution)/shard_map/pallas_call | solution.py:376
  63.6 1.0 %copy-done.14 = f32[2,17,64,128]{3,2,1,0:T(8,128)} copy-done((f32[2,17,64,128]{3,2,1,0:T(8,128)}, f32[2,17,64,128]{3,2,1,0:T(8,128)S(1)}, u32[]{:S(2)}) %copy-start.14) | copy-done | bytes 1114136
  64.6 0.0 all-to-all-done.1.refs_7_
  64.6 0.0 collective-permute-done.9.refs_6_
  64.6 0.0 collective-permute-done.7.refs_4_
  64.6 0.0 collective-permute-done.8.refs_5_
  64.7 0.1 pad_maximum_fusion.1
  64.8 0.1 collective-permute-start.10
  64.9 1.0 %copy-done.15 = f32[2,17,64,128]{3,2,1,0:T(8,128)S(1)} copy-done((f32[2,17,64,128]{3,2,1,0:T(8,128)S(1)}, f32[2,17,64,128]{3,2,1,0:T(8,128)}, u32[]{:S(2)}) %copy-start.15) | copy-done | bytes 1114136
  65.9 1.4 %shard_map.147 = (f32[2,17,64,128]{3,2,1,0:T(8,128)S(1)}, f32[128,64]{1,0:T(8,128)S(1)}) custom-call(s32[2]{0:T(128)S(1)} %pad_add_fusion.place_ref.refs_0_, s32[1,2,72]{2,1,0:T(2,128)S(1)} %copy-done.11, s32[1,2,24]{2,1,0:T(2,128)S(1)} %copy-done.12, s32[1,2,32]{2,1,0:T(2,128)S(1)} %copy-done.13, ...), custom_call_target="tpu_custom_call", output_to_operand_aliasing={{0}: (8, {})} | custom-call | flops 2000000000 | bytes 3015688 | tf_op jit(solution)/shard_map/pallas_call | solution.py:376
  67.3 2.6 %shard_map.148 = (f32[2,17,64,128]{3,2,1,0:T(8,128)S(1)}, bf16[64,1024]{1,0:T(8,128)(2,1)}) custom-call(s32[2]{0:T(128)S(1)} %pad_add_fusion.place_ref.refs_0_, s32[1,2,72]{2,1,0:T(2,128)S(1)} %copy-done.11, s32[1,2,24]{2,1,0:T(2,128)S(1)} %copy-done.12, s32[1,2,32]{2,1,0:T(2,128)S(1)} %copy-done.13, ...), custom_call_target="tpu_custom_call", output_to_operand_aliasing={{0}: (5, {})} | custom-call | flops 2000000000 | bytes 2917384 | tf_op jit(solution)/shard_map/pallas_call | solution.py:376
  (34 shorter events, 0.2 us)
Async XLA Ops:
  0.6 9.8 %copy-start.16 = (bf16[1,72,64,64]{1,3,2,0:T(8,128)(2,1)S(1)}, bf16[1,72,64,64]{1,3,2,0:T(8,128)(2,1)}, u32[]{:S(2)}) copy-start(bf16[1,72,64,64]{1,3,2,0:T(8,128)(2,1)} %param.23) | copy-start | bytes 1769476
  3.1 14.9 %all-to-all-start = ((bf16[8,80,128]{2,1,0:T(8,128)(2,1)}), bf16[8,80,128]{2,1,0:T(8,128)(2,1)S(1)}, u32[]{:S(2)}, u32[]{:S(2)}) async-start(bf16[8,80,128]{2,1,0:T(8,128)(2,1)} %get-tuple-element.38), calls=%async_computation | async-start | bytes 327680 | tf_op jit(solution)/shard_map/all_to_all | solution.py:436
  10.4 7.8 %collective-permute-start.1 = (bf16[16,64,128]{2,1,0:T(8,128)(2,1)}, bf16[16,64,128]{2,1,0:T(8,128)(2,1)S(1)}, u32[]{:S(2)}, u32[]{:S(2)}) collective-permute-start(bf16[16,64,128]{2,1,0:T(8,128)(2,1)} %get-tuple-element.40.own.refs_5_), channel_id=1, source_target_pairs={{0,1},{1,0},{2,3},{3,2},{4,5},{5,4},{6,7},{7,6},{8,9},{9,8},{10,11... | collective-permute-start | bytes 786440 | tf_op jit(solution)/shard_map/ppermute | solution.py:432
  10.4 8.8 %copy-start.8 = (bf16[16,64,128]{2,1,0:T(8,128)(2,1)S(1)}, bf16[16,64,128]{2,1,0:T(8,128)(2,1)}, u32[]{:S(2)}) copy-start(bf16[16,64,128]{2,1,0:T(8,128)(2,1)} %get-tuple-element.40.own.refs_5_) | copy-start | bytes 786436
  10.5 8.8 %copy-start.11 = (s32[1,2,72]{2,1,0:T(2,128)S(1)}, s32[1,2,72]{2,1,0:T(2,128)}, u32[]{:S(2)}) copy-start(s32[1,2,72]{2,1,0:T(2,128)} %refs_1_.9) | copy-start | bytes 1732
  10.5 8.8 %copy-start.12 = (s32[1,2,24]{2,1,0:T(2,128)S(1)}, s32[1,2,24]{2,1,0:T(2,128)}, u32[]{:S(2)}) copy-start(s32[1,2,24]{2,1,0:T(2,128)} %refs_2_.9) | copy-start | bytes 580
  18.0 1.2 %collective-permute-start = (s32[8,128]{1,0:T(8,128)S(1)}, s32[8,128]{1,0:T(8,128)S(1)}, u32[]{:S(2)}, u32[]{:S(2)}) collective-permute-start(s32[8,128]{1,0:T(8,128)S(1)} %fusion.asks), channel_id=1, source_target_pairs={{0,1},{1,0},{2,3},{3,2},{4,5},{5,4},{6,7},{7,6},{8,9},{9,8},{10,11... | collective-permute-start | bytes 12296 | tf_op jit(solution)/shard_map/ppermute | solution.py:432
  18.2 11.3 %copy-start = (bf16[16,8,64,64]{3,2,1,0:T(8,128)(2,1)S(1)}, bf16[16,8,64,64]{3,2,1,0:T(8,128)(2,1)}, u32[]{:S(2)}) copy-start(bf16[16,8,64,64]{3,2,1,0:T(8,128)(2,1)} %refs_7_.3) | copy-start | bytes 3145732
  18.2 11.3 %copy-start.2 = (bf16[16,8,64,64]{3,2,1,0:T(8,128)(2,1)S(1)}, bf16[16,8,64,64]{3,2,1,0:T(8,128)(2,1)}, u32[]{:S(2)}) copy-start(bf16[16,8,64,64]{3,2,1,0:T(8,128)(2,1)} %refs_8_.3) | copy-start | bytes 3145732
  18.2 11.3 %copy-start.4 = (bf16[1,32,64,64]{3,2,1,0:T(8,128)(2,1)S(1)}, bf16[1,32,64,64]{3,2,1,0:T(8,128)(2,1)}, u32[]{:S(2)}) copy-start(bf16[1,32,64,64]{3,2,1,0:T(8,128)(2,1)} %param.25) | copy-start | bytes 786436
  18.2 11.3 %copy-start.5 = (bf16[1,24,64,64]{3,2,1,0:T(8,128)(2,1)S(1)}, bf16[1,24,64,64]{3,2,1,0:T(8,128)(2,1)}, u32[]{:S(2)}) copy-start(bf16[1,24,64,64]{3,2,1,0:T(8,128)(2,1)} %param.21) | copy-start | bytes 589828
  18.2 11.3 %copy-start.6 = (bf16[16,64,64]{2,1,0:T(8,128)(2,1)S(1)}, bf16[16,64,64]{2,1,0:T(8,128)(2,1)}, u32[]{:S(2)}) copy-start(bf16[16,64,64]{2,1,0:T(8,128)(2,1)} %refs_10_.1) | copy-start | bytes 393220
  18.2 11.3 %copy-start.7 = (bf16[16,64,64]{2,1,0:T(8,128)(2,1)S(1)}, bf16[16,64,64]{2,1,0:T(8,128)(2,1)}, u32[]{:S(2)}) copy-start(bf16[16,64,64]{2,1,0:T(8,128)(2,1)} %refs_11_.1) | copy-start | bytes 393220
  18.2 11.3 %copy-start.9 = (s32[16,8]{0,1:T(8,128)S(1)}, s32[16,8]{0,1:T(8,128)}, u32[]{:S(2)}) copy-start(s32[16,8]{0,1:T(8,128)} %param.18) | copy-start | bytes 1540
  18.3 11.3 %copy-start.10 = (s32[16,8]{0,1:T(8,128)S(1)}, s32[16,8]{0,1:T(8,128)}, u32[]{:S(2)}) copy-start(s32[16,8]{0,1:T(8,128)} %param.16) | copy-start | bytes 1540
  20.8 13.3 %collective-permute-start.4 = (bf16[12,64,128]{2,1,0:T(8,128)(2,1)S(1)}, bf16[12,64,128]{2,1,0:T(8,128)(2,1)S(1)}, u32[]{:S(2)}, u32[]{:S(2)}) collective-permute-start(bf16[12,64,128]{2,1,0:T(8,128)(2,1)S(1)} %get-tuple-element.43), channel_id=1, source_target_pairs={{0,6},{2,8},{4,10},{6,12},{8,14},{7,1},{9,3},{11,5},{13,7},{15,9},... | collective-permute-start | bytes 589832 | tf_op jit(solution)/shard_map/ppermute | solution.py:448
  23.6 10.7 %collective-permute-start.2 = (bf16[16,64,128]{2,1,0:T(8,128)(2,1)S(1)}, bf16[16,64,128]{2,1,0:T(8,128)(2,1)S(1)}, u32[]{:S(2)}, u32[]{:S(2)}) collective-permute-start(bf16[16,64,128]{2,1,0:T(8,128)(2,1)S(1)} %get-tuple-element.41), channel_id=1, source_target_pairs={{0,2},{2,4},{4,6},{6,8},{8,10},{10,12},{12,14},{3,1},{5,3},{7,5},{... | collective-permute-start | bytes 786440 | tf_op jit(solution)/shard_map/ppermute | solution.py:448
  26.7 7.5 %collective-permute-start.3 = (bf16[16,64,128]{2,1,0:T(8,128)(2,1)S(1)}, bf16[16,64,128]{2,1,0:T(8,128)(2,1)S(1)}, u32[]{:S(2)}, u32[]{:S(2)}) collective-permute-start(bf16[16,64,128]{2,1,0:T(8,128)(2,1)S(1)} %get-tuple-element.42), channel_id=1, source_target_pairs={{0,4},{2,6},{4,8},{6,10},{8,12},{10,14},{5,1},{7,3},{9,5},{11,7},{... | collective-permute-start | bytes 786440 | tf_op jit(solution)/shard_map/ppermute | solution.py:448
  34.2 0.7 %copy-start.13 = (s32[1,2,32]{2,1,0:T(2,128)S(1)}, s32[1,2,32]{2,1,0:T(2,128)}, u32[]{:S(2)}) copy-start(s32[1,2,32]{2,1,0:T(2,128)} %refs_3_.13) | copy-start | bytes 772
  34.4 2.0 %collective-permute-start.5 = (bf16[28,64,128]{2,1,0:T(8,128)(2,1)S(1)}, bf16[28,64,128]{2,1,0:T(8,128)(2,1)S(1)}, u32[]{:S(2)}, u32[]{:S(2)}) collective-permute-start(bf16[28,64,128]{2,1,0:T(8,128)(2,1)S(1)} %pad_maximum_fusion), channel_id=1, source_target_pairs={{0,1},{1,0},{2,3},{3,2},{4,5},{5,4},{6,7},{7,6},{8,9},{9,8},{10,11... | collective-permute-start | bytes 1376264 | tf_op jit(solution)/shard_map/ppermute | solution.py:432
  39.4 5.1 %collective-permute-start.6 = (bf16[16,64,128]{2,1,0:T(8,128)(2,1)}, bf16[16,64,128]{2,1,0:T(8,128)(2,1)S(1)}, u32[]{:S(2)}, u32[]{:S(2)}) collective-permute-start(bf16[16,64,128]{2,1,0:T(8,128)(2,1)} %get-tuple-element.60.own.refs_5_), channel_id=1, source_target_pairs={{0,1},{1,0},{2,3},{3,2},{4,5},{5,4},{6,7},{7,6},{8,9},{9,8},{10,11... | collective-permute-start | bytes 786440 | tf_op jit(solution)/shard_map/ppermute | solution.py:432
  39.8 24.8 %all-to-all-start.1 = ((bf16[8,64,128]{2,1,0:T(8,128)(2,1)}), bf16[8,64,128]{2,1,0:T(8,128)(2,1)S(1)}, u32[]{:S(2)}, u32[]{:S(2)}) async-start(bf16[8,64,128]{2,1,0:T(8,128)(2,1)} %get-tuple-element.64), calls=%async_computation.1 | async-start | bytes 262144 | tf_op jit(solution)/shard_map/all_to_all | solution.py:436
  44.5 14.4 %copy-start.1 = (bf16[16,8,64,64]{3,2,1,0:T(8,128)(2,1)S(1)}, bf16[16,8,64,64]{3,2,1,0:T(8,128)(2,1)}, u32[]{:S(2)}) copy-start(bf16[16,8,64,64]{3,2,1,0:T(8,128)(2,1)} %refs_7_.3) | copy-start | bytes 3145732
  44.5 14.4 %copy-start.3 = (bf16[16,8,64,64]{3,2,1,0:T(8,128)(2,1)S(1)}, bf16[16,8,64,64]{3,2,1,0:T(8,128)(2,1)}, u32[]{:S(2)}) copy-start(bf16[16,8,64,64]{3,2,1,0:T(8,128)(2,1)} %refs_8_.3) | copy-start | bytes 3145732
  47.2 17.4 %collective-permute-start.9 = (bf16[12,64,128]{2,1,0:T(8,128)(2,1)}, bf16[12,64,128]{2,1,0:T(8,128)(2,1)S(1)}, u32[]{:S(2)}, u32[]{:S(2)}) collective-permute-start(bf16[12,64,128]{2,1,0:T(8,128)(2,1)} %get-tuple-element.63), channel_id=1, source_target_pairs={{0,6},{2,8},{4,10},{6,12},{8,14},{7,1},{9,3},{11,5},{13,7},{15,9},... | collective-permute-start | bytes 589832 | tf_op jit(solution)/shard_map/ppermute | solution.py:448
  52.0 12.6 %collective-permute-start.7 = (bf16[16,64,128]{2,1,0:T(8,128)(2,1)}, bf16[16,64,128]{2,1,0:T(8,128)(2,1)S(1)}, u32[]{:S(2)}, u32[]{:S(2)}) collective-permute-start(bf16[16,64,128]{2,1,0:T(8,128)(2,1)} %get-tuple-element.61), channel_id=1, source_target_pairs={{0,2},{2,4},{4,6},{6,8},{8,10},{10,12},{12,14},{3,1},{5,3},{7,5},{... | collective-permute-start | bytes 786440 | tf_op jit(solution)/shard_map/ppermute | solution.py:448
  55.4 9.3 %collective-permute-start.8 = (bf16[16,64,128]{2,1,0:T(8,128)(2,1)}, bf16[16,64,128]{2,1,0:T(8,128)(2,1)S(1)}, u32[]{:S(2)}, u32[]{:S(2)}) collective-permute-start(bf16[16,64,128]{2,1,0:T(8,128)(2,1)} %get-tuple-element.62), channel_id=1, source_target_pairs={{0,4},{2,6},{4,8},{6,10},{8,12},{10,14},{5,1},{7,3},{9,5},{11,7},{... | collective-permute-start | bytes 786440 | tf_op jit(solution)/shard_map/ppermute | solution.py:448
  63.6 1.0 %copy-start.14 = (f32[2,17,64,128]{3,2,1,0:T(8,128)}, f32[2,17,64,128]{3,2,1,0:T(8,128)S(1)}, u32[]{:S(2)}) copy-start(f32[2,17,64,128]{3,2,1,0:T(8,128)S(1)} %shard_map.146.refs_8_) | copy-start | bytes 3342340
  64.6 1.2 %copy-start.15 = (f32[2,17,64,128]{3,2,1,0:T(8,128)S(1)}, f32[2,17,64,128]{3,2,1,0:T(8,128)}, u32[]{:S(2)}) copy-start(f32[2,17,64,128]{3,2,1,0:T(8,128)} %copy-done.14) | copy-start | bytes 3342340
  64.8 2.5 %collective-permute-start.10 = (bf16[28,64,128]{2,1,0:T(8,128)(2,1)S(1)}, bf16[28,64,128]{2,1,0:T(8,128)(2,1)S(1)}, u32[]{:S(2)}, u32[]{:S(2)}) collective-permute-start(bf16[28,64,128]{2,1,0:T(8,128)(2,1)S(1)} %pad_maximum_fusion.1), channel_id=1, source_target_pairs={{0,1},{1,0},{2,3},{3,2},{4,5},{5,4},{6,7},{7,6},{8,9},{9,8},{10,11... | collective-permute-start | bytes 1376264 | tf_op jit(solution)/shard_map/ppermute | solution.py:432
